TPU v7x, 256 devices: a whole 4x4x8 slice. The times are simulated.
256 devices in a mesh: rep: 8 (over y, x_lo), own: 32 (over z, x_hi, core).
Axes of the slice: x: 4 (x_hi: 2, x_lo: 2; x = x_hi * 2 + x_lo), y: 4, z: 8, core: 2. Of those that a mesh axis runs over, the one named last changes fastest.
Arguments:
- act_wide: bfloat16 [1024, 14, 14, 1024], P(('rep', 'own')), may hold values from -6 to 6
- act_middle: bfloat16 [1024, 14, 14, 256], P(('rep', 'own')), may hold values from -6 to 6
- act_narrow: bfloat16 [1024, 14, 14, 256], P(('rep', 'own')), may hold values from -6 to 6
- grad_first: bfloat16 [1024, 14, 14, 256], P(('rep', 'own')), may hold values from -6 to 6
- grad_second: bfloat16 [1024, 14, 14, 256], P(('rep', 'own')), may hold values from -6 to 6
- grad_third: bfloat16 [1024, 14, 14, 1024], P(('rep', 'own')), may hold values from -6 to 6
Outputs:
- update_first: bfloat16 [1024, 256], replicated
- update_second: bfloat16 [2304, 256], replicated
- update_third: bfloat16 [256, 1024], replicated
All inputs are finite; a program needn't handle non-finite values. Where the computation divides by a largest or mean magnitude, that divisor is 1e-20 or more.
Results may differ from a plain program's by a relative error of at most 0.0013.
Values may be sent and summed in bfloat16 or wider, within the bound.
No kernel may reach another device: no remote copies, remote signals or barrier semaphores. Data moves between devices by JAX's collectives and lax.ppermute only.
A program may use at most 128 MiB of HBM per device.

v0:
```python
import functools

import jax
import jax.numpy as jnp
from jax import lax
from jax.experimental import pallas as pl
from jax.experimental.pallas import tpu as pltpu
from jax.sharding import Mesh
from jax.sharding import PartitionSpec as P

NS_ITERS = 6
DAMPING = 0.1
MID = 256
HALF = 128
SETS = 2
F32 = jnp.float32
BF16 = jnp.bfloat16

REC = (200, 192)
SHARED = (72, 64)
ORDER = (((3, 2, 1, 0), (1, 0, 3, 2)), ((2, 3, 0, 1), (0, 1, 2, 3)))
LEAF = tuple(REC[s] + SHARED[s] for s in range(SETS))
LEAF_AT = tuple(sum(LEAF[:s]) for s in range(SETS + 1))


def slot(order, q):
    return sum(((q >> order[k]) & 1) << (3 - k) for k in range(4))


def part_rows(s):
    return (8 * REC[s] + 2 * SHARED[s], 9 * REC[s] + SHARED[s])


def dot_t(a, b):
    return lax.dot_general(a, b, (((0,), (0,)), ((), ())), preferred_element_type=F32)


def iotas(n=HALF):
    return lax.broadcasted_iota(jnp.int32, (n, n), 0), lax.broadcasted_iota(jnp.int32, (n, n), 1)


def put(side, keep, send, at, low, high):
    n = low.shape[0]
    keep[at : at + n, :] = jnp.where(side, high, low)
    send[at : at + n, :] = jnp.where(side, low, high)


def put_gram(side, keep, send, at, gram):
    r, c = iotas()
    a, b, d = gram[:HALF, :HALF], gram[:HALF, HALF:], gram[HALF:, HALF:]
    fold = jnp.where(r <= c, a, d)
    for s in range(SETS):
        put(side, keep, send, at[s], fold[64 * s : 64 * s + 64], b[64 * s : 64 * s + 64])
    diag = jnp.broadcast_to(jnp.sum(jnp.where(r == c, d, 0.0), axis=0, keepdims=True), (8, HALF))
    put(side, keep, send, at[0] + 64, diag, diag)


def put_tile(side, keep, send, at, tile):
    for s in range(SETS):
        rows = tile[HALF * s : HALF * s + HALF]
        put(side, keep, send, at[s], rows[:, :HALF], rows[:, HALF:])


def part_at(part, s, index):
    return sum(part_rows(t)[part] for t in range(s)) + index * REC[s]


def widen(ref, pad):
    images, h, w, c = ref.shape
    pad[:, :w, :] = ref[...].reshape(images * h, w, c)
    pad[:, w:, :] = jnp.zeros((images * h, 16 - w, c), BF16)


def ends_kernel(bits, aw, an, g1, g3, keep, send, pw, pn, p1, p3):
    side = bits[0] == 1
    for ref, pad in ((aw, pw), (an, pn), (g1, p1), (g3, p3)):
        widen(ref, pad)
    rows = pw.shape[0] * 16

    def block(pad, k):
        return pad[:, :, MID * k : MID * k + MID].reshape(rows, MID)

    first_out, third_in = block(p1, 0), block(pn, 0)
    for q in range(8):
        at = [part_at(0, s, q) for s in range(SETS)]
        if q < 4:
            own = block(pw, q)
            tile = dot_t(own, first_out)
        else:
            own = block(p3, q - 4)
            tile = dot_t(third_in, own)
        put_tile(side, keep, send, at, tile)
        put_gram(side, keep, send, [x + HALF for x in at], dot_t(own, own))
    for i, own in enumerate((first_out, third_in)):
        at = [part_at(0, s, 8) + i * SHARED[s] for s in range(SETS)]
        put_gram(side, keep, send, at, dot_t(own, own))


def patch_kernel(bits, am, g2, keep, send, shifted, grads):
    side = bits[0] == 1
    images, h, w, c = am.shape
    shifted[1, :, :, :] = jnp.zeros(shifted.shape[1:], BF16)
    for n in range(images):
        shifted[1, 1 + n * (h + 1) : 1 + n * (h + 1) + h, :w, :] = am[n]
    whole = shifted[1].astype(F32)
    lines = whole.shape[0]
    j = lax.broadcasted_iota(jnp.int32, (lines, 16, c), 1)
    shifted[0] = jnp.where(j < w, pltpu.roll(whole, 1, 1), 0.0).astype(BF16)
    shifted[2] = jnp.where(j < w, pltpu.roll(whole, 15, 1), 0.0).astype(BF16)
    grads[...] = jnp.zeros(grads.shape, BF16)
    for n in range(images):
        grads[n * (h + 1) : n * (h + 1) + h, :w, :] = g2[n]
    span = grads.shape[0]
    second_out = grads[...].reshape(span * 16, c)
    for dx in range(3):
        def picked(lo, hi):
            parts = [shifted[dx, 1 + n * (h + 1) + lo : 1 + n * (h + 1) + hi] for n in range(images)]
            return jnp.concatenate(parts, axis=0).reshape(images * (hi - lo) * 16, c)

        top, inner, bottom = (picked(lo, hi) for lo, hi in ((0, 1), (1, h - 1), (h - 1, h)))
        inner = dot_t(inner, inner)
        top = dot_t(top, top)
        bottom = dot_t(bottom, bottom)
        for dy in range(3):
            q = 3 * dy + dx
            at = [part_at(1, s, q) for s in range(SETS)]
            patch = shifted[dx, dy : dy + span].reshape(span * 16, c)
            put_tile(side, keep, send, at, dot_t(patch, second_out))
            gram = inner
            if dy < 2:
                gram = gram + top
            if dy > 0:
                gram = gram + bottom
            put_gram(side, keep, send, [x + HALF for x in at], gram)
    at = [part_at(1, s, 9) for s in range(SETS)]
    put_gram(side, keep, send, at, dot_t(second_out, second_out))


def held_rows(s, tiles):
    return (tiles + 1) * REC[s] + 3 * SHARED[s]


def first_split_kernel(bits, keep0, got0, keep1, got1, *outs):
    for core in range(2):

        @pl.when(bits[0] == core)
        def _(core=core):
            first_split(ORDER[core], bits, keep0, got0, keep1, got1, outs)


def first_split(orders, bits, keep0, got0, keep1, got1, outs):
    for s in range(SETS):
        keep, send = outs[2 * s], outs[2 * s + 1]
        lead = orders[s][0]
        side = bits[1 + lead] == 1
        n = REC[s]

        def summed(q):
            part, mine, got = (0, keep0, got0) if q < 8 else (1, keep1, got1)
            at = part_at(part, s, q % 8)
            return mine[at : at + n, :] + got[at : at + n, :]

        for q in range(16):
            if (q >> lead) & 1:
                continue
            put(side, keep, send, slot(orders[s], q) * n, summed(q), summed(q | 1 << lead))
        at = 8 * n
        shared = SHARED[s]
        for part, mine, got, i, size in (
            (1, keep1, got1, 8, n),
            (0, keep0, got0, 8, 2 * shared),
            (1, keep1, got1, 9, shared),
        ):
            src = part_at(part, s, i)
            value = mine[src : src + size, :] + got[src : src + size, :]
            keep[at : at + size, :] = value
            send[at : at + size, :] = value
            at += size


def split_kernel(step, bits, *refs):
    tiles = 16 >> step
    for s in range(SETS):
        mine, got = refs[2 * s], refs[2 * s + 1]
        keep, send = refs[2 * SETS + 2 * s], refs[2 * SETS + 2 * s + 1]
        size = (tiles // 2) * REC[s]
        bit = bits[9 + 4 * s + step]
        here = pl.ds(pl.multiple_of(bit * size, 8), size)
        there = pl.ds(pl.multiple_of((1 - bit) * size, 8), size)
        keep[:size, :] = mine[here, :] + got[here, :]
        send[:size, :] = mine[there, :] + got[there, :]
        value = mine[2 * size :, :] + got[2 * size :, :]
        keep[size:, :] = value
        send[size:, :] = value


def leaf_kernel(bits, *refs):
    kind = bits[6]
    side = bits[5] == 1
    keep, send = refs[2 * SETS], refs[2 * SETS + 1]
    for s in range(SETS):
        mine, got = refs[2 * s], refs[2 * s + 1]
        n, shared = REC[s], SHARED[s]
        at = LEAF_AT[s]
        put(side, keep, send, at, mine[:n, :] + got[:n, :], mine[n : 2 * n, :] + got[n : 2 * n, :])
        chosen = pl.ds(pl.multiple_of(2 * n + kind * shared, 8), shared)
        last = slice(2 * n + 2 * shared, 2 * n + 3 * shared)
        put(side, keep, send, at + n, mine[chosen, :] + got[chosen, :], mine[last, :] + got[last, :])


def mm(a, b):
    return jnp.dot(a, b, precision=lax.Precision.HIGHEST, preferred_element_type=F32)


def unfold(fold, b, diag):
    r, c = iotas()
    turned = fold.T
    a = jnp.where(r <= c, fold, turned)
    d = jnp.where(r > c, fold, jnp.where(r < c, turned, jnp.broadcast_to(diag, fold.shape)))
    top = jnp.concatenate([a, b], axis=1)
    return jnp.concatenate([top, jnp.concatenate([b.T, d], axis=1)], axis=0)


def residual(gram, count):
    r, c = iotas(MID)
    matrix = gram / count
    level = jnp.sum(jnp.where(r == c, matrix, 0.0)) / MID
    matrix = matrix + jnp.where(r == c, DAMPING * level, 0.0)
    bound = jnp.max(jnp.sum(jnp.abs(matrix), axis=0, keepdims=True))
    return jnp.where(r == c, 1.0, 0.0) - matrix / bound, bound


def solve_kernel(count, bits, mine, mate, out):
    side = bits[0] == 1
    low = jnp.where(side, mate[...], mine[...])
    high = jnp.where(side, mine[...], mate[...])

    def gather(part, offset, rows):
        starts = [LEAF_AT[s] + offset(s) for s in range(SETS)]
        return jnp.concatenate([part[at : at + rows] for at in starts], axis=0)

    def gram(offset):
        at = offset(0) + 64
        return unfold(gather(low, offset, 64), gather(high, offset, 64), low[at : at + 1])

    zero = lambda s: 0
    tile = jnp.concatenate([gather(low, zero, HALF), gather(high, zero, HALF)], axis=1) / count
    own, own_bound = residual(gram(lambda s: HALF), count)
    shared, shared_bound = residual(gram(lambda s: REC[s]), count)
    third = bits[7] == 1
    left, right = jnp.where(third, shared, own), jnp.where(third, own, shared)
    r, c = iotas(MID)
    product = jnp.where(r == c, 1.0, 0.0) + right
    tile = tile + mm(left, tile)
    for step in range(1, NS_ITERS):
        left, right = mm(left, left), mm(right, right)
        tile = tile + mm(left, tile)
        product = product + mm(product, right)
    result = mm(tile / own_bound, product / shared_bound)
    out[...] = jnp.where(side, result[HALF:], result[:HALF]).astype(BF16)


def place_kernel(bits, mine, mate, last, last_mate, out1, out2, out3):
    side = bits[0] == 1
    for half in range(2):
        swap = side if half == 0 else jnp.logical_not(side)
        at = half * HALF
        for j in range(16):
            value = jnp.where(swap, mate[j], mine[j])
            q = tile_of(j // 4, j % 2 * 2 + j // 2 % 2)
            if q < 4:
                out1[q * MID + at : q * MID + at + HALF, :] = value
            elif q < 8:
                out3[at : at + HALF, (q - 4) * MID : (q - 3) * MID] = value
            else:
                out2[(q - 8) * MID + at : (q - 8) * MID + at + HALF, :] = value
        out2[8 * MID + at : 8 * MID + at + HALF, :] = jnp.where(swap, last_mate[...], last[...])


VMEM = pl.BlockSpec(memory_space=pltpu.VMEM)
SMEM = pl.BlockSpec(memory_space=pltpu.SMEM)


def scratch_arrays(scratch):
    return [jax.ShapeDtypeStruct(a.shape, a.dtype) for a in scratch]


def call(kernel, bits, args, outs, scratch=(), flops=0, room=4):
    size = sum(a.size * a.dtype.itemsize for a in args) + sum(o.size * o.dtype.itemsize for o in outs)
    held = sum(a.size * a.dtype.itemsize for a in scratch_arrays(scratch))
    many = len(outs) > 1
    return pl.pallas_call(
        kernel,
        out_shape=tuple(outs) if many else outs[0],
        in_specs=[SMEM] + [VMEM] * len(args),
        out_specs=tuple([VMEM] * len(outs)) if many else VMEM,
        scratch_shapes=list(scratch),
        compiler_params=pltpu.CompilerParams(vmem_limit_bytes=size * 5 // 4 + held + room * 2**20),
        cost_estimate=pl.CostEstimate(flops=flops, bytes_accessed=size, transcendentals=0),
    )(bits, *args)


AXES = ("y", "x_lo", "z", "x_hi", "core")
SIZES = (4, 2, 8, 2, 2)


def place_of(device):
    rep, own = divmod(device, 32)
    return rep // 2, (own // 2) % 2 * 2 + rep % 2, own // 4, own % 2


def device_of(y, x, z, c):
    return (y * 2 + x % 2) * 32 + z * 4 + x // 2 * 2 + c


def route(move):
    return [(d, device_of(*move(*place_of(d)))) for d in range(256)]


ROUTE_C = route(lambda y, x, z, c: (y, x, z, 1 - c))
MOVE = {
    3: lambda y, x, z, c: (y, x ^ 1, z, c),
    2: lambda y, x, z, c: (y, 3 - x, z, c),
    1: lambda y, x, z, c: (y ^ 1, x, z, c),
    0: lambda y, x, z, c: (3 - y, x, z, c),
}
ROUTE_XY = [
    [route(lambda y, x, z, c: MOVE[ORDER[c][s][step]](y, x, z, c)) for step in range(4)] for s in range(SETS)
]
ROUTE_Z1 = route(lambda y, x, z, c: (y, x, z ^ 1, c))
ROUTE_Z2 = route(lambda y, x, z, c: (y, x, 7 - z if c else z ^ 3, c))
ROUTE_Z3 = route(lambda y, x, z, c: (y, x, z ^ 3 if c else 7 - z, c))


def tile_of(y, x):
    return ((x ^ (x >> 1)) & 1) * 8 + (x >> 1) * 4 + ((y ^ (y >> 1)) & 1) * 2 + (y >> 1)


def send_to(value, way):
    return lax.ppermute(value, AXES, way)


def on_device(act_wide, act_middle, act_narrow, grad_first, grad_second, grad_third):
    images, height, width, wide = act_wide.shape
    middle = act_middle.shape[3]
    count = float(images * height * width * 256)
    y, z, core = lax.axis_index("y"), lax.axis_index("z"), lax.axis_index("core")
    x = lax.axis_index("x_hi") * 2 + lax.axis_index("x_lo")
    q = tile_of(y, x)
    own = [(q >> i) & 1 for i in range(4)]
    turns = [jnp.where(core == 1, own[ORDER[1][s][k]], own[ORDER[0][s][k]]) for s in range(SETS) for k in range(4)]
    odd = ((z + 1) >> 1) & 1
    kind = jnp.where(q < 4, 0, jnp.where(q < 8, 1, 2))
    third = jnp.where((kind == 1) & (odd == 0), 1, 0)
    bits = jnp.stack([core, *own, odd, kind, third, q, *turns]).astype(jnp.int32)

    lines = images * height
    rows = [sum(part_rows(s)[part] for s in range(SETS)) for part in range(2)]
    made = [jax.ShapeDtypeStruct((n, HALF), F32) for n in rows]
    pads = [pltpu.VMEM((lines, 16, n), BF16) for n in (wide, middle, middle, wide)]
    keep0, send0 = call(
        ends_kernel, bits, (act_wide, act_narrow, grad_first, grad_third), [made[0]] * 2, pads, 2 * 18 * 896 * 65536
    )
    got0 = send_to(send0, ROUTE_C)
    span = images * (height + 1)
    keep1, send1 = call(
        patch_kernel,
        bits,
        (act_middle, grad_second),
        [made[1]] * 2,
        [pltpu.VMEM((3, span + 2, 16, middle), BF16), pltpu.VMEM((span, 16, middle), BF16)],
        2 * 13 * 960 * 65536,
    )
    got1 = send_to(send1, ROUTE_C)

    def pairs(tiles):
        shapes = [jax.ShapeDtypeStruct((held_rows(s, tiles), HALF), F32) for s in range(SETS)]
        return [shape for shape in shapes for _ in range(2)]

    held = call(first_split_kernel, bits, (keep0, got0, keep1, got1), pairs(8))
    for step in range(4):
        args = []
        for s in range(SETS):
            args += [held[2 * s], send_to(held[2 * s + 1], ROUTE_XY[s][step])]
        if step < 3:
            held = call(functools.partial(split_kernel, step + 1), bits, args, pairs(4 >> step))
    leaf = jax.ShapeDtypeStruct((LEAF_AT[-1], HALF), F32)
    keep, send = call(leaf_kernel, bits, args, [leaf] * 2)
    total = keep + send_to(send, ROUTE_Z1)
    total = total + send_to(total, ROUTE_Z2)
    total = total + send_to(total, ROUTE_Z3)
    mine = call(
        functools.partial(solve_kernel, count),
        bits,
        (total, send_to(total, ROUTE_C)),
        [jax.ShapeDtypeStruct((HALF, MID), BF16)],
        flops=2 * 22 * 6 * MID**3,
        room=24,
    )

    other = send_to(mine, ROUTE_Z1)
    tile, last = jnp.where(odd == 0, mine, other), jnp.where(odd == 0, other, mine)
    tiles = jnp.broadcast_to(tile[None], (16, HALF, MID))
    tiles = lax.all_to_all(tiles, ("y", "x_lo", "x_hi"), 0, 0)
    pieces = (tiles, send_to(tiles, ROUTE_C), last, send_to(last, ROUTE_C))
    outs = [
        jax.ShapeDtypeStruct((wide, middle), BF16),
        jax.ShapeDtypeStruct((9 * middle, middle), BF16),
        jax.ShapeDtypeStruct((middle, wide), BF16),
    ]
    return call(place_kernel, bits, pieces, outs)


def solution(mesh):
    mesh = Mesh(mesh.devices.reshape(SIZES), AXES)
    placed = P(AXES, None, None, None)
    return jax.shard_map(on_device, mesh=mesh, in_specs=(placed,) * 6, out_specs=(P(), P(), P()), check_vma=False)
```

profile of v0, /device:TPU:1, one launch (start us, length us, event | category | flops | bytes accessed | tf_op | source)
XLA Modules:
  0.0 141.1 jit_solution(11836298379082947503)
XLA Ops:
  0.7 1.1 copy.13.am
  1.8 1.1 copy.14.g2
  2.9 2.8 %shard_map.86 = (f32[3664,128]{1,0:T(8,128)S(1)}, f32[3664,128]{1,0:T(8,128)S(1)}) custom-call(s32[17]{0:T(128)S(1)} %stack.59.bits, bf16[4,14,14,256]{3,2,1,0:T(8,128)(2,1)S(1)} %copy.13.am, bf16[4,14,14,256]{3,2,1,0:T(8,128)(2,1)S(1)} %copy.14.g2), custom_call_target="tpu_custom_call" | custom-call | flops 1635778560 | bytes 4554752 | tf_op jit(solution)/shard_map/pallas_call | solution.py:292
  5.7 3.3 %collective-permute-start.1 = (f32[3664,128]{1,0:T(8,128)S(1)}, f32[3664,128]{1,0:T(8,128)S(1)}, u32[]{:S(2)}, u32[]{:S(2)}) collective-permute-start(f32[3664,128]{1,0:T(8,128)S(1)} %get-tuple-element.28), channel_id=1, source_target_pairs={{0,1},{1,0},{2,3},{3,2},{4,5},{5,4},{6,7},{7,6},{8,9},{9,8},{10,11... | collective-permute-start | bytes 5627912 | tf_op jit(solution)/shard_map/ppermute | solution.py:340
  9.8 0.9 copy-done.1
  11.2 3.5 %shard_map.85 = (f32[3408,128]{1,0:T(8,128)S(1)}, f32[3408,128]{1,0:T(8,128)S(1)}) custom-call(s32[17]{0:T(128)S(1)} %stack.59.bits, bf16[4,14,14,1024]{3,2,1,0:T(8,128)(2,1)S(1)} %copy.9.aw, bf16[4,14,14,256]{3,2,1,0:T(8,128)(2,1)S(1)} %copy.10.an, bf16[4,14,14,256]{3,2,1,0:T(8,128)(2,1)S(1)} %copy.11.g1, bf16[4,14,14,1024]{3,2,1,0:T(8,128)(2,1)S(1)} %copy.12.g3), custom_call_target="tpu_custom_call" | custom-call | flops 2113929216 | bytes 7503872 | tf_op jit(solution)/shard_map/pallas_call | solution.py:292
  14.7 1.3 collective-permute-start
  16.0 3.3 %collective-permute-done.got0 = f32[3408,128]{1,0:T(8,128)S(1)} collective-permute-done((f32[3408,128]{1,0:T(8,128)S(1)}, f32[3408,128]{1,0:T(8,128)S(1)}, u32[]{:S(2)}, u32[]{:S(2)}) %collective-permute-start) | collective-permute-done | bytes 1744928 | tf_op jit(solution)/shard_map/ppermute | solution.py:340
  19.2 1.1 shard_map.87
  20.3 0.8 collective-permute-start.2
  21.2 2.7 %collective-permute-start.3 = (f32[1920,128]{1,0:T(8,128)S(1)}, f32[1920,128]{1,0:T(8,128)S(1)}, u32[]{:S(2)}, u32[]{:S(2)}) collective-permute-start(f32[1920,128]{1,0:T(8,128)S(1)} %get-tuple-element.32), channel_id=1, source_target_pairs={{0,64},{1,193},{2,66},{3,195},{4,68},{5,197},{6,70},{7,199},{8,72}... | collective-permute-start | bytes 2949128 | tf_op jit(solution)/shard_map/ppermute | solution.py:340
  23.9 11.5 %collective-permute-done.3.refs_3_ = f32[1920,128]{1,0:T(8,128)S(1)} collective-permute-done((f32[1920,128]{1,0:T(8,128)S(1)}, f32[1920,128]{1,0:T(8,128)S(1)}, u32[]{:S(2)}, u32[]{:S(2)}) %collective-permute-start.3) | collective-permute-done | bytes 983072 | tf_op jit(solution)/shard_map/ppermute | solution.py:340
  35.4 0.8 shard_map.88
  36.5 8.9 %collective-permute-done.5.refs_3_ = f32[1152,128]{1,0:T(8,128)S(1)} collective-permute-done((f32[1152,128]{1,0:T(8,128)S(1)}, f32[1152,128]{1,0:T(8,128)S(1)}, u32[]{:S(2)}, u32[]{:S(2)}) %collective-permute-start.5) | collective-permute-done | bytes 589856 | tf_op jit(solution)/shard_map/ppermute | solution.py:340
  46.4 2.8 %collective-permute-start.6 = (f32[816,128]{1,0:T(8,128)S(1)}, f32[816,128]{1,0:T(8,128)S(1)}, u32[]{:S(2)}, u32[]{:S(2)}) collective-permute-start(f32[816,128]{1,0:T(8,128)S(1)} %get-tuple-element.38), channel_id=1, source_target_pairs={{0,64},{1,193},{2,66},{3,195},{4,68},{5,197},{6,70},{7,199},{8,72}... | collective-permute-start | bytes 1253384 | tf_op jit(solution)/shard_map/ppermute | solution.py:340
  49.6 7.3 %collective-permute-done.7.refs_3_ = f32[768,128]{1,0:T(8,128)S(1)} collective-permute-done((f32[768,128]{1,0:T(8,128)S(1)}, f32[768,128]{1,0:T(8,128)S(1)}, u32[]{:S(2)}, u32[]{:S(2)}) %collective-permute-start.7) | collective-permute-done | bytes 393248 | tf_op jit(solution)/shard_map/ppermute | solution.py:340
  58.2 5.7 %collective-permute-done.9.refs_3_ = f32[576,128]{1,0:T(8,128)S(1)} collective-permute-done((f32[576,128]{1,0:T(8,128)S(1)}, f32[576,128]{1,0:T(8,128)S(1)}, u32[]{:S(2)}, u32[]{:S(2)}) %collective-permute-start.9) | collective-permute-done | bytes 294944 | tf_op jit(solution)/shard_map/ppermute | solution.py:340
  64.6 1.7 %collective-permute-start.10 = (f32[528,128]{1,0:T(8,128)S(1)}, f32[528,128]{1,0:T(8,128)S(1)}, u32[]{:S(2)}, u32[]{:S(2)}) collective-permute-start(f32[528,128]{1,0:T(8,128)S(1)} %get-tuple-element.46), channel_id=1, source_target_pairs={{0,4},{1,5},{2,6},{3,7},{4,0},{5,1},{6,2},{7,3},{8,12},{9,13},{10,... | collective-permute-start | bytes 811016 | tf_op jit(solution)/shard_map/ppermute | solution.py:340
  66.3 3.9 %collective-permute-done.10 = f32[528,128]{1,0:T(8,128)S(1)} collective-permute-done((f32[528,128]{1,0:T(8,128)S(1)}, f32[528,128]{1,0:T(8,128)S(1)}, u32[]{:S(2)}, u32[]{:S(2)}) %collective-permute-start.10) | collective-permute-done | bytes 270368 | tf_op jit(solution)/shard_map/ppermute | solution.py:340
  70.2 5.5 %collective-permute-start.11 = (f32[528,128]{1,0:T(8,128)S(1)}, f32[528,128]{1,0:T(8,128)S(1)}, u32[]{:S(2)}, u32[]{:S(2)}) collective-permute-start(f32[528,128]{1,0:T(8,128)S(1)} %add.29), channel_id=1, source_target_pairs={{0,12},{1,29},{2,14},{3,31},{4,8},{5,25},{6,10},{7,27},{8,4},{9,21... | collective-permute-start | bytes 811016 | tf_op jit(solution)/shard_map/ppermute | solution.py:340
  75.7 6.7 %collective-permute-done.11 = f32[528,128]{1,0:T(8,128)S(1)} collective-permute-done((f32[528,128]{1,0:T(8,128)S(1)}, f32[528,128]{1,0:T(8,128)S(1)}, u32[]{:S(2)}, u32[]{:S(2)}) %collective-permute-start.11) | collective-permute-done | bytes 270368 | tf_op jit(solution)/shard_map/ppermute | solution.py:340
  82.5 1.7 %collective-permute-start.12 = (f32[528,128]{1,0:T(8,128)S(1)}, f32[528,128]{1,0:T(8,128)S(1)}, u32[]{:S(2)}, u32[]{:S(2)}) collective-permute-start(f32[528,128]{1,0:T(8,128)S(1)} %add.30), channel_id=1, source_target_pairs={{0,28},{1,13},{2,30},{3,15},{4,24},{5,9},{6,26},{7,11},{8,20},{9,5... | collective-permute-start | bytes 811016 | tf_op jit(solution)/shard_map/ppermute | solution.py:340
  84.2 5.6 %collective-permute-done.12 = f32[528,128]{1,0:T(8,128)S(1)} collective-permute-done((f32[528,128]{1,0:T(8,128)S(1)}, f32[528,128]{1,0:T(8,128)S(1)}, u32[]{:S(2)}, u32[]{:S(2)}) %collective-permute-start.12) | collective-permute-done | bytes 270368 | tf_op jit(solution)/shard_map/ppermute | solution.py:340
  89.8 9.7 %collective-permute-start.13 = (f32[528,128]{1,0:T(8,128)S(1)}, f32[528,128]{1,0:T(8,128)S(1)}, u32[]{:S(2)}, u32[]{:S(2)}) collective-permute-start(f32[528,128]{1,0:T(8,128)S(1)} %add.31.mine), channel_id=1, source_target_pairs={{0,1},{1,0},{2,3},{3,2},{4,5},{5,4},{6,7},{7,6},{8,9},{9,8},{10,11... | collective-permute-start | bytes 811016 | tf_op jit(solution)/shard_map/ppermute | solution.py:340
  99.5 1.2 collective-permute-done.13.mate
  100.7 7.3 %shard_map.92 = bf16[128,256]{1,0:T(8,128)(2,1)S(1)} custom-call(s32[17]{0:T(128)S(1)} %stack.59.bits, f32[528,128]{1,0:T(8,128)S(1)} %add.31.mine, f32[528,128]{1,0:T(8,128)S(1)} %collective-permute-done.13.mate), custom_call_target="tpu_custom_call" | custom-call | flops 4429185024 | bytes 606208 | tf_op jit(solution)/shard_map/pallas_call | solution.py:292
  108.0 6.1 %collective-permute-start.14 = (bf16[128,256]{1,0:T(8,128)(2,1)S(1)}, bf16[128,256]{1,0:T(8,128)(2,1)S(1)}, u32[]{:S(2)}, u32[]{:S(2)}) collective-permute-start(bf16[128,256]{1,0:T(8,128)(2,1)S(1)} %shard_map.92), channel_id=1, source_target_pairs={{0,4},{1,5},{2,6},{3,7},{4,0},{5,1},{6,2},{7,3},{8,12},{9,13},{10,... | collective-permute-start | bytes 196616 | tf_op jit(solution)/shard_map/ppermute | solution.py:340
  114.1 2.2 %collective-permute-done.14 = bf16[128,256]{1,0:T(8,128)(2,1)S(1)} collective-permute-done((bf16[128,256]{1,0:T(8,128)(2,1)S(1)}, bf16[128,256]{1,0:T(8,128)(2,1)S(1)}, u32[]{:S(2)}, u32[]{:S(2)}) %collective-permute-start.14) | collective-permute-done | bytes 65568 | tf_op jit(solution)/shard_map/ppermute | solution.py:340
  116.4 17.1 %all_to_all.5.mine = bf16[16,128,256]{2,1,0:T(8,128)(2,1)S(1)} all-to-all(bf16[16,128,256]{2,1,0:T(8,128)(2,1)S(1)} %broadcast_in_dim.2), channel_id=1, replica_groups=mesh['y'=4,'x_lo'=2,'z'=8,'x_hi'=2,'core'=2] {'y','x_lo','x_hi'}, dimensions={0} | all-to-all | bytes 2097152 | tf_op jit(solution)/shard_map/all_to_all | solution.py:404
  133.5 3.1 %collective-permute-start.15 = (bf16[16,128,256]{2,1,0:T(8,128)(2,1)S(1)}, bf16[16,128,256]{2,1,0:T(8,128)(2,1)S(1)}, u32[]{:S(2)}, u32[]{:S(2)}) collective-permute-start(bf16[16,128,256]{2,1,0:T(8,128)(2,1)S(1)} %all_to_all.5.mine), channel_id=1, source_target_pairs={{0,1},{1,0},{2,3},{3,2},{4,5},{5,4},{6,7},{7,6},{8,9},{9,8},{10,11... | collective-permute-start | bytes 3145736 | tf_op jit(solution)/shard_map/ppermute | solution.py:340
  136.6 2.4 %collective-permute-done.16.last_mate = bf16[128,256]{1,0:T(8,128)(2,1)S(1)} collective-permute-done((bf16[128,256]{1,0:T(8,128)(2,1)S(1)}, bf16[128,256]{1,0:T(8,128)(2,1)S(1)}, u32[]{:S(2)}, u32[]{:S(2)}) %collective-permute-start.16) | collective-permute-done | bytes 65568 | tf_op jit(solution)/shard_map/ppermute | solution.py:340
  139.0 2.1 %shard_map.93 = (bf16[1024,256]{1,0:T(8,128)(2,1)}, bf16[2304,256]{1,0:T(8,128)(2,1)}, bf16[256,1024]{1,0:T(8,128)(2,1)}) custom-call(s32[17]{0:T(128)S(1)} %stack.59.bits, bf16[16,128,256]{2,1,0:T(8,128)(2,1)S(1)} %all_to_all.5.mine, bf16[16,128,256]{2,1,0:T(8,128)(2,1)S(1)} %collective-permute-done.15.mate, bf16[128,256]{1,0:T(8,128)(2,1)S(1)} %get-tuple-element.47.last, ...), custom_call_target="tpu_custom_call" | custom-call | bytes 4456448 | tf_op jit(solution)/shard_map/pallas_call | solution.py:292
  (32 shorter events, 5.3 us)
Async XLA Ops:
  2.9 6.2 %copy-start.2 = (bf16[4,14,14,256]{3,0,2,1:T(4,128)(2,1)S(1)}, bf16[4,14,14,256]{3,0,2,1:T(4,128)(2,1)}, u32[]{:S(2)}) copy-start(bf16[4,14,14,256]{3,0,2,1:T(4,128)(2,1)} %param.8) | copy-start | bytes 1204228
  2.9 6.2 %copy-start.3 = (bf16[4,14,14,256]{3,0,2,1:T(4,128)(2,1)S(1)}, bf16[4,14,14,256]{3,0,2,1:T(4,128)(2,1)}, u32[]{:S(2)}) copy-start(bf16[4,14,14,256]{3,0,2,1:T(4,128)(2,1)} %param.9) | copy-start | bytes 1204228
  5.7 3.5 %copy-start = (bf16[4,14,14,1024]{3,0,2,1:T(4,128)(2,1)S(1)}, bf16[4,14,14,1024]{3,0,2,1:T(4,128)(2,1)}, u32[]{:S(2)}) copy-start(bf16[4,14,14,1024]{3,0,2,1:T(4,128)(2,1)} %param.6) | copy-start | bytes 4816900
  5.7 13.5 %collective-permute-start.1 = (f32[3664,128]{1,0:T(8,128)S(1)}, f32[3664,128]{1,0:T(8,128)S(1)}, u32[]{:S(2)}, u32[]{:S(2)}) collective-permute-start(f32[3664,128]{1,0:T(8,128)S(1)} %get-tuple-element.28), channel_id=1, source_target_pairs={{0,1},{1,0},{2,3},{3,2},{4,5},{5,4},{6,7},{7,6},{8,9},{9,8},{10,11... | collective-permute-start | bytes 5627912 | tf_op jit(solution)/shard_map/ppermute | solution.py:340
  9.2 1.4 %copy-start.1 = (bf16[4,14,14,1024]{3,0,2,1:T(4,128)(2,1)S(1)}, bf16[4,14,14,1024]{3,0,2,1:T(4,128)(2,1)}, u32[]{:S(2)}) copy-start(bf16[4,14,14,1024]{3,0,2,1:T(4,128)(2,1)} %param.11) | copy-start | bytes 4816900
  14.7 4.5 %collective-permute-start = (f32[3408,128]{1,0:T(8,128)S(1)}, f32[3408,128]{1,0:T(8,128)S(1)}, u32[]{:S(2)}, u32[]{:S(2)}) collective-permute-start(f32[3408,128]{1,0:T(8,128)S(1)} %get-tuple-element.26), channel_id=1, source_target_pairs={{0,1},{1,0},{2,3},{3,2},{4,5},{5,4},{6,7},{7,6},{8,9},{9,8},{10,11... | collective-permute-start | bytes 5234696 | tf_op jit(solution)/shard_map/ppermute | solution.py:340
  20.3 15.1 %collective-permute-start.2 = (f32[2016,128]{1,0:T(8,128)S(1)}, f32[2016,128]{1,0:T(8,128)S(1)}, u32[]{:S(2)}, u32[]{:S(2)}) collective-permute-start(f32[2016,128]{1,0:T(8,128)S(1)} %get-tuple-element.30), channel_id=1, source_target_pairs={{0,32},{1,35},{2,34},{3,33},{4,36},{5,39},{6,38},{7,37},{8,40},{9,... | collective-permute-start | bytes 3096584 | tf_op jit(solution)/shard_map/ppermute | solution.py:340
  21.2 14.2 %collective-permute-start.3 = (f32[1920,128]{1,0:T(8,128)S(1)}, f32[1920,128]{1,0:T(8,128)S(1)}, u32[]{:S(2)}, u32[]{:S(2)}) collective-permute-start(f32[1920,128]{1,0:T(8,128)S(1)} %get-tuple-element.32), channel_id=1, source_target_pairs={{0,64},{1,193},{2,66},{3,195},{4,68},{5,197},{6,70},{7,199},{8,72}... | collective-permute-start | bytes 2949128 | tf_op jit(solution)/shard_map/ppermute | solution.py:340
  36.2 9.5 %collective-permute-start.4 = (f32[1216,128]{1,0:T(8,128)S(1)}, f32[1216,128]{1,0:T(8,128)S(1)}, u32[]{:S(2)}, u32[]{:S(2)}) collective-permute-start(f32[1216,128]{1,0:T(8,128)S(1)} %get-tuple-element.34), channel_id=1, source_target_pairs={{0,34},{1,33},{2,32},{3,35},{4,38},{5,37},{6,36},{7,39},{8,42},{9,... | collective-permute-start | bytes 1867784 | tf_op jit(solution)/shard_map/ppermute | solution.py:340
  36.3 9.1 %collective-permute-start.5 = (f32[1152,128]{1,0:T(8,128)S(1)}, f32[1152,128]{1,0:T(8,128)S(1)}, u32[]{:S(2)}, u32[]{:S(2)}) collective-permute-start(f32[1152,128]{1,0:T(8,128)S(1)} %get-tuple-element.36), channel_id=1, source_target_pairs={{0,192},{1,65},{2,194},{3,67},{4,196},{5,69},{6,198},{7,71},{8,200... | collective-permute-start | bytes 1769480 | tf_op jit(solution)/shard_map/ppermute | solution.py:340
  46.4 10.6 %collective-permute-start.6 = (f32[816,128]{1,0:T(8,128)S(1)}, f32[816,128]{1,0:T(8,128)S(1)}, u32[]{:S(2)}, u32[]{:S(2)}) collective-permute-start(f32[816,128]{1,0:T(8,128)S(1)} %get-tuple-element.38), channel_id=1, source_target_pairs={{0,64},{1,193},{2,66},{3,195},{4,68},{5,197},{6,70},{7,199},{8,72}... | collective-permute-start | bytes 1253384 | tf_op jit(solution)/shard_map/ppermute | solution.py:340
  49.1 7.8 %collective-permute-start.7 = (f32[768,128]{1,0:T(8,128)S(1)}, f32[768,128]{1,0:T(8,128)S(1)}, u32[]{:S(2)}, u32[]{:S(2)}) collective-permute-start(f32[768,128]{1,0:T(8,128)S(1)} %get-tuple-element.40), channel_id=1, source_target_pairs={{0,32},{1,35},{2,34},{3,33},{4,36},{5,39},{6,38},{7,37},{8,40},{9,... | collective-permute-start | bytes 1179656 | tf_op jit(solution)/shard_map/ppermute | solution.py:340
  57.6 6.4 %collective-permute-start.8 = (f32[616,128]{1,0:T(8,128)S(1)}, f32[616,128]{1,0:T(8,128)S(1)}, u32[]{:S(2)}, u32[]{:S(2)}) collective-permute-start(f32[616,128]{1,0:T(8,128)S(1)} %get-tuple-element.42), channel_id=1, source_target_pairs={{0,192},{1,65},{2,194},{3,67},{4,196},{5,69},{6,198},{7,71},{8,200... | collective-permute-start | bytes 946184 | tf_op jit(solution)/shard_map/ppermute | solution.py:340
  57.9 6.0 %collective-permute-start.9 = (f32[576,128]{1,0:T(8,128)S(1)}, f32[576,128]{1,0:T(8,128)S(1)}, u32[]{:S(2)}, u32[]{:S(2)}) collective-permute-start(f32[576,128]{1,0:T(8,128)S(1)} %get-tuple-element.44), channel_id=1, source_target_pairs={{0,34},{1,33},{2,32},{3,35},{4,38},{5,37},{6,36},{7,39},{8,42},{9,... | collective-permute-start | bytes 884744 | tf_op jit(solution)/shard_map/ppermute | solution.py:340
  64.6 5.6 %collective-permute-start.10 = (f32[528,128]{1,0:T(8,128)S(1)}, f32[528,128]{1,0:T(8,128)S(1)}, u32[]{:S(2)}, u32[]{:S(2)}) collective-permute-start(f32[528,128]{1,0:T(8,128)S(1)} %get-tuple-element.46), channel_id=1, source_target_pairs={{0,4},{1,5},{2,6},{3,7},{4,0},{5,1},{6,2},{7,3},{8,12},{9,13},{10,... | collective-permute-start | bytes 811016 | tf_op jit(solution)/shard_map/ppermute | solution.py:340
  70.2 12.2 %collective-permute-start.11 = (f32[528,128]{1,0:T(8,128)S(1)}, f32[528,128]{1,0:T(8,128)S(1)}, u32[]{:S(2)}, u32[]{:S(2)}) collective-permute-start(f32[528,128]{1,0:T(8,128)S(1)} %add.29), channel_id=1, source_target_pairs={{0,12},{1,29},{2,14},{3,31},{4,8},{5,25},{6,10},{7,27},{8,4},{9,21... | collective-permute-start | bytes 811016 | tf_op jit(solution)/shard_map/ppermute | solution.py:340
  82.5 7.3 %collective-permute-start.12 = (f32[528,128]{1,0:T(8,128)S(1)}, f32[528,128]{1,0:T(8,128)S(1)}, u32[]{:S(2)}, u32[]{:S(2)}) collective-permute-start(f32[528,128]{1,0:T(8,128)S(1)} %add.30), channel_id=1, source_target_pairs={{0,28},{1,13},{2,30},{3,15},{4,24},{5,9},{6,26},{7,11},{8,20},{9,5... | collective-permute-start | bytes 811016 | tf_op jit(solution)/shard_map/ppermute | solution.py:340
  89.8 10.9 %collective-permute-start.13 = (f32[528,128]{1,0:T(8,128)S(1)}, f32[528,128]{1,0:T(8,128)S(1)}, u32[]{:S(2)}, u32[]{:S(2)}) collective-permute-start(f32[528,128]{1,0:T(8,128)S(1)} %add.31.mine), channel_id=1, source_target_pairs={{0,1},{1,0},{2,3},{3,2},{4,5},{5,4},{6,7},{7,6},{8,9},{9,8},{10,11... | collective-permute-start | bytes 811016 | tf_op jit(solution)/shard_map/ppermute | solution.py:340
  108.0 8.3 %collective-permute-start.14 = (bf16[128,256]{1,0:T(8,128)(2,1)S(1)}, bf16[128,256]{1,0:T(8,128)(2,1)S(1)}, u32[]{:S(2)}, u32[]{:S(2)}) collective-permute-start(bf16[128,256]{1,0:T(8,128)(2,1)S(1)} %shard_map.92), channel_id=1, source_target_pairs={{0,4},{1,5},{2,6},{3,7},{4,0},{5,1},{6,2},{7,3},{8,12},{9,13},{10,... | collective-permute-start | bytes 196616 | tf_op jit(solution)/shard_map/ppermute | solution.py:340
  133.5 5.5 %collective-permute-start.15 = (bf16[16,128,256]{2,1,0:T(8,128)(2,1)S(1)}, bf16[16,128,256]{2,1,0:T(8,128)(2,1)S(1)}, u32[]{:S(2)}, u32[]{:S(2)}) collective-permute-start(bf16[16,128,256]{2,1,0:T(8,128)(2,1)S(1)} %all_to_all.5.mine), channel_id=1, source_target_pairs={{0,1},{1,0},{2,3},{3,2},{4,5},{5,4},{6,7},{7,6},{8,9},{9,8},{10,11... | collective-permute-start | bytes 3145736 | tf_op jit(solution)/shard_map/ppermute | solution.py:340
  136.6 2.4 %collective-permute-start.16 = (bf16[128,256]{1,0:T(8,128)(2,1)S(1)}, bf16[128,256]{1,0:T(8,128)(2,1)S(1)}, u32[]{:S(2)}, u32[]{:S(2)}) collective-permute-start(bf16[128,256]{1,0:T(8,128)(2,1)S(1)} %get-tuple-element.47.last), channel_id=1, source_target_pairs={{0,1},{1,0},{2,3},{3,2},{4,5},{5,4},{6,7},{7,6},{8,9},{9,8},{10,11... | collective-permute-start | bytes 196616 | tf_op jit(solution)/shard_map/ppermute | solution.py:340
where the time goes:
time: 141 us
  waiting for transfers between devices  58.9 us (42%)
  starting transfers between devices  40.2 us (29%)
  Pallas kernels  19.5 us (14%)
  blocking collectives  17.1 us (12%)
  local copies, waits for them, and re-layouts  4.38 us (3%)
    ppermute x17, waiting for transfers between devices, send_to(): return lax.ppermute(value, AXES, way)  58.9 us
    ppermute x17, starting transfers between devices, send_to(): return lax.ppermute(value, AXES, way)  40.2 us
    pallas_call x9, Pallas kernels, call(): pl.pallas_call(kernel, out_shape=tuple(outs) if many else outs[0], in_spe...  19.5 us
    all_to_all x1, blocking collectives, on_device(): tiles = lax.all_to_all(tiles, ('y', 'x_lo', 'x_hi'), 0, 0)  17.1 us
    unnamed x14, local copies, waits for them, and re-layouts  4.19 us
  transfers between devices with their start and end apart: 17, of which 13 were waited for; matrix products, arithmetic and copies ran while one was open for 1% of the time, Pallas kernels for 3%

commit v1 on v0

v1 whole, which is shorter than its diff:
```python
import functools

import jax
import jax.numpy as jnp
from jax import lax
from jax.experimental import pallas as pl
from jax.experimental.pallas import tpu as pltpu
from jax.sharding import Mesh
from jax.sharding import PartitionSpec as P

NS_ITERS = 6
DAMPING = 0.1
MID = 256
HALF = 128
SETS = 2
F32 = jnp.float32
BF16 = jnp.bfloat16

GRAM = (72, 64)
TILE = (128, 128)
ORDER = (((3, 2, 1, 0), (1, 0, 3, 2)), ((2, 3, 0, 1), (0, 1, 2, 3)))
def slot(order, q):
    return sum(((q >> order[k]) & 1) << (3 - k) for k in range(4))


def dot_t(a, b):
    return lax.dot_general(a, b, (((0,), (0,)), ((), ())), preferred_element_type=F32)


def iotas(n=HALF):
    return lax.broadcasted_iota(jnp.int32, (n, n), 0), lax.broadcasted_iota(jnp.int32, (n, n), 1)


def put(side, keep, send, at, low, high):
    n = low.shape[0]
    keep[at : at + n, :] = jnp.where(side, high, low)
    send[at : at + n, :] = jnp.where(side, low, high)


def put_gram(side, keep, send, many, i, gram):
    r, c = iotas()
    a, b, d = gram[:HALF, :HALF], gram[:HALF, HALF:], gram[HALF:, HALF:]
    fold = jnp.where(r <= c, a, d)
    for s in range(SETS):
        at = many * sum(GRAM[:s]) + i * GRAM[s]
        put(side, keep, send, at, fold[64 * s : 64 * s + 64], b[64 * s : 64 * s + 64])
    diag = jnp.broadcast_to(jnp.sum(jnp.where(r == c, d, 0.0), axis=0, keepdims=True), (8, HALF))
    put(side, keep, send, i * GRAM[0] + 64, diag, diag)


def put_tile(side, keep, send, many, i, tile):
    for s in range(SETS):
        rows = tile[HALF * s : HALF * s + HALF]
        put(side, keep, send, many * sum(TILE[:s]) + i * TILE[s], rows[:, :HALF], rows[:, HALF:])


def widen(ref, pad):
    images, h, w, c = ref.shape
    pad[:, :w, :] = ref[...].reshape(images * h, w, c)
    pad[:, w:, :] = jnp.zeros((images * h, 16 - w, c), BF16)


def columns(pad, k):
    return pad[:, :, MID * k : MID * k + MID].reshape(pad.shape[0] * 16, MID)


def end_grams_kernel(bits, aw, an, g1, g3, keep, send, pw, pn, p1, p3):
    side = bits[0] == 1
    for ref, pad in ((aw, pw), (an, pn), (g1, p1), (g3, p3)):
        widen(ref, pad)
    blocks = [(pw, k) for k in range(4)] + [(p3, k) for k in range(4)] + [(p1, 0), (pn, 0)]
    for i, block in enumerate(blocks):
        own = columns(*block)
        put_gram(side, keep, send, 10, i, dot_t(own, own))


def end_tiles_kernel(bits, aw, an, g1, g3, keep, send, pw, pn, p1, p3):
    side = bits[0] == 1
    for ref, pad in ((aw, pw), (an, pn), (g1, p1), (g3, p3)):
        widen(ref, pad)
    first_out, third_in = columns(p1, 0), columns(pn, 0)
    for q in range(8):
        tile = dot_t(columns(pw, q), first_out) if q < 4 else dot_t(third_in, columns(p3, q - 4))
        put_tile(side, keep, send, 8, q, tile)


def shift(am, shifted):
    images, h, w, c = am.shape
    shifted[1, :, :, :] = jnp.zeros(shifted.shape[1:], BF16)
    for n in range(images):
        shifted[1, 1 + n * (h + 1) : 1 + n * (h + 1) + h, :w, :] = am[n]
    whole = shifted[1].astype(F32)
    j = lax.broadcasted_iota(jnp.int32, whole.shape, 1)
    shifted[0] = jnp.where(j < w, pltpu.roll(whole, 1, 1), 0.0).astype(BF16)
    shifted[2] = jnp.where(j < w, pltpu.roll(whole, 15, 1), 0.0).astype(BF16)


def spread(g2, grads):
    images, h, w, c = g2.shape
    grads[...] = jnp.zeros(grads.shape, BF16)
    for n in range(images):
        grads[n * (h + 1) : n * (h + 1) + h, :w, :] = g2[n]
    return grads[...].reshape(grads.shape[0] * 16, c)


def patch_grams_kernel(bits, am, g2, keep, send, shifted, grads):
    side = bits[0] == 1
    images, h, w, c = am.shape
    shift(am, shifted)
    second_out = spread(g2, grads)
    put_gram(side, keep, send, 10, 9, dot_t(second_out, second_out))
    for dx in range(3):
        def picked(lo, hi):
            parts = [shifted[dx, 1 + n * (h + 1) + lo : 1 + n * (h + 1) + hi] for n in range(images)]
            return jnp.concatenate(parts, axis=0).reshape(images * (hi - lo) * 16, c)

        top, inner, bottom = (dot_t(x, x) for x in (picked(0, 1), picked(1, h - 1), picked(h - 1, h)))
        upper = inner + top
        put_gram(side, keep, send, 10, dx, upper)
        put_gram(side, keep, send, 10, 3 + dx, upper + bottom)
        put_gram(side, keep, send, 10, 6 + dx, inner + bottom)


def patch_tiles_kernel(bits, am, g2, keep, send, shifted, grads):
    side = bits[0] == 1
    shift(am, shifted)
    second_out = spread(g2, grads)
    span, c = grads.shape[0], am.shape[3]
    for q in range(9):
        patch = shifted[q % 3, q // 3 : q // 3 + span].reshape(span * 16, c)
        put_tile(side, keep, send, 9, q, dot_t(patch, second_out))


def first_split_kernel(rec, many, extra, bits, keep0, got0, keep1, got1, *outs):
    for core in range(2):

        @pl.when(bits[0] == core)
        def _(core=core):
            first_split(ORDER[core], rec, many, extra, bits, ((keep0, got0), (keep1, got1)), outs)


def first_split(orders, rec, many, extra, bits, parts, outs):
    for s in range(SETS):
        keep, send = outs[2 * s], outs[2 * s + 1]
        lead = orders[s][0]
        side = bits[1 + lead] == 1
        n = rec[s]

        def summed(part, i):
            mine, got = parts[part]
            at = many[part] * sum(rec[:s]) + i * n
            return mine[at : at + n, :] + got[at : at + n, :]

        for q in range(16):
            if (q >> lead) & 1:
                continue
            other = q | 1 << lead
            put(side, keep, send, slot(orders[s], q) * n, summed(q // 8, q % 8), summed(other // 8, other % 8))
        for i, (part, j) in enumerate(extra):
            value = summed(part, j)
            keep[(8 + i) * n : (9 + i) * n, :] = value
            send[(8 + i) * n : (9 + i) * n, :] = value


def split_kernel(rec, step, bits, *refs):
    tiles = 16 >> step
    for s in range(SETS):
        mine, got = refs[2 * s], refs[2 * s + 1]
        keep, send = refs[2 * SETS + 2 * s], refs[2 * SETS + 2 * s + 1]
        size = (tiles // 2) * rec[s]
        bit = bits[9 + 4 * s + step]
        here = pl.ds(pl.multiple_of(bit * size, 8), size)
        there = pl.ds(pl.multiple_of((1 - bit) * size, 8), size)
        keep[:size, :] = mine[here, :] + got[here, :]
        send[:size, :] = mine[there, :] + got[there, :]
        value = mine[2 * size :, :] + got[2 * size :, :]
        keep[size:, :] = value
        send[size:, :] = value


def gram_leaf_kernel(bits, mine0, got0, mine1, got1, keep, send):
    kind = bits[6]
    side = bits[5] == 1
    for s, (mine, got) in enumerate(((mine0, got0), (mine1, got1))):
        n = GRAM[s]
        at = 2 * sum(GRAM[:s])
        put(side, keep, send, at, mine[:n, :] + got[:n, :], mine[n : 2 * n, :] + got[n : 2 * n, :])
        chosen = pl.ds(pl.multiple_of((2 + kind) * n, 8), n)
        put(side, keep, send, at + n, mine[chosen, :] + got[chosen, :], mine[4 * n :, :] + got[4 * n :, :])


def tile_leaf_kernel(bits, mine0, got0, mine1, got1, keep, send):
    side = bits[5] == 1
    for s, (mine, got) in enumerate(((mine0, got0), (mine1, got1))):
        n = TILE[s]
        put(side, keep, send, n * s, mine[:n, :] + got[:n, :], mine[n:, :] + got[n:, :])


def mm(a, b):
    return jnp.dot(a, b, precision=lax.Precision.HIGHEST, preferred_element_type=F32)


def unfold(fold, b, diag):
    r, c = iotas()
    turned = fold.T
    a = jnp.where(r <= c, fold, turned)
    d = jnp.where(r > c, fold, jnp.where(r < c, turned, jnp.broadcast_to(diag, fold.shape)))
    top = jnp.concatenate([a, b], axis=1)
    return jnp.concatenate([top, jnp.concatenate([b.T, d], axis=1)], axis=0)


def residual(gram, count):
    r, c = iotas(MID)
    matrix = gram / count
    level = jnp.sum(jnp.where(r == c, matrix, 0.0)) / MID
    matrix = matrix + jnp.where(r == c, DAMPING * level, 0.0)
    bound = jnp.max(jnp.sum(jnp.abs(matrix), axis=0, keepdims=True))
    return jnp.where(r == c, 1.0, 0.0) - matrix / bound, bound


def inverse_kernel(count, bits, mine, mate, left_out, right_out):
    side = bits[0] == 1
    low = jnp.where(side, mate[...], mine[...])
    high = jnp.where(side, mine[...], mate[...])

    def gram(i):
        starts = [2 * sum(GRAM[:s]) + i * GRAM[s] for s in range(SETS)]
        fold, b = (jnp.concatenate([part[at : at + 64] for at in starts], axis=0) for part in (low, high))
        return unfold(fold, b, low[starts[0] + 64 : starts[0] + 65])

    r, c = iotas(MID)
    own, shared = residual(gram(0), count), residual(gram(1), count)
    powers = [own[0], shared[0]]
    sums = [jnp.where(r == c, 1.0, 0.0) + e for e in powers]
    for step in range(1, NS_ITERS):
        powers = [mm(e, e) for e in powers]
        sums = [x + mm(x, e) for x, e in zip(sums, powers)]
    own, shared = sums[0] / own[1], sums[1] / shared[1]
    third = bits[7] == 1
    left_out[...] = jnp.where(third, shared, own)
    right_out[...] = jnp.where(third, own, shared)


def apply_kernel(count, bits, left, right, mine, mate, out):
    side = bits[0] == 1
    low = jnp.where(side, mate[...], mine[...])
    high = jnp.where(side, mine[...], mate[...])
    tile = jnp.concatenate([low, high], axis=1) / count
    rows = left[pl.ds(pl.multiple_of(bits[0] * HALF, HALF), HALF), :]
    out[...] = mm(mm(rows, tile), right[...]).astype(BF16)


def place_kernel(bits, mine, mate, last, last_mate, out1, out2, out3):
    side = bits[0] == 1
    for half in range(2):
        swap = side if half == 0 else jnp.logical_not(side)
        at = half * HALF
        for j in range(16):
            value = jnp.where(swap, mate[j], mine[j])
            q = tile_of(j // 4, j % 2 * 2 + j // 2 % 2)
            if q < 4:
                out1[q * MID + at : q * MID + at + HALF, :] = value
            elif q < 8:
                out3[at : at + HALF, (q - 4) * MID : (q - 3) * MID] = value
            else:
                out2[(q - 8) * MID + at : (q - 8) * MID + at + HALF, :] = value
        out2[8 * MID + at : 8 * MID + at + HALF, :] = jnp.where(swap, last_mate[...], last[...])


VMEM = pl.BlockSpec(memory_space=pltpu.VMEM)
SMEM = pl.BlockSpec(memory_space=pltpu.SMEM)


def scratch_arrays(scratch):
    return [jax.ShapeDtypeStruct(a.shape, a.dtype) for a in scratch]


def call(kernel, bits, args, outs, scratch=(), flops=0, room=4):
    size = sum(a.size * a.dtype.itemsize for a in args) + sum(o.size * o.dtype.itemsize for o in outs)
    held = sum(a.size * a.dtype.itemsize for a in scratch_arrays(scratch))
    many = len(outs) > 1
    return pl.pallas_call(
        kernel,
        out_shape=tuple(outs) if many else outs[0],
        in_specs=[SMEM] + [VMEM] * len(args),
        out_specs=tuple([VMEM] * len(outs)) if many else VMEM,
        scratch_shapes=list(scratch),
        compiler_params=pltpu.CompilerParams(vmem_limit_bytes=size * 5 // 4 + held + room * 2**20),
        cost_estimate=pl.CostEstimate(flops=flops, bytes_accessed=size, transcendentals=0),
    )(bits, *args)


AXES = ("y", "x_lo", "z", "x_hi", "core")
SIZES = (4, 2, 8, 2, 2)


def place_of(device):
    rep, own = divmod(device, 32)
    return rep // 2, (own // 2) % 2 * 2 + rep % 2, own // 4, own % 2


def device_of(y, x, z, c):
    return (y * 2 + x % 2) * 32 + z * 4 + x // 2 * 2 + c


def route(move):
    return [(d, device_of(*move(*place_of(d)))) for d in range(256)]


ROUTE_C = route(lambda y, x, z, c: (y, x, z, 1 - c))
MOVE = {
    3: lambda y, x, z, c: (y, x ^ 1, z, c),
    2: lambda y, x, z, c: (y, 3 - x, z, c),
    1: lambda y, x, z, c: (y ^ 1, x, z, c),
    0: lambda y, x, z, c: (3 - y, x, z, c),
}
ROUTE_XY = [
    [route(lambda y, x, z, c: MOVE[ORDER[c][s][step]](y, x, z, c)) for step in range(4)] for s in range(SETS)
]
ROUTE_Z1 = route(lambda y, x, z, c: (y, x, z ^ 1, c))
ROUTE_Z2 = route(lambda y, x, z, c: (y, x, 7 - z if c else z ^ 3, c))
ROUTE_Z3 = route(lambda y, x, z, c: (y, x, z ^ 3 if c else 7 - z, c))


def tile_of(y, x):
    return ((x ^ (x >> 1)) & 1) * 8 + (x >> 1) * 4 + ((y ^ (y >> 1)) & 1) * 2 + (y >> 1)


def send_to(value, way):
    return lax.ppermute(value, AXES, way)


def on_device(act_wide, act_middle, act_narrow, grad_first, grad_second, grad_third):
    images, height, width, wide = act_wide.shape
    middle = act_middle.shape[3]
    count = float(images * height * width * 256)
    y, z, core = lax.axis_index("y"), lax.axis_index("z"), lax.axis_index("core")
    x = lax.axis_index("x_hi") * 2 + lax.axis_index("x_lo")
    q = tile_of(y, x)
    own = [(q >> i) & 1 for i in range(4)]
    turns = [jnp.where(core == 1, own[ORDER[1][s][k]], own[ORDER[0][s][k]]) for s in range(SETS) for k in range(4)]
    odd = ((z + 1) >> 1) & 1
    kind = jnp.where(q < 4, 0, jnp.where(q < 8, 1, 2))
    third = jnp.where((kind == 1) & (odd == 0), 1, 0)
    bits = jnp.stack([core, *own, odd, kind, third, q, *turns]).astype(jnp.int32)

    def shape(*dims):
        return jax.ShapeDtypeStruct(dims, F32)

    lines, span = images * height, images * (height + 1)
    pads = [pltpu.VMEM((lines, 16, n), BF16) for n in (wide, middle, middle, wide)]
    maps = [pltpu.VMEM((3, span + 2, 16, middle), BF16), pltpu.VMEM((span, 16, middle), BF16)]
    ends = (act_wide, act_narrow, grad_first, grad_third)
    patches = (act_middle, grad_second)

    def pairs(rec, records):
        return [shape(records * rec[s], HALF) for s in range(SETS) for _ in range(2)]

    def start(rec, many, extra, kernels, bits):
        parts = []
        for part, args, scratch in ((1, patches, maps), (0, ends, pads)):
            outs = [shape(many[part] * sum(rec), HALF)] * 2
            keep, send = call(kernels[part], bits, args, outs, scratch, 2 * many[part] * 900 * 65536)
            parts = [keep, send_to(send, ROUTE_C)] + parts
        outs = pairs(rec, 8 + len(extra))
        return call(functools.partial(first_split_kernel, rec, many, extra), bits, parts, outs)

    def chain(rec, extra, held, leaf):
        for step in range(4):
            args = []
            for s in range(SETS):
                args += [held[2 * s], send_to(held[2 * s + 1], ROUTE_XY[s][step])]
            if step < 3:
                held = call(functools.partial(split_kernel, rec, step + 1), bits, args, pairs(rec, (4 >> step) + extra))
        size = sum(rec) * (1 if extra == 1 else 2)
        keep, send = call(leaf, bits, args, [shape(size, HALF)] * 2)
        total = keep + send_to(send, ROUTE_Z1)
        total = total + send_to(total, ROUTE_Z2)
        total = total + send_to(total, ROUTE_Z3)
        return total, send_to(total, ROUTE_C)

    shared = ((1, 8), (0, 8), (0, 9), (1, 9))
    held = start(GRAM, (10, 10), shared, (end_grams_kernel, patch_grams_kernel), bits)
    *held, later = lax.optimization_barrier((*held, bits))
    grams = chain(GRAM, 4, held, gram_leaf_kernel)
    held = start(TILE, (8, 9), ((1, 8),), (end_tiles_kernel, patch_tiles_kernel), later)
    tiles = chain(TILE, 1, held, tile_leaf_kernel)
    inverses = call(
        functools.partial(inverse_kernel, count),
        bits,
        grams,
        [shape(MID, MID)] * 2,
        flops=2 * 20 * 6 * MID**3,
        room=16,
    )
    mine = call(
        functools.partial(apply_kernel, count),
        bits,
        (*inverses, *tiles),
        [jax.ShapeDtypeStruct((HALF, MID), BF16)],
        flops=2 * 6 * MID**3,
    )
    other = send_to(mine, ROUTE_Z1)
    tile, last = jnp.where(odd == 0, mine, other), jnp.where(odd == 0, other, mine)
    tiles = jnp.broadcast_to(tile[None], (16, HALF, MID))
    tiles = lax.all_to_all(tiles, ("y", "x_lo", "x_hi"), 0, 0)
    pieces = (tiles, send_to(tiles, ROUTE_C), last, send_to(last, ROUTE_C))
    outs = [
        jax.ShapeDtypeStruct((wide, middle), BF16),
        jax.ShapeDtypeStruct((9 * middle, middle), BF16),
        jax.ShapeDtypeStruct((middle, wide), BF16),
    ]
    return call(place_kernel, bits, pieces, outs)


def solution(mesh):
    mesh = Mesh(mesh.devices.reshape(SIZES), AXES)
    placed = P(AXES, None, None, None)
    return jax.shard_map(on_device, mesh=mesh, in_specs=(placed,) * 6, out_specs=(P(), P(), P()), check_vma=False)
```

time: 141 us -> 134 us (0.950)
  waiting for transfers between devices: 58.9 us -> 40.9 us
  Pallas kernels: 19.5 us -> 24.3 us
  starting transfers between devices: 40.2 us -> 44.8 us
  blocking collectives: 17.1 us -> 18.7 us
    ppermute x17 -> x31, waiting for transfers between devices: 58.9 us -> 40.9 us  [send_to(): return lax.ppermute(value, AXES, way)]
    pallas_call x9 -> x17, Pallas kernels: 19.5 us -> 24.3 us  [call(): pl.pallas_call(kernel, out_shape=tuple(outs) if many else outs[0], in_spe...]
    ppermute x17 -> x31, starting transfers between devices: 40.2 us -> 44.8 us  [send_to(): return lax.ppermute(value, AXES, way)]
    all_to_all x1, blocking collectives: 17.1 us -> 18.7 us  [on_device(): tiles = lax.all_to_all(tiles, ('y', 'x_lo', 'x_hi'), 0, 0)]
  transfers between devices with their start and end apart: 17 -> 31, of which waited for: 13 -> 13; matrix products, arithmetic and copies ran while one was open for 1% -> 1% of each run, Pallas kernels for 3% -> 12%
where the time goes in v1:
time: 134 us
  starting transfers between devices  44.8 us (33%)
  waiting for transfers between devices  40.9 us (31%)
  Pallas kernels  24.3 us (18%)
  blocking collectives  18.7 us (14%)
  local copies, waits for them, and re-layouts  4.38 us (3%)
    ppermute x31, starting transfers between devices, send_to(): return lax.ppermute(value, AXES, way)  44.8 us
    ppermute x31, waiting for transfers between devices, send_to(): return lax.ppermute(value, AXES, way)  40.9 us
    pallas_call x17, Pallas kernels, call(): pl.pallas_call(kernel, out_shape=tuple(outs) if many else outs[0], in_spe...  24.3 us
    all_to_all x1, blocking collectives, on_device(): tiles = lax.all_to_all(tiles, ('y', 'x_lo', 'x_hi'), 0, 0)  18.7 us
    unnamed x14, local copies, waits for them, and re-layouts  4.19 us
  transfers between devices with their start and end apart: 31, of which 13 were waited for; matrix products, arithmetic and copies ran while one was open for 1% of the time, Pallas kernels for 12%

profile of v1, /device:TPU:1, one launch (start us, length us, event | category | flops | bytes accessed | tf_op | source)
XLA Modules:
  0.0 134.2 jit_solution(15028421863485731148)
XLA Ops:
  2.9 1.6 %shard_map.86 = (f32[1360,128]{1,0:T(8,128)S(1)}, f32[1360,128]{1,0:T(8,128)S(1)}) custom-call(s32[17]{0:T(128)S(1)} %stack.59.bits, bf16[4,14,14,256]{3,2,1,0:T(8,128)(2,1)S(1)} %copy.13.am, bf16[4,14,14,256]{3,2,1,0:T(8,128)(2,1)S(1)} %copy.14.g2), custom_call_target="tpu_custom_call" | custom-call | flops 1179648000 | bytes 2195456 | tf_op jit(solution)/shard_map/pallas_call | solution.py:282
  4.5 3.3 %collective-permute-start.1 = (f32[1360,128]{1,0:T(8,128)S(1)}, f32[1360,128]{1,0:T(8,128)S(1)}, u32[]{:S(2)}, u32[]{:S(2)}) collective-permute-start(f32[1360,128]{1,0:T(8,128)S(1)} %get-tuple-element.57), channel_id=1, source_target_pairs={{0,1},{1,0},{2,3},{3,2},{4,5},{5,4},{6,7},{7,6},{8,9},{9,8},{10,11... | collective-permute-start | bytes 2088968 | tf_op jit(solution)/shard_map/ppermute | solution.py:330
  10.0 2.4 %shard_map.85 = (f32[1360,128]{1,0:T(8,128)S(1)}, f32[1360,128]{1,0:T(8,128)S(1)}) custom-call(s32[17]{0:T(128)S(1)} %stack.59.bits, bf16[4,14,14,1024]{3,2,1,0:T(8,128)(2,1)S(1)} %copy.9.aw, bf16[4,14,14,256]{3,2,1,0:T(8,128)(2,1)S(1)} %copy.10.an, bf16[4,14,14,256]{3,2,1,0:T(8,128)(2,1)S(1)} %copy.11.g1, bf16[4,14,14,1024]{3,2,1,0:T(8,128)(2,1)S(1)} %copy.12.g3), custom_call_target="tpu_custom_call" | custom-call | flops 1179648000 | bytes 5406720 | tf_op jit(solution)/shard_map/pallas_call | solution.py:282
  12.3 1.2 collective-permute-start
  13.6 1.8 %collective-permute-done.got0 = f32[1360,128]{1,0:T(8,128)S(1)} collective-permute-done((f32[1360,128]{1,0:T(8,128)S(1)}, f32[1360,128]{1,0:T(8,128)S(1)}, u32[]{:S(2)}, u32[]{:S(2)}) %collective-permute-start) | collective-permute-done | bytes 696352 | tf_op jit(solution)/shard_map/ppermute | solution.py:330
  16.1 2.2 %shard_map.94 = (f32[2304,128]{1,0:T(8,128)S(1)}, f32[2304,128]{1,0:T(8,128)S(1)}) custom-call(s32[17]{0:T(128)S(1)} %stack.59.bits, bf16[4,14,14,256]{3,2,1,0:T(8,128)(2,1)S(1)} %copy.13.am, bf16[4,14,14,256]{3,2,1,0:T(8,128)(2,1)S(1)} %copy.14.g2), custom_call_target="tpu_custom_call" | custom-call | flops 1061683200 | bytes 3162112 | tf_op jit(solution)/shard_map/pallas_call | solution.py:282
  18.7 2.1 %shard_map.93 = (f32[2048,128]{1,0:T(8,128)S(1)}, f32[2048,128]{1,0:T(8,128)S(1)}) custom-call(s32[17]{0:T(128)S(1)} %stack.59.bits, bf16[4,14,14,1024]{3,2,1,0:T(8,128)(2,1)S(1)} %copy.9.aw, bf16[4,14,14,256]{3,2,1,0:T(8,128)(2,1)S(1)} %copy.10.an, bf16[4,14,14,256]{3,2,1,0:T(8,128)(2,1)S(1)} %copy.11.g1, bf16[4,14,14,1024]{3,2,1,0:T(8,128)(2,1)S(1)} %copy.12.g3), custom_call_target="tpu_custom_call" | custom-call | flops 943718400 | bytes 6111232 | tf_op jit(solution)/shard_map/pallas_call | solution.py:282
  21.8 2.7 %collective-permute-start.3 = (f32[768,128]{1,0:T(8,128)S(1)}, f32[768,128]{1,0:T(8,128)S(1)}, u32[]{:S(2)}, u32[]{:S(2)}) collective-permute-start(f32[768,128]{1,0:T(8,128)S(1)} %get-tuple-element.65), channel_id=1, source_target_pairs={{0,64},{1,193},{2,66},{3,195},{4,68},{5,197},{6,70},{7,199},{8,72}... | collective-permute-start | bytes 1179656 | tf_op jit(solution)/shard_map/ppermute | solution.py:330
  25.7 2.3 %collective-permute-start.17 = (f32[1152,128]{1,0:T(8,128)S(1)}, f32[1152,128]{1,0:T(8,128)S(1)}, u32[]{:S(2)}, u32[]{:S(2)}) collective-permute-start(f32[1152,128]{1,0:T(8,128)S(1)} %get-tuple-element.90), channel_id=1, source_target_pairs={{0,64},{1,193},{2,66},{3,195},{4,68},{5,197},{6,70},{7,199},{8,72}... | collective-permute-start | bytes 1769480 | tf_op jit(solution)/shard_map/ppermute | solution.py:330
  28.0 1.7 %collective-permute-done.3.refs_3_ = f32[768,128]{1,0:T(8,128)S(1)} collective-permute-done((f32[768,128]{1,0:T(8,128)S(1)}, f32[768,128]{1,0:T(8,128)S(1)}, u32[]{:S(2)}, u32[]{:S(2)}) %collective-permute-start.3) | collective-permute-done | bytes 393248 | tf_op jit(solution)/shard_map/ppermute | solution.py:330
  30.8 6.3 %collective-permute-done.16.refs_1_ = f32[1152,128]{1,0:T(8,128)S(1)} collective-permute-done((f32[1152,128]{1,0:T(8,128)S(1)}, f32[1152,128]{1,0:T(8,128)S(1)}, u32[]{:S(2)}, u32[]{:S(2)}) %collective-permute-start.16) | collective-permute-done | bytes 589856 | tf_op jit(solution)/shard_map/ppermute | solution.py:330
  39.4 1.7 %collective-permute-start.6 = (f32[432,128]{1,0:T(8,128)S(1)}, f32[432,128]{1,0:T(8,128)S(1)}, u32[]{:S(2)}, u32[]{:S(2)}) collective-permute-start(f32[432,128]{1,0:T(8,128)S(1)} %get-tuple-element.71), channel_id=1, source_target_pairs={{0,64},{1,193},{2,66},{3,195},{4,68},{5,197},{6,70},{7,199},{8,72}... | collective-permute-start | bytes 663560 | tf_op jit(solution)/shard_map/ppermute | solution.py:330
  41.1 1.9 %collective-permute-start.7 = (f32[384,128]{1,0:T(8,128)S(1)}, f32[384,128]{1,0:T(8,128)S(1)}, u32[]{:S(2)}, u32[]{:S(2)}) collective-permute-start(f32[384,128]{1,0:T(8,128)S(1)} %get-tuple-element.73), channel_id=1, source_target_pairs={{0,32},{1,35},{2,34},{3,33},{4,36},{5,39},{6,38},{7,37},{8,40},{9,... | collective-permute-start | bytes 589832 | tf_op jit(solution)/shard_map/ppermute | solution.py:330
  43.0 6.3 %collective-permute-done.7.refs_3_ = f32[384,128]{1,0:T(8,128)S(1)} collective-permute-done((f32[384,128]{1,0:T(8,128)S(1)}, f32[384,128]{1,0:T(8,128)S(1)}, u32[]{:S(2)}, u32[]{:S(2)}) %collective-permute-start.7) | collective-permute-done | bytes 196640 | tf_op jit(solution)/shard_map/ppermute | solution.py:330
  51.8 1.5 %collective-permute-start.21 = (f32[384,128]{1,0:T(8,128)S(1)}, f32[384,128]{1,0:T(8,128)S(1)}, u32[]{:S(2)}, u32[]{:S(2)}) collective-permute-start(f32[384,128]{1,0:T(8,128)S(1)} %get-tuple-element.98), channel_id=1, source_target_pairs={{0,32},{1,35},{2,34},{3,33},{4,36},{5,39},{6,38},{7,37},{8,40},{9,... | collective-permute-start | bytes 589832 | tf_op jit(solution)/shard_map/ppermute | solution.py:330
  53.3 5.3 %collective-permute-done.9.got1 = f32[320,128]{1,0:T(8,128)S(1)} collective-permute-done((f32[320,128]{1,0:T(8,128)S(1)}, f32[320,128]{1,0:T(8,128)S(1)}, u32[]{:S(2)}, u32[]{:S(2)}) %collective-permute-start.9) | collective-permute-done | bytes 163872 | tf_op jit(solution)/shard_map/ppermute | solution.py:330
  59.1 3.6 %collective-permute-start.10 = (f32[272,128]{1,0:T(8,128)S(1)}, f32[272,128]{1,0:T(8,128)S(1)}, u32[]{:S(2)}, u32[]{:S(2)}) collective-permute-start(f32[272,128]{1,0:T(8,128)S(1)} %get-tuple-element.79), channel_id=1, source_target_pairs={{0,4},{1,5},{2,6},{3,7},{4,0},{5,1},{6,2},{7,3},{8,12},{9,13},{10,... | collective-permute-start | bytes 417800 | tf_op jit(solution)/shard_map/ppermute | solution.py:330
  63.6 3.1 %collective-permute-done.10 = f32[272,128]{1,0:T(8,128)S(1)} collective-permute-done((f32[272,128]{1,0:T(8,128)S(1)}, f32[272,128]{1,0:T(8,128)S(1)}, u32[]{:S(2)}, u32[]{:S(2)}) %collective-permute-start.10) | collective-permute-done | bytes 139296 | tf_op jit(solution)/shard_map/ppermute | solution.py:330
  66.7 5.3 %collective-permute-start.11 = (f32[272,128]{1,0:T(8,128)S(1)}, f32[272,128]{1,0:T(8,128)S(1)}, u32[]{:S(2)}, u32[]{:S(2)}) collective-permute-start(f32[272,128]{1,0:T(8,128)S(1)} %add.38), channel_id=1, source_target_pairs={{0,12},{1,29},{2,14},{3,31},{4,8},{5,25},{6,10},{7,27},{8,4},{9,21... | collective-permute-start | bytes 417800 | tf_op jit(solution)/shard_map/ppermute | solution.py:330
  72.5 1.7 %collective-permute-start.24 = (f32[256,128]{1,0:T(8,128)S(1)}, f32[256,128]{1,0:T(8,128)S(1)}, u32[]{:S(2)}, u32[]{:S(2)}) collective-permute-start(f32[256,128]{1,0:T(8,128)S(1)} %get-tuple-element.104), channel_id=1, source_target_pairs={{0,4},{1,5},{2,6},{3,7},{4,0},{5,1},{6,2},{7,3},{8,12},{9,13},{10,... | collective-permute-start | bytes 393224 | tf_op jit(solution)/shard_map/ppermute | solution.py:330
  74.3 1.6 %collective-permute-done.11 = f32[272,128]{1,0:T(8,128)S(1)} collective-permute-done((f32[272,128]{1,0:T(8,128)S(1)}, f32[272,128]{1,0:T(8,128)S(1)}, u32[]{:S(2)}, u32[]{:S(2)}) %collective-permute-start.11) | collective-permute-done | bytes 139296 | tf_op jit(solution)/shard_map/ppermute | solution.py:330
  75.9 2.0 %collective-permute-start.12 = (f32[272,128]{1,0:T(8,128)S(1)}, f32[272,128]{1,0:T(8,128)S(1)}, u32[]{:S(2)}, u32[]{:S(2)}) collective-permute-start(f32[272,128]{1,0:T(8,128)S(1)} %add.39), channel_id=1, source_target_pairs={{0,28},{1,13},{2,30},{3,15},{4,24},{5,9},{6,26},{7,11},{8,20},{9,5... | collective-permute-start | bytes 417800 | tf_op jit(solution)/shard_map/ppermute | solution.py:330
  79.9 1.9 %collective-permute-done.12 = f32[272,128]{1,0:T(8,128)S(1)} collective-permute-done((f32[272,128]{1,0:T(8,128)S(1)}, f32[272,128]{1,0:T(8,128)S(1)}, u32[]{:S(2)}, u32[]{:S(2)}) %collective-permute-start.12) | collective-permute-done | bytes 139296 | tf_op jit(solution)/shard_map/ppermute | solution.py:330
  81.8 6.7 %collective-permute-start.13 = (f32[272,128]{1,0:T(8,128)S(1)}, f32[272,128]{1,0:T(8,128)S(1)}, u32[]{:S(2)}, u32[]{:S(2)}) collective-permute-start(f32[272,128]{1,0:T(8,128)S(1)} %add.40.mine), channel_id=1, source_target_pairs={{0,1},{1,0},{2,3},{3,2},{4,5},{5,4},{6,7},{7,6},{8,9},{9,8},{10,11... | collective-permute-start | bytes 417800 | tf_op jit(solution)/shard_map/ppermute | solution.py:330
  88.6 2.1 %collective-permute-start.26 = (f32[256,128]{1,0:T(8,128)S(1)}, f32[256,128]{1,0:T(8,128)S(1)}, u32[]{:S(2)}, u32[]{:S(2)}) collective-permute-start(f32[256,128]{1,0:T(8,128)S(1)} %add.42), channel_id=1, source_target_pairs={{0,28},{1,13},{2,30},{3,15},{4,24},{5,9},{6,26},{7,11},{8,20},{9,5... | collective-permute-start | bytes 393224 | tf_op jit(solution)/shard_map/ppermute | solution.py:330
  90.7 5.0 %collective-permute-done.26 = f32[256,128]{1,0:T(8,128)S(1)} collective-permute-done((f32[256,128]{1,0:T(8,128)S(1)}, f32[256,128]{1,0:T(8,128)S(1)}, u32[]{:S(2)}, u32[]{:S(2)}) %collective-permute-start.26) | collective-permute-done | bytes 131104 | tf_op jit(solution)/shard_map/ppermute | solution.py:330
  96.5 6.4 %shard_map.92 = (f32[256,256]{1,0:T(8,128)S(1)}, f32[256,256]{1,0:T(8,128)S(1)}) custom-call(s32[17]{0:T(128)S(1)} %stack.59.bits, f32[272,128]{1,0:T(8,128)S(1)} %add.40.mine, f32[272,128]{1,0:T(8,128)S(1)} %collective-permute-done.13.mate), custom_call_target="tpu_custom_call" | custom-call | flops 4026531840 | bytes 802816 | tf_op jit(solution)/shard_map/pallas_call | solution.py:282
  104.2 3.7 %collective-permute-done.28 = bf16[128,256]{1,0:T(8,128)(2,1)S(1)} collective-permute-done((bf16[128,256]{1,0:T(8,128)(2,1)S(1)}, bf16[128,256]{1,0:T(8,128)(2,1)S(1)}, u32[]{:S(2)}, u32[]{:S(2)}) %collective-permute-start.28) | collective-permute-done | bytes 65568 | tf_op jit(solution)/shard_map/ppermute | solution.py:330
  108.0 18.7 %all_to_all.5.mine = bf16[16,128,256]{2,1,0:T(8,128)(2,1)S(1)} all-to-all(bf16[16,128,256]{2,1,0:T(8,128)(2,1)S(1)} %broadcast_in_dim.2), channel_id=1, replica_groups=mesh['y'=4,'x_lo'=2,'z'=8,'x_hi'=2,'core'=2] {'y','x_lo','x_hi'}, dimensions={0} | all-to-all | bytes 2097152 | tf_op jit(solution)/shard_map/all_to_all | solution.py:406
  126.8 3.0 %collective-permute-start.29 = (bf16[16,128,256]{2,1,0:T(8,128)(2,1)S(1)}, bf16[16,128,256]{2,1,0:T(8,128)(2,1)S(1)}, u32[]{:S(2)}, u32[]{:S(2)}) collective-permute-start(bf16[16,128,256]{2,1,0:T(8,128)(2,1)S(1)} %all_to_all.5.mine), channel_id=1, source_target_pairs={{0,1},{1,0},{2,3},{3,2},{4,5},{5,4},{6,7},{7,6},{8,9},{9,8},{10,11... | collective-permute-start | bytes 3145736 | tf_op jit(solution)/shard_map/ppermute | solution.py:330
  129.7 2.4 %collective-permute-done.30.last_mate = bf16[128,256]{1,0:T(8,128)(2,1)S(1)} collective-permute-done((bf16[128,256]{1,0:T(8,128)(2,1)S(1)}, bf16[128,256]{1,0:T(8,128)(2,1)S(1)}, u32[]{:S(2)}, u32[]{:S(2)}) %collective-permute-start.30) | collective-permute-done | bytes 65568 | tf_op jit(solution)/shard_map/ppermute | solution.py:330
  132.1 2.1 %shard_map.101 = (bf16[1024,256]{1,0:T(8,128)(2,1)}, bf16[2304,256]{1,0:T(8,128)(2,1)}, bf16[256,1024]{1,0:T(8,128)(2,1)}) custom-call(s32[17]{0:T(128)S(1)} %stack.59.bits, bf16[16,128,256]{2,1,0:T(8,128)(2,1)S(1)} %all_to_all.5.mine, bf16[16,128,256]{2,1,0:T(8,128)(2,1)S(1)} %collective-permute-done.29.mate, bf16[128,256]{1,0:T(8,128)(2,1)S(1)} %get-tuple-element.105.last, ...), custom_call_target="tpu_custom_call" | custom-call | bytes 4456448 | tf_op jit(solution)/shard_map/pallas_call | solution.py:282
  (71 shorter events, 19.7 us)
Async XLA Ops:
  2.9 5.0 %copy-start.3 = (bf16[4,14,14,256]{3,0,2,1:T(4,128)(2,1)S(1)}, bf16[4,14,14,256]{3,0,2,1:T(4,128)(2,1)}, u32[]{:S(2)}) copy-start(bf16[4,14,14,256]{3,0,2,1:T(4,128)(2,1)} %param.9) | copy-start | bytes 1204228
  4.5 9.0 %collective-permute-start.1 = (f32[1360,128]{1,0:T(8,128)S(1)}, f32[1360,128]{1,0:T(8,128)S(1)}, u32[]{:S(2)}, u32[]{:S(2)}) collective-permute-start(f32[1360,128]{1,0:T(8,128)S(1)} %get-tuple-element.57), channel_id=1, source_target_pairs={{0,1},{1,0},{2,3},{3,2},{4,5},{5,4},{6,7},{7,6},{8,9},{9,8},{10,11... | collective-permute-start | bytes 2088968 | tf_op jit(solution)/shard_map/ppermute | solution.py:330
  12.3 3.0 %collective-permute-start = (f32[1360,128]{1,0:T(8,128)S(1)}, f32[1360,128]{1,0:T(8,128)S(1)}, u32[]{:S(2)}, u32[]{:S(2)}) collective-permute-start(f32[1360,128]{1,0:T(8,128)S(1)} %get-tuple-element.55), channel_id=1, source_target_pairs={{0,1},{1,0},{2,3},{3,2},{4,5},{5,4},{6,7},{7,6},{8,9},{9,8},{10,11... | collective-permute-start | bytes 2088968 | tf_op jit(solution)/shard_map/ppermute | solution.py:330
  18.2 6.3 %collective-permute-start.15 = (f32[2304,128]{1,0:T(8,128)S(1)}, f32[2304,128]{1,0:T(8,128)S(1)}, u32[]{:S(2)}, u32[]{:S(2)}) collective-permute-start(f32[2304,128]{1,0:T(8,128)S(1)} %get-tuple-element.86), channel_id=1, source_target_pairs={{0,1},{1,0},{2,3},{3,2},{4,5},{5,4},{6,7},{7,6},{8,9},{9,8},{10,11... | collective-permute-start | bytes 3538952 | tf_op jit(solution)/shard_map/ppermute | solution.py:330
  20.8 3.7 %collective-permute-start.14 = (f32[2048,128]{1,0:T(8,128)S(1)}, f32[2048,128]{1,0:T(8,128)S(1)}, u32[]{:S(2)}, u32[]{:S(2)}) collective-permute-start(f32[2048,128]{1,0:T(8,128)S(1)} %get-tuple-element.84), channel_id=1, source_target_pairs={{0,1},{1,0},{2,3},{3,2},{4,5},{5,4},{6,7},{7,6},{8,9},{9,8},{10,11... | collective-permute-start | bytes 3145736 | tf_op jit(solution)/shard_map/ppermute | solution.py:330
  21.0 8.7 %collective-permute-start.2 = (f32[864,128]{1,0:T(8,128)S(1)}, f32[864,128]{1,0:T(8,128)S(1)}, u32[]{:S(2)}, u32[]{:S(2)}) collective-permute-start(f32[864,128]{1,0:T(8,128)S(1)} %get-tuple-element.63), channel_id=1, source_target_pairs={{0,32},{1,35},{2,34},{3,33},{4,36},{5,39},{6,38},{7,37},{8,40},{9,... | collective-permute-start | bytes 1327112 | tf_op jit(solution)/shard_map/ppermute | solution.py:330
  21.8 7.9 %collective-permute-start.3 = (f32[768,128]{1,0:T(8,128)S(1)}, f32[768,128]{1,0:T(8,128)S(1)}, u32[]{:S(2)}, u32[]{:S(2)}) collective-permute-start(f32[768,128]{1,0:T(8,128)S(1)} %get-tuple-element.65), channel_id=1, source_target_pairs={{0,64},{1,193},{2,66},{3,195},{4,68},{5,197},{6,70},{7,199},{8,72}... | collective-permute-start | bytes 1179656 | tf_op jit(solution)/shard_map/ppermute | solution.py:330
  25.4 11.7 %collective-permute-start.16 = (f32[1152,128]{1,0:T(8,128)S(1)}, f32[1152,128]{1,0:T(8,128)S(1)}, u32[]{:S(2)}, u32[]{:S(2)}) collective-permute-start(f32[1152,128]{1,0:T(8,128)S(1)} %get-tuple-element.88), channel_id=1, source_target_pairs={{0,32},{1,35},{2,34},{3,33},{4,36},{5,39},{6,38},{7,37},{8,40},{9,... | collective-permute-start | bytes 1769480 | tf_op jit(solution)/shard_map/ppermute | solution.py:330
  25.7 11.5 %collective-permute-start.17 = (f32[1152,128]{1,0:T(8,128)S(1)}, f32[1152,128]{1,0:T(8,128)S(1)}, u32[]{:S(2)}, u32[]{:S(2)}) collective-permute-start(f32[1152,128]{1,0:T(8,128)S(1)} %get-tuple-element.90), channel_id=1, source_target_pairs={{0,64},{1,193},{2,66},{3,195},{4,68},{5,197},{6,70},{7,199},{8,72}... | collective-permute-start | bytes 1769480 | tf_op jit(solution)/shard_map/ppermute | solution.py:330
  30.3 8.5 %collective-permute-start.4 = (f32[576,128]{1,0:T(8,128)S(1)}, f32[576,128]{1,0:T(8,128)S(1)}, u32[]{:S(2)}, u32[]{:S(2)}) collective-permute-start(f32[576,128]{1,0:T(8,128)S(1)} %get-tuple-element.67), channel_id=1, source_target_pairs={{0,34},{1,33},{2,32},{3,35},{4,38},{5,37},{6,36},{7,39},{8,42},{9,... | collective-permute-start | bytes 884744 | tf_op jit(solution)/shard_map/ppermute | solution.py:330
  30.4 7.6 %collective-permute-start.5 = (f32[512,128]{1,0:T(8,128)S(1)}, f32[512,128]{1,0:T(8,128)S(1)}, u32[]{:S(2)}, u32[]{:S(2)}) collective-permute-start(f32[512,128]{1,0:T(8,128)S(1)} %get-tuple-element.69), channel_id=1, source_target_pairs={{0,192},{1,65},{2,194},{3,67},{4,196},{5,69},{6,198},{7,71},{8,200... | collective-permute-start | bytes 786440 | tf_op jit(solution)/shard_map/ppermute | solution.py:330
  37.8 12.5 %collective-permute-start.18 = (f32[640,128]{1,0:T(8,128)S(1)}, f32[640,128]{1,0:T(8,128)S(1)}, u32[]{:S(2)}, u32[]{:S(2)}) collective-permute-start(f32[640,128]{1,0:T(8,128)S(1)} %get-tuple-element.92), channel_id=1, source_target_pairs={{0,34},{1,33},{2,32},{3,35},{4,38},{5,37},{6,36},{7,39},{8,42},{9,... | collective-permute-start | bytes 983048 | tf_op jit(solution)/shard_map/ppermute | solution.py:330
  37.9 12.4 %collective-permute-start.19 = (f32[640,128]{1,0:T(8,128)S(1)}, f32[640,128]{1,0:T(8,128)S(1)}, u32[]{:S(2)}, u32[]{:S(2)}) collective-permute-start(f32[640,128]{1,0:T(8,128)S(1)} %get-tuple-element.94), channel_id=1, source_target_pairs={{0,192},{1,65},{2,194},{3,67},{4,196},{5,69},{6,198},{7,71},{8,200... | collective-permute-start | bytes 983048 | tf_op jit(solution)/shard_map/ppermute | solution.py:330
  39.4 9.8 %collective-permute-start.6 = (f32[432,128]{1,0:T(8,128)S(1)}, f32[432,128]{1,0:T(8,128)S(1)}, u32[]{:S(2)}, u32[]{:S(2)}) collective-permute-start(f32[432,128]{1,0:T(8,128)S(1)} %get-tuple-element.71), channel_id=1, source_target_pairs={{0,64},{1,193},{2,66},{3,195},{4,68},{5,197},{6,70},{7,199},{8,72}... | collective-permute-start | bytes 663560 | tf_op jit(solution)/shard_map/ppermute | solution.py:330
  41.1 8.1 %collective-permute-start.7 = (f32[384,128]{1,0:T(8,128)S(1)}, f32[384,128]{1,0:T(8,128)S(1)}, u32[]{:S(2)}, u32[]{:S(2)}) collective-permute-start(f32[384,128]{1,0:T(8,128)S(1)} %get-tuple-element.73), channel_id=1, source_target_pairs={{0,32},{1,35},{2,34},{3,33},{4,36},{5,39},{6,38},{7,37},{8,40},{9,... | collective-permute-start | bytes 589832 | tf_op jit(solution)/shard_map/ppermute | solution.py:330
  49.9 8.7 %collective-permute-start.8 = (f32[360,128]{1,0:T(8,128)S(1)}, f32[360,128]{1,0:T(8,128)S(1)}, u32[]{:S(2)}, u32[]{:S(2)}) collective-permute-start(f32[360,128]{1,0:T(8,128)S(1)} %get-tuple-element.75), channel_id=1, source_target_pairs={{0,192},{1,65},{2,194},{3,67},{4,196},{5,69},{6,198},{7,71},{8,200... | collective-permute-start | bytes 552968 | tf_op jit(solution)/shard_map/ppermute | solution.py:330
  50.9 11.9 %collective-permute-start.20 = (f32[384,128]{1,0:T(8,128)S(1)}, f32[384,128]{1,0:T(8,128)S(1)}, u32[]{:S(2)}, u32[]{:S(2)}) collective-permute-start(f32[384,128]{1,0:T(8,128)S(1)} %get-tuple-element.96), channel_id=1, source_target_pairs={{0,64},{1,193},{2,66},{3,195},{4,68},{5,197},{6,70},{7,199},{8,72}... | collective-permute-start | bytes 589832 | tf_op jit(solution)/shard_map/ppermute | solution.py:330
  51.8 11.0 %collective-permute-start.21 = (f32[384,128]{1,0:T(8,128)S(1)}, f32[384,128]{1,0:T(8,128)S(1)}, u32[]{:S(2)}, u32[]{:S(2)}) collective-permute-start(f32[384,128]{1,0:T(8,128)S(1)} %get-tuple-element.98), channel_id=1, source_target_pairs={{0,32},{1,35},{2,34},{3,33},{4,36},{5,39},{6,38},{7,37},{8,40},{9,... | collective-permute-start | bytes 589832 | tf_op jit(solution)/shard_map/ppermute | solution.py:330
  53.3 5.3 %collective-permute-start.9 = (f32[320,128]{1,0:T(8,128)S(1)}, f32[320,128]{1,0:T(8,128)S(1)}, u32[]{:S(2)}, u32[]{:S(2)}) collective-permute-start(f32[320,128]{1,0:T(8,128)S(1)} %get-tuple-element.77), channel_id=1, source_target_pairs={{0,34},{1,33},{2,32},{3,35},{4,38},{5,37},{6,36},{7,39},{8,42},{9,... | collective-permute-start | bytes 491528 | tf_op jit(solution)/shard_map/ppermute | solution.py:330
  59.1 7.5 %collective-permute-start.10 = (f32[272,128]{1,0:T(8,128)S(1)}, f32[272,128]{1,0:T(8,128)S(1)}, u32[]{:S(2)}, u32[]{:S(2)}) collective-permute-start(f32[272,128]{1,0:T(8,128)S(1)} %get-tuple-element.79), channel_id=1, source_target_pairs={{0,4},{1,5},{2,6},{3,7},{4,0},{5,1},{6,2},{7,3},{8,12},{9,13},{10,... | collective-permute-start | bytes 417800 | tf_op jit(solution)/shard_map/ppermute | solution.py:330
  63.4 8.6 %collective-permute-start.22 = (f32[256,128]{1,0:T(8,128)S(1)}, f32[256,128]{1,0:T(8,128)S(1)}, u32[]{:S(2)}, u32[]{:S(2)}) collective-permute-start(f32[256,128]{1,0:T(8,128)S(1)} %get-tuple-element.100), channel_id=1, source_target_pairs={{0,192},{1,65},{2,194},{3,67},{4,196},{5,69},{6,198},{7,71},{8,200... | collective-permute-start | bytes 393224 | tf_op jit(solution)/shard_map/ppermute | solution.py:330
  63.5 8.5 %collective-permute-start.23 = (f32[256,128]{1,0:T(8,128)S(1)}, f32[256,128]{1,0:T(8,128)S(1)}, u32[]{:S(2)}, u32[]{:S(2)}) collective-permute-start(f32[256,128]{1,0:T(8,128)S(1)} %get-tuple-element.102), channel_id=1, source_target_pairs={{0,34},{1,33},{2,32},{3,35},{4,38},{5,37},{6,36},{7,39},{8,42},{9,... | collective-permute-start | bytes 393224 | tf_op jit(solution)/shard_map/ppermute | solution.py:330
  66.7 9.2 %collective-permute-start.11 = (f32[272,128]{1,0:T(8,128)S(1)}, f32[272,128]{1,0:T(8,128)S(1)}, u32[]{:S(2)}, u32[]{:S(2)}) collective-permute-start(f32[272,128]{1,0:T(8,128)S(1)} %add.38), channel_id=1, source_target_pairs={{0,12},{1,29},{2,14},{3,31},{4,8},{5,25},{6,10},{7,27},{8,4},{9,21... | collective-permute-start | bytes 417800 | tf_op jit(solution)/shard_map/ppermute | solution.py:330
  72.5 6.5 %collective-permute-start.24 = (f32[256,128]{1,0:T(8,128)S(1)}, f32[256,128]{1,0:T(8,128)S(1)}, u32[]{:S(2)}, u32[]{:S(2)}) collective-permute-start(f32[256,128]{1,0:T(8,128)S(1)} %get-tuple-element.104), channel_id=1, source_target_pairs={{0,4},{1,5},{2,6},{3,7},{4,0},{5,1},{6,2},{7,3},{8,12},{9,13},{10,... | collective-permute-start | bytes 393224 | tf_op jit(solution)/shard_map/ppermute | solution.py:330
  75.9 5.9 %collective-permute-start.12 = (f32[272,128]{1,0:T(8,128)S(1)}, f32[272,128]{1,0:T(8,128)S(1)}, u32[]{:S(2)}, u32[]{:S(2)}) collective-permute-start(f32[272,128]{1,0:T(8,128)S(1)} %add.39), channel_id=1, source_target_pairs={{0,28},{1,13},{2,30},{3,15},{4,24},{5,9},{6,26},{7,11},{8,20},{9,5... | collective-permute-start | bytes 417800 | tf_op jit(solution)/shard_map/ppermute | solution.py:330
  79.0 9.5 %collective-permute-start.25 = (f32[256,128]{1,0:T(8,128)S(1)}, f32[256,128]{1,0:T(8,128)S(1)}, u32[]{:S(2)}, u32[]{:S(2)}) collective-permute-start(f32[256,128]{1,0:T(8,128)S(1)} %add.41), channel_id=1, source_target_pairs={{0,12},{1,29},{2,14},{3,31},{4,8},{5,25},{6,10},{7,27},{8,4},{9,21... | collective-permute-start | bytes 393224 | tf_op jit(solution)/shard_map/ppermute | solution.py:330
  81.8 14.7 %collective-permute-start.13 = (f32[272,128]{1,0:T(8,128)S(1)}, f32[272,128]{1,0:T(8,128)S(1)}, u32[]{:S(2)}, u32[]{:S(2)}) collective-permute-start(f32[272,128]{1,0:T(8,128)S(1)} %add.40.mine), channel_id=1, source_target_pairs={{0,1},{1,0},{2,3},{3,2},{4,5},{5,4},{6,7},{7,6},{8,9},{9,8},{10,11... | collective-permute-start | bytes 417800 | tf_op jit(solution)/shard_map/ppermute | solution.py:330
  88.6 7.1 %collective-permute-start.26 = (f32[256,128]{1,0:T(8,128)S(1)}, f32[256,128]{1,0:T(8,128)S(1)}, u32[]{:S(2)}, u32[]{:S(2)}) collective-permute-start(f32[256,128]{1,0:T(8,128)S(1)} %add.42), channel_id=1, source_target_pairs={{0,28},{1,13},{2,30},{3,15},{4,24},{5,9},{6,26},{7,11},{8,20},{9,5... | collective-permute-start | bytes 393224 | tf_op jit(solution)/shard_map/ppermute | solution.py:330
  95.7 7.2 %collective-permute-start.27 = (f32[256,128]{1,0:T(8,128)S(1)}, f32[256,128]{1,0:T(8,128)S(1)}, u32[]{:S(2)}, u32[]{:S(2)}) collective-permute-start(f32[256,128]{1,0:T(8,128)S(1)} %add.43.mine), channel_id=1, source_target_pairs={{0,1},{1,0},{2,3},{3,2},{4,5},{5,4},{6,7},{7,6},{8,9},{9,8},{10,11... | collective-permute-start | bytes 393224 | tf_op jit(solution)/shard_map/ppermute | solution.py:330
  104.1 3.8 %collective-permute-start.28 = (bf16[128,256]{1,0:T(8,128)(2,1)S(1)}, bf16[128,256]{1,0:T(8,128)(2,1)S(1)}, u32[]{:S(2)}, u32[]{:S(2)}) collective-permute-start(bf16[128,256]{1,0:T(8,128)(2,1)S(1)} %shard_map.100), channel_id=1, source_target_pairs={{0,4},{1,5},{2,6},{3,7},{4,0},{5,1},{6,2},{7,3},{8,12},{9,13},{10,... | collective-permute-start | bytes 196616 | tf_op jit(solution)/shard_map/ppermute | solution.py:330
  126.8 5.4 %collective-permute-start.29 = (bf16[16,128,256]{2,1,0:T(8,128)(2,1)S(1)}, bf16[16,128,256]{2,1,0:T(8,128)(2,1)S(1)}, u32[]{:S(2)}, u32[]{:S(2)}) collective-permute-start(bf16[16,128,256]{2,1,0:T(8,128)(2,1)S(1)} %all_to_all.5.mine), channel_id=1, source_target_pairs={{0,1},{1,0},{2,3},{3,2},{4,5},{5,4},{6,7},{7,6},{8,9},{9,8},{10,11... | collective-permute-start | bytes 3145736 | tf_op jit(solution)/shard_map/ppermute | solution.py:330
  129.7 2.4 %collective-permute-start.30 = (bf16[128,256]{1,0:T(8,128)(2,1)S(1)}, bf16[128,256]{1,0:T(8,128)(2,1)S(1)}, u32[]{:S(2)}, u32[]{:S(2)}) collective-permute-start(bf16[128,256]{1,0:T(8,128)(2,1)S(1)} %get-tuple-element.105.last), channel_id=1, source_target_pairs={{0,1},{1,0},{2,3},{3,2},{4,5},{5,4},{6,7},{7,6},{8,9},{9,8},{10,11... | collective-permute-start | bytes 196616 | tf_op jit(solution)/shard_map/ppermute | solution.py:330
  (3 other events, 9.9 us)

commit v2 on v1

--- a/solution.py
+++ b/solution.py
@@ -54,81 +54,67 @@
         put(side, keep, send, many * sum(TILE[:s]) + i * TILE[s], rows[:, :HALF], rows[:, HALF:])
 
 
-def widen(ref, pad):
-    images, h, w, c = ref.shape
-    pad[:, :w, :] = ref[...].reshape(images * h, w, c)
-    pad[:, w:, :] = jnp.zeros((images * h, 16 - w, c), BF16)
-
-
-def columns(pad, k):
-    return pad[:, :, MID * k : MID * k + MID].reshape(pad.shape[0] * 16, MID)
-
-
-def end_grams_kernel(bits, aw, an, g1, g3, keep, send, pw, pn, p1, p3):
-    side = bits[0] == 1
-    for ref, pad in ((aw, pw), (an, pn), (g1, p1), (g3, p3)):
-        widen(ref, pad)
-    blocks = [(pw, k) for k in range(4)] + [(p3, k) for k in range(4)] + [(p1, 0), (pn, 0)]
+def columns(ref, k=0):
+    h, w, n, _ = ref.shape
+    return ref[:, :, :, MID * k : MID * k + MID].reshape(h * w * n, MID)
+
+
+def end_grams_kernel(bits, aw, an, g1, g3, keep, send):
+    side = bits[0] == 1
+    blocks = [(aw, k) for k in range(4)] + [(g3, k) for k in range(4)] + [(g1, 0), (an, 0)]
     for i, block in enumerate(blocks):
         own = columns(*block)
         put_gram(side, keep, send, 10, i, dot_t(own, own))
 
 
-def end_tiles_kernel(bits, aw, an, g1, g3, keep, send, pw, pn, p1, p3):
-    side = bits[0] == 1
-    for ref, pad in ((aw, pw), (an, pn), (g1, p1), (g3, p3)):
-        widen(ref, pad)
-    first_out, third_in = columns(p1, 0), columns(pn, 0)
+def end_tiles_kernel(bits, aw, an, g1, g3, keep, send):
+    side = bits[0] == 1
+    first_out, third_in = columns(g1), columns(an)
     for q in range(8):
-        tile = dot_t(columns(pw, q), first_out) if q < 4 else dot_t(third_in, columns(p3, q - 4))
+        tile = dot_t(columns(aw, q), first_out) if q < 4 else dot_t(third_in, columns(g3, q - 4))
         put_tile(side, keep, send, 8, q, tile)
 
 
-def shift(am, shifted):
-    images, h, w, c = am.shape
-    shifted[1, :, :, :] = jnp.zeros(shifted.shape[1:], BF16)
-    for n in range(images):
-        shifted[1, 1 + n * (h + 1) : 1 + n * (h + 1) + h, :w, :] = am[n]
-    whole = shifted[1].astype(F32)
-    j = lax.broadcasted_iota(jnp.int32, whole.shape, 1)
-    shifted[0] = jnp.where(j < w, pltpu.roll(whole, 1, 1), 0.0).astype(BF16)
-    shifted[2] = jnp.where(j < w, pltpu.roll(whole, 15, 1), 0.0).astype(BF16)
-
-
-def spread(g2, grads):
-    images, h, w, c = g2.shape
-    grads[...] = jnp.zeros(grads.shape, BF16)
-    for n in range(images):
-        grads[n * (h + 1) : n * (h + 1) + h, :w, :] = g2[n]
-    return grads[...].reshape(grads.shape[0] * 16, c)
-
-
-def patch_grams_kernel(bits, am, g2, keep, send, shifted, grads):
-    side = bits[0] == 1
-    images, h, w, c = am.shape
-    shift(am, shifted)
-    second_out = spread(g2, grads)
+def widen(value, before):
+    h, w, n, c = value.shape
+    blank = lambda k: [jnp.zeros((h, k, n, c), BF16)] if k else []
+    return jnp.concatenate(blank(before) + [value] + blank(16 - w - before), axis=1).reshape(h * 16 * n, c)
+
+
+def shift(am, lines):
+    h, w, n, c = am.shape
+    step = 16 * n
+    whole = am[...]
+    for dx, moved in enumerate((widen(whole[:, : w - 1], 1), widen(whole, 0), widen(whole[:, 1:], 0))):
+        lines[dx, :step, :] = jnp.zeros((step, c), BF16)
+        lines[dx, step : step + h * step, :] = moved
+        lines[dx, step + h * step :, :] = jnp.zeros((step, c), BF16)
+    return step
+
+
+def patch_grams_kernel(bits, am, g2, keep, send, lines):
+    side = bits[0] == 1
+    step = shift(am, lines)
+    second_out = columns(g2)
     put_gram(side, keep, send, 10, 9, dot_t(second_out, second_out))
+    end = step * (am.shape[0] + 1)
     for dx in range(3):
-        def picked(lo, hi):
-            parts = [shifted[dx, 1 + n * (h + 1) + lo : 1 + n * (h + 1) + hi] for n in range(images)]
-            return jnp.concatenate(parts, axis=0).reshape(images * (hi - lo) * 16, c)
-
-        top, inner, bottom = (dot_t(x, x) for x in (picked(0, 1), picked(1, h - 1), picked(h - 1, h)))
+        cuts = (step, 2 * step), (2 * step, end - step), (end - step, end)
+        top, inner, bottom = (dot_t(lines[dx, lo:hi, :], lines[dx, lo:hi, :]) for lo, hi in cuts)
         upper = inner + top
         put_gram(side, keep, send, 10, dx, upper)
         put_gram(side, keep, send, 10, 3 + dx, upper + bottom)
         put_gram(side, keep, send, 10, 6 + dx, inner + bottom)
 
 
-def patch_tiles_kernel(bits, am, g2, keep, send, shifted, grads):
-    side = bits[0] == 1
-    shift(am, shifted)
-    second_out = spread(g2, grads)
-    span, c = grads.shape[0], am.shape[3]
+def patch_tiles_kernel(bits, am, g2, keep, send, lines):
+    side = bits[0] == 1
+    step = shift(am, lines)
+    second_out = widen(g2[...], 0)
+    span = second_out.shape[0]
     for q in range(9):
-        patch = shifted[q % 3, q // 3 : q // 3 + span].reshape(span * 16, c)
-        put_tile(side, keep, send, 9, q, dot_t(patch, second_out))
+        at = step * (q // 3)
+        put_tile(side, keep, send, 9, q, dot_t(lines[q % 3, at : at + span, :], second_out))
 
 
 def first_split_kernel(rec, many, extra, bits, keep0, got0, keep1, got1, *outs):
@@ -196,6 +182,18 @@
         put(side, keep, send, n * s, mine[:n, :] + got[:n, :], mine[n:, :] + got[n:, :])
 
 
+def halves(x):
+    high = x.astype(BF16)
+    return high, (x - high.astype(F32)).astype(BF16)
+
+
+def mm3(a, b):
+    (ah, al), (bh, bl) = halves(a), halves(b)
+    return jnp.dot(ah, bh, preferred_element_type=F32) + (
+        jnp.dot(ah, bl, preferred_element_type=F32) + jnp.dot(al, bh, preferred_element_type=F32)
+    )
+
+
 def mm(a, b):
     return jnp.dot(a, b, precision=lax.Precision.HIGHEST, preferred_element_type=F32)
 
@@ -233,8 +231,9 @@
     powers = [own[0], shared[0]]
     sums = [jnp.where(r == c, 1.0, 0.0) + e for e in powers]
     for step in range(1, NS_ITERS):
-        powers = [mm(e, e) for e in powers]
-        sums = [x + mm(x, e) for x, e in zip(sums, powers)]
+        times = mm if step < 3 else mm3
+        powers = [times(e, e) for e in powers]
+        sums = [x + mm3(x, e) for x, e in zip(sums, powers)]
     own, shared = sums[0] / own[1], sums[1] / shared[1]
     third = bits[7] == 1
     left_out[...] = jnp.where(third, shared, own)
@@ -286,7 +285,7 @@
         out_specs=tuple([VMEM] * len(outs)) if many else VMEM,
         scratch_shapes=list(scratch),
         compiler_params=pltpu.CompilerParams(vmem_limit_bytes=size * 5 // 4 + held + room * 2**20),
-        cost_estimate=pl.CostEstimate(flops=flops, bytes_accessed=size, transcendentals=0),
+        cost_estimate=pl.CostEstimate(flops=flops, bytes_accessed=size if flops else 1024, transcendentals=0),
     )(bits, *args)
 
 
@@ -317,9 +316,16 @@
 ROUTE_XY = [
     [route(lambda y, x, z, c: MOVE[ORDER[c][s][step]](y, x, z, c)) for step in range(4)] for s in range(SETS)
 ]
-ROUTE_Z1 = route(lambda y, x, z, c: (y, x, z ^ 1, c))
-ROUTE_Z2 = route(lambda y, x, z, c: (y, x, 7 - z if c else z ^ 3, c))
-ROUTE_Z3 = route(lambda y, x, z, c: (y, x, z ^ 3 if c else 7 - z, c))
+STEP_Z = (
+    lambda z: z ^ 1,
+    lambda z: z - 1 + 2 * (z % 2),
+    lambda z: z ^ 2,
+    lambda z: z - 2 + 4 * (z // 2 % 2),
+)
+ROUTE_Z1, ROUTE_Z2, ROUTE_Z3 = (
+    [(d, device_of(*(lambda y, x, z, c: (y, x, STEP_Z[pair[c]](z) % 8, c))(*place_of(d)))) for d in range(256)]
+    for pair in ((0, 1), (2, 3), (3, 2))
+)
 
 
 def tile_of(y, x):
@@ -339,7 +345,7 @@
     q = tile_of(y, x)
     own = [(q >> i) & 1 for i in range(4)]
     turns = [jnp.where(core == 1, own[ORDER[1][s][k]], own[ORDER[0][s][k]]) for s in range(SETS) for k in range(4)]
-    odd = ((z + 1) >> 1) & 1
+    odd = z & 1
     kind = jnp.where(q < 4, 0, jnp.where(q < 8, 1, 2))
     third = jnp.where((kind == 1) & (odd == 0), 1, 0)
     bits = jnp.stack([core, *own, odd, kind, third, q, *turns]).astype(jnp.int32)
@@ -347,25 +353,26 @@
     def shape(*dims):
         return jax.ShapeDtypeStruct(dims, F32)
 
-    lines, span = images * height, images * (height + 1)
-    pads = [pltpu.VMEM((lines, 16, n), BF16) for n in (wide, middle, middle, wide)]
-    maps = [pltpu.VMEM((3, span + 2, 16, middle), BF16), pltpu.VMEM((span, 16, middle), BF16)]
-    ends = (act_wide, act_narrow, grad_first, grad_third)
-    patches = (act_middle, grad_second)
+    maps = [pltpu.VMEM((3, (height + 2) * 16 * images, middle), BF16)]
+    ends = [a.transpose(1, 2, 0, 3) for a in (act_wide, act_narrow, grad_first, grad_third)]
+    patches = [a.transpose(1, 2, 0, 3) for a in (act_middle, grad_second)]
 
     def pairs(rec, records):
         return [shape(records * rec[s], HALF) for s in range(SETS) for _ in range(2)]
 
     def start(rec, many, extra, kernels, bits):
         parts = []
-        for part, args, scratch in ((1, patches, maps), (0, ends, pads)):
+        for part, args, scratch in ((1, patches, maps), (0, ends, ())):
             outs = [shape(many[part] * sum(rec), HALF)] * 2
-            keep, send = call(kernels[part], bits, args, outs, scratch, 2 * many[part] * 900 * 65536)
+            keep, send = call(kernels[part], bits[part], args, outs, scratch, 2 * many[part] * 900 * 65536)
             parts = [keep, send_to(send, ROUTE_C)] + parts
+        return parts
+
+    def begin(rec, many, extra, parts):
         outs = pairs(rec, 8 + len(extra))
         return call(functools.partial(first_split_kernel, rec, many, extra), bits, parts, outs)
 
-    def chain(rec, extra, held, leaf):
+    def chain(rec, extra, held, leaf, meanwhile=()):
         for step in range(4):
             args = []
             for s in range(SETS):
@@ -376,29 +383,32 @@
         keep, send = call(leaf, bits, args, [shape(size, HALF)] * 2)
         total = keep + send_to(send, ROUTE_Z1)
         total = total + send_to(total, ROUTE_Z2)
-        total = total + send_to(total, ROUTE_Z3)
-        return total, send_to(total, ROUTE_C)
+        got, *meanwhile = lax.optimization_barrier((send_to(total, ROUTE_Z3), *meanwhile))
+        total = total + got
+        return (total, send_to(total, ROUTE_C), *meanwhile)
 
     shared = ((1, 8), (0, 8), (0, 9), (1, 9))
-    held = start(GRAM, (10, 10), shared, (end_grams_kernel, patch_grams_kernel), bits)
-    *held, later = lax.optimization_barrier((*held, bits))
+    gram_parts = start(GRAM, (10, 10), shared, (end_grams_kernel, patch_grams_kernel), (bits, bits))
+    got0, later0 = lax.optimization_barrier((gram_parts[1], bits))
+    got1, later1 = lax.optimization_barrier((gram_parts[3], bits))
+    gram_parts = [gram_parts[0], got0, gram_parts[2], got1]
+    tile_parts = start(TILE, (8, 9), ((1, 8),), (end_tiles_kernel, patch_tiles_kernel), (later0, later1))
+    held = begin(GRAM, (10, 10), shared, gram_parts)
     grams = chain(GRAM, 4, held, gram_leaf_kernel)
-    held = start(TILE, (8, 9), ((1, 8),), (end_tiles_kernel, patch_tiles_kernel), later)
-    tiles = chain(TILE, 1, held, tile_leaf_kernel)
+    held = begin(TILE, (8, 9), ((1, 8),), tile_parts)
     inverses = call(
         functools.partial(inverse_kernel, count),
         bits,
         grams,
         [shape(MID, MID)] * 2,
-        flops=2 * 20 * 6 * MID**3,
         room=16,
     )
+    *tiles, left, right = chain(TILE, 1, held, tile_leaf_kernel, inverses)
     mine = call(
         functools.partial(apply_kernel, count),
         bits,
-        (*inverses, *tiles),
+        (left, right, *tiles),
         [jax.ShapeDtypeStruct((HALF, MID), BF16)],
-        flops=2 * 6 * MID**3,
     )
     other = send_to(mine, ROUTE_Z1)
     tile, last = jnp.where(odd == 0, mine, other), jnp.where(odd == 0, other, mine)

time: 134 us -> 125 us (0.933)
  waiting for transfers between devices: 40.9 us -> 36.1 us
  Pallas kernels: 24.3 us -> 21.8 us
  local copies, waits for them, and re-layouts: 4.38 us -> 2.21 us
    ppermute x31, waiting for transfers between devices: 40.9 us -> 36.1 us  [send_to(): return lax.ppermute(value, AXES, way)]
    pallas_call x17, Pallas kernels: 24.3 us -> 21.8 us  [call(): pl.pallas_call(kernel, out_shape=tuple(outs) if many else outs[0], in_spe...]
    unnamed x14 -> x16, local copies, waits for them, and re-layouts: 4.19 us -> 2.02 us
  transfers between devices with their start and end apart: 31 -> 31, of which waited for: 13 -> 12; matrix products, arithmetic and copies ran while one was open for 1% -> 0% of each run, Pallas kernels for 12% -> 14%
where the time goes in v2:
time: 125 us; the launch traced here: 124 us
  starting transfers between devices  45.9 us (37%)
  waiting for transfers between devices  36.1 us (29%)
  Pallas kernels  21.8 us (17%)
  blocking collectives  17.4 us (14%)
  local copies, waits for them, and re-layouts  2.21 us (2%)
    ppermute x31, starting transfers between devices, send_to(): return lax.ppermute(value, AXES, way)  45.9 us
    ppermute x31, waiting for transfers between devices, send_to(): return lax.ppermute(value, AXES, way)  36.1 us
    pallas_call x17, Pallas kernels, call(): pl.pallas_call(kernel, out_shape=tuple(outs) if many else outs[0], in_spe...  21.8 us
    all_to_all x1, blocking collectives, on_device(): tiles = lax.all_to_all(tiles, ('y', 'x_lo', 'x_hi'), 0, 0)  17.4 us
  transfers between devices with their start and end apart: 31, of which 12 were waited for; matrix products, arithmetic and copies ran while one was open for 0% of the time, Pallas kernels for 14%

profile of v2, /device:TPU:1, one launch (start us, length us, event | category | flops | bytes accessed | tf_op | source)
XLA Modules:
  0.0 124.5 jit_solution(17570035533876371407)
XLA Ops:
  2.8 1.6 %shard_map.87 = (f32[1360,128]{1,0:T(8,128)S(1)}, f32[1360,128]{1,0:T(8,128)S(1)}) custom-call(s32[17]{0:T(128)S(1)} %stack.59.bits, bf16[14,14,4,256]{3,2,1,0:T(4,128)(2,1)S(1)} %bitcast.27, bf16[14,14,4,256]{3,2,1,0:T(4,128)(2,1)S(1)} %bitcast.29), custom_call_target="tpu_custom_call" | custom-call | flops 1179648000 | bytes 2195456 | tf_op jit(solution)/shard_map/pallas_call | solution.py:281
  4.4 3.3 %collective-permute-start.2 = (f32[1360,128]{1,0:T(8,128)S(1)}, f32[1360,128]{1,0:T(8,128)S(1)}, u32[]{:S(2)}, u32[]{:S(2)}) collective-permute-start(f32[1360,128]{1,0:T(8,128)S(1)} %get-tuple-element.60), channel_id=1, source_target_pairs={{0,1},{1,0},{2,3},{3,2},{4,5},{5,4},{6,7},{7,6},{8,9},{9,8},{10,11... | collective-permute-start | bytes 2088968 | tf_op jit(solution)/shard_map/ppermute | solution.py:336
  7.7 2.2 %shard_map.85 = (f32[1360,128]{1,0:T(8,128)S(1)}, f32[1360,128]{1,0:T(8,128)S(1)}) custom-call(s32[17]{0:T(128)S(1)} %stack.59.bits, bf16[14,14,4,1024]{3,2,1,0:T(4,128)(2,1)S(1)} %bitcast.19, bf16[14,14,4,256]{3,2,1,0:T(4,128)(2,1)S(1)} %bitcast.23, bf16[14,14,4,256]{3,2,1,0:T(4,128)(2,1)S(1)} %bitcast.25, bf16[14,14,4,1024]{3,2,1,0:T(4,128)(2,1)S(1)} %bitcast.21), custom_call_target="tpu_custom_call" | custom-call | flops 1179648000 | bytes 5406720 | tf_op jit(solution)/shard_map/pallas_call | solution.py:281
  10.4 2.1 %shard_map.88 = (f32[2304,128]{1,0:T(8,128)S(1)}, f32[2304,128]{1,0:T(8,128)S(1)}) custom-call(s32[17]{0:T(128)S(1)} %stack.59.bits, bf16[14,14,4,256]{3,2,1,0:T(4,128)(2,1)S(1)} %bitcast.28, bf16[14,14,4,256]{3,2,1,0:T(4,128)(2,1)S(1)} %bitcast.30), custom_call_target="tpu_custom_call" | custom-call | flops 1061683200 | bytes 3162112 | tf_op jit(solution)/shard_map/pallas_call | solution.py:281
  12.7 1.9 %shard_map.86 = (f32[2048,128]{1,0:T(8,128)S(1)}, f32[2048,128]{1,0:T(8,128)S(1)}) custom-call(s32[17]{0:T(128)S(1)} %stack.59.bits, bf16[14,14,4,1024]{3,2,1,0:T(4,128)(2,1)S(1)} %bitcast.20, bf16[14,14,4,256]{3,2,1,0:T(4,128)(2,1)S(1)} %bitcast.24, bf16[14,14,4,256]{3,2,1,0:T(4,128)(2,1)S(1)} %bitcast.26, bf16[14,14,4,1024]{3,2,1,0:T(4,128)(2,1)S(1)} %bitcast.22), custom_call_target="tpu_custom_call" | custom-call | flops 943718400 | bytes 6111232 | tf_op jit(solution)/shard_map/pallas_call | solution.py:281
  16.6 2.7 %collective-permute-start.16 = (f32[768,128]{1,0:T(8,128)S(1)}, f32[768,128]{1,0:T(8,128)S(1)}, u32[]{:S(2)}, u32[]{:S(2)}) collective-permute-start(f32[768,128]{1,0:T(8,128)S(1)} %get-tuple-element.89), channel_id=1, source_target_pairs={{0,64},{1,193},{2,66},{3,195},{4,68},{5,197},{6,70},{7,199},{8,72}... | collective-permute-start | bytes 1179656 | tf_op jit(solution)/shard_map/ppermute | solution.py:336
  20.4 1.7 %collective-permute-start.5 = (f32[1152,128]{1,0:T(8,128)S(1)}, f32[1152,128]{1,0:T(8,128)S(1)}, u32[]{:S(2)}, u32[]{:S(2)}) collective-permute-start(f32[1152,128]{1,0:T(8,128)S(1)} %get-tuple-element.67), channel_id=1, source_target_pairs={{0,64},{1,193},{2,66},{3,195},{4,68},{5,197},{6,70},{7,199},{8,72}... | collective-permute-start | bytes 1769480 | tf_op jit(solution)/shard_map/ppermute | solution.py:336
  22.1 2.4 %collective-permute-done.16.refs_3_ = f32[768,128]{1,0:T(8,128)S(1)} collective-permute-done((f32[768,128]{1,0:T(8,128)S(1)}, f32[768,128]{1,0:T(8,128)S(1)}, u32[]{:S(2)}, u32[]{:S(2)}) %collective-permute-start.16) | collective-permute-done | bytes 393248 | tf_op jit(solution)/shard_map/ppermute | solution.py:336
  25.6 6.5 %collective-permute-done.4.refs_1_ = f32[1152,128]{1,0:T(8,128)S(1)} collective-permute-done((f32[1152,128]{1,0:T(8,128)S(1)}, f32[1152,128]{1,0:T(8,128)S(1)}, u32[]{:S(2)}, u32[]{:S(2)}) %collective-permute-start.4) | collective-permute-done | bytes 589856 | tf_op jit(solution)/shard_map/ppermute | solution.py:336
  34.0 1.8 %collective-permute-start.19 = (f32[432,128]{1,0:T(8,128)S(1)}, f32[432,128]{1,0:T(8,128)S(1)}, u32[]{:S(2)}, u32[]{:S(2)}) collective-permute-start(f32[432,128]{1,0:T(8,128)S(1)} %get-tuple-element.95), channel_id=1, source_target_pairs={{0,64},{1,193},{2,66},{3,195},{4,68},{5,197},{6,70},{7,199},{8,72}... | collective-permute-start | bytes 663560 | tf_op jit(solution)/shard_map/ppermute | solution.py:336
  35.8 1.8 %collective-permute-start.20 = (f32[384,128]{1,0:T(8,128)S(1)}, f32[384,128]{1,0:T(8,128)S(1)}, u32[]{:S(2)}, u32[]{:S(2)}) collective-permute-start(f32[384,128]{1,0:T(8,128)S(1)} %get-tuple-element.97), channel_id=1, source_target_pairs={{0,32},{1,35},{2,34},{3,33},{4,36},{5,39},{6,38},{7,37},{8,40},{9,... | collective-permute-start | bytes 589832 | tf_op jit(solution)/shard_map/ppermute | solution.py:336
  37.5 6.2 %collective-permute-done.20.refs_3_ = f32[384,128]{1,0:T(8,128)S(1)} collective-permute-done((f32[384,128]{1,0:T(8,128)S(1)}, f32[384,128]{1,0:T(8,128)S(1)}, u32[]{:S(2)}, u32[]{:S(2)}) %collective-permute-start.20) | collective-permute-done | bytes 196640 | tf_op jit(solution)/shard_map/ppermute | solution.py:336
  45.4 1.6 %collective-permute-start.8 = (f32[384,128]{1,0:T(8,128)S(1)}, f32[384,128]{1,0:T(8,128)S(1)}, u32[]{:S(2)}, u32[]{:S(2)}) collective-permute-start(f32[384,128]{1,0:T(8,128)S(1)} %get-tuple-element.73), channel_id=1, source_target_pairs={{0,64},{1,193},{2,66},{3,195},{4,68},{5,197},{6,70},{7,199},{8,72}... | collective-permute-start | bytes 589832 | tf_op jit(solution)/shard_map/ppermute | solution.py:336
  47.0 1.7 %collective-permute-start.9 = (f32[384,128]{1,0:T(8,128)S(1)}, f32[384,128]{1,0:T(8,128)S(1)}, u32[]{:S(2)}, u32[]{:S(2)}) collective-permute-start(f32[384,128]{1,0:T(8,128)S(1)} %get-tuple-element.75), channel_id=1, source_target_pairs={{0,32},{1,35},{2,34},{3,33},{4,36},{5,39},{6,38},{7,37},{8,40},{9,... | collective-permute-start | bytes 589832 | tf_op jit(solution)/shard_map/ppermute | solution.py:336
  48.7 6.2 %collective-permute-done.22.got1 = f32[320,128]{1,0:T(8,128)S(1)} collective-permute-done((f32[320,128]{1,0:T(8,128)S(1)}, f32[320,128]{1,0:T(8,128)S(1)}, u32[]{:S(2)}, u32[]{:S(2)}) %collective-permute-start.22) | collective-permute-done | bytes 163872 | tf_op jit(solution)/shard_map/ppermute | solution.py:336
  55.5 5.8 %collective-permute-start.23 = (f32[272,128]{1,0:T(8,128)S(1)}, f32[272,128]{1,0:T(8,128)S(1)}, u32[]{:S(2)}, u32[]{:S(2)}) collective-permute-start(f32[272,128]{1,0:T(8,128)S(1)} %get-tuple-element.103), channel_id=1, source_target_pairs={{0,4},{1,29},{2,6},{3,31},{4,0},{5,9},{6,2},{7,11},{8,12},{9,5},{1... | collective-permute-start | bytes 417800 | tf_op jit(solution)/shard_map/ppermute | solution.py:336
  62.3 1.7 %collective-permute-done.23 = f32[272,128]{1,0:T(8,128)S(1)} collective-permute-done((f32[272,128]{1,0:T(8,128)S(1)}, f32[272,128]{1,0:T(8,128)S(1)}, u32[]{:S(2)}, u32[]{:S(2)}) %collective-permute-start.23) | collective-permute-done | bytes 139296 | tf_op jit(solution)/shard_map/ppermute | solution.py:336
  64.0 2.0 %collective-permute-start.24 = (f32[272,128]{1,0:T(8,128)S(1)}, f32[272,128]{1,0:T(8,128)S(1)}, u32[]{:S(2)}, u32[]{:S(2)}) collective-permute-start(f32[272,128]{1,0:T(8,128)S(1)} %add.36), channel_id=1, source_target_pairs={{0,8},{1,25},{2,10},{3,27},{4,12},{5,29},{6,14},{7,31},{8,0},{9,17... | collective-permute-start | bytes 417800 | tf_op jit(solution)/shard_map/ppermute | solution.py:336
  67.2 3.0 %collective-permute-done.24 = f32[272,128]{1,0:T(8,128)S(1)} collective-permute-done((f32[272,128]{1,0:T(8,128)S(1)}, f32[272,128]{1,0:T(8,128)S(1)}, u32[]{:S(2)}, u32[]{:S(2)}) %collective-permute-start.24) | collective-permute-done | bytes 139296 | tf_op jit(solution)/shard_map/ppermute | solution.py:336
  70.2 1.9 %collective-permute-start.25 = (f32[272,128]{1,0:T(8,128)S(1)}, f32[272,128]{1,0:T(8,128)S(1)}, u32[]{:S(2)}, u32[]{:S(2)}) collective-permute-start(f32[272,128]{1,0:T(8,128)S(1)} %add.37), channel_id=1, source_target_pairs={{0,24},{1,9},{2,26},{3,11},{4,28},{5,13},{6,30},{7,15},{8,16},{9,1... | collective-permute-start | bytes 417800 | tf_op jit(solution)/shard_map/ppermute | solution.py:336
  72.1 3.0 %collective-permute-start.13 = (f32[256,128]{1,0:T(8,128)S(1)}, f32[256,128]{1,0:T(8,128)S(1)}, u32[]{:S(2)}, u32[]{:S(2)}) collective-permute-start(f32[256,128]{1,0:T(8,128)S(1)} %add.34), channel_id=1, source_target_pairs={{0,8},{1,25},{2,10},{3,27},{4,12},{5,29},{6,14},{7,31},{8,0},{9,17... | collective-permute-start | bytes 393224 | tf_op jit(solution)/shard_map/ppermute | solution.py:336
  75.1 1.7 %collective-permute-done.25 = f32[272,128]{1,0:T(8,128)S(1)} collective-permute-done((f32[272,128]{1,0:T(8,128)S(1)}, f32[272,128]{1,0:T(8,128)S(1)}, u32[]{:S(2)}, u32[]{:S(2)}) %collective-permute-start.25) | collective-permute-done | bytes 139296 | tf_op jit(solution)/shard_map/ppermute | solution.py:336
  76.9 5.1 %collective-permute-start.26 = (f32[272,128]{1,0:T(8,128)S(1)}, f32[272,128]{1,0:T(8,128)S(1)}, u32[]{:S(2)}, u32[]{:S(2)}) collective-permute-start(f32[272,128]{1,0:T(8,128)S(1)} %add.38.mine), channel_id=1, source_target_pairs={{0,1},{1,0},{2,3},{3,2},{4,5},{5,4},{6,7},{7,6},{8,9},{9,8},{10,11... | collective-permute-start | bytes 417800 | tf_op jit(solution)/shard_map/ppermute | solution.py:336
  82.0 2.9 %collective-permute-start.14 = (f32[256,128]{1,0:T(8,128)S(1)}, f32[256,128]{1,0:T(8,128)S(1)}, u32[]{:S(2)}, u32[]{:S(2)}) collective-permute-start(f32[256,128]{1,0:T(8,128)S(1)} %add.35), channel_id=1, source_target_pairs={{0,24},{1,9},{2,26},{3,11},{4,28},{5,13},{6,30},{7,15},{8,16},{9,1... | collective-permute-start | bytes 393224 | tf_op jit(solution)/shard_map/ppermute | solution.py:336
  84.9 4.5 %shard_map.99 = (f32[256,256]{1,0:T(8,128)S(1)}, f32[256,256]{1,0:T(8,128)S(1)}) custom-call(s32[17]{0:T(128)S(1)} %stack.59.bits, f32[272,128]{1,0:T(8,128)S(1)} %add.38.mine, f32[272,128]{1,0:T(8,128)S(1)} %collective-permute-done.26.mate), custom_call_target="tpu_custom_call" | custom-call | bytes 1024 | tf_op jit(solution)/shard_map/pallas_call | solution.py:281
  89.4 3.1 %collective-permute-start.27 = (f32[256,128]{1,0:T(8,128)S(1)}, f32[256,128]{1,0:T(8,128)S(1)}, u32[]{:S(2)}, u32[]{:S(2)}) collective-permute-start(f32[256,128]{1,0:T(8,128)S(1)} %add.39.mine), channel_id=1, source_target_pairs={{0,1},{1,0},{2,3},{3,2},{4,5},{5,4},{6,7},{7,6},{8,9},{9,8},{10,11... | collective-permute-start | bytes 393224 | tf_op jit(solution)/shard_map/ppermute | solution.py:336
  93.5 1.2 shard_map.100
  94.8 4.3 %collective-permute-done.28 = bf16[128,256]{1,0:T(8,128)(2,1)S(1)} collective-permute-done((bf16[128,256]{1,0:T(8,128)(2,1)S(1)}, bf16[128,256]{1,0:T(8,128)(2,1)S(1)}, u32[]{:S(2)}, u32[]{:S(2)}) %collective-permute-start.28) | collective-permute-done | bytes 65568 | tf_op jit(solution)/shard_map/ppermute | solution.py:336
  99.2 17.4 %all_to_all.5.mine = bf16[16,128,256]{2,1,0:T(8,128)(2,1)S(1)} all-to-all(bf16[16,128,256]{2,1,0:T(8,128)(2,1)S(1)} %broadcast_in_dim.2), channel_id=1, replica_groups=mesh['y'=4,'x_lo'=2,'z'=8,'x_hi'=2,'core'=2] {'y','x_lo','x_hi'}, dimensions={0} | all-to-all | bytes 2097152 | tf_op jit(solution)/shard_map/all_to_all | solution.py:416
  116.6 3.4 %collective-permute-start.29 = (bf16[16,128,256]{2,1,0:T(8,128)(2,1)S(1)}, bf16[16,128,256]{2,1,0:T(8,128)(2,1)S(1)}, u32[]{:S(2)}, u32[]{:S(2)}) collective-permute-start(bf16[16,128,256]{2,1,0:T(8,128)(2,1)S(1)} %all_to_all.5.mine), channel_id=1, source_target_pairs={{0,1},{1,0},{2,3},{3,2},{4,5},{5,4},{6,7},{7,6},{8,9},{9,8},{10,11... | collective-permute-start | bytes 3145736 | tf_op jit(solution)/shard_map/ppermute | solution.py:336
  120.0 2.4 %collective-permute-done.30.last_mate = bf16[128,256]{1,0:T(8,128)(2,1)S(1)} collective-permute-done((bf16[128,256]{1,0:T(8,128)(2,1)S(1)}, bf16[128,256]{1,0:T(8,128)(2,1)S(1)}, u32[]{:S(2)}, u32[]{:S(2)}) %collective-permute-start.30) | collective-permute-done | bytes 65568 | tf_op jit(solution)/shard_map/ppermute | solution.py:336
  122.3 2.1 %shard_map.101 = (bf16[1024,256]{1,0:T(8,128)(2,1)}, bf16[2304,256]{1,0:T(8,128)(2,1)}, bf16[256,1024]{1,0:T(8,128)(2,1)}) custom-call(s32[17]{0:T(128)S(1)} %stack.59.bits, bf16[16,128,256]{2,1,0:T(8,128)(2,1)S(1)} %all_to_all.5.mine, bf16[16,128,256]{2,1,0:T(8,128)(2,1)S(1)} %collective-permute-done.29.mate, bf16[128,256]{1,0:T(8,128)(2,1)S(1)} %get-tuple-element.109.last, ...), custom_call_target="tpu_custom_call" | custom-call | bytes 1024 | tf_op jit(solution)/shard_map/pallas_call | solution.py:281
  (73 shorter events, 14.6 us)
Async XLA Ops:
  2.8 4.9 %copy-start.3 = (bf16[4,14,14,256]{3,0,2,1:T(4,128)(2,1)S(1)}, bf16[4,14,14,256]{3,0,2,1:T(4,128)(2,1)}, u32[]{:S(2)}) copy-start(bf16[4,14,14,256]{3,0,2,1:T(4,128)(2,1)} %param.9) | copy-start | bytes 1204228
  4.4 6.0 %collective-permute-start.2 = (f32[1360,128]{1,0:T(8,128)S(1)}, f32[1360,128]{1,0:T(8,128)S(1)}, u32[]{:S(2)}, u32[]{:S(2)}) collective-permute-start(f32[1360,128]{1,0:T(8,128)S(1)} %get-tuple-element.60), channel_id=1, source_target_pairs={{0,1},{1,0},{2,3},{3,2},{4,5},{5,4},{6,7},{7,6},{8,9},{9,8},{10,11... | collective-permute-start | bytes 2088968 | tf_op jit(solution)/shard_map/ppermute | solution.py:336
  9.9 2.8 %collective-permute-start = (f32[1360,128]{1,0:T(8,128)S(1)}, f32[1360,128]{1,0:T(8,128)S(1)}, u32[]{:S(2)}, u32[]{:S(2)}) collective-permute-start(f32[1360,128]{1,0:T(8,128)S(1)} %get-tuple-element.56), channel_id=1, source_target_pairs={{0,1},{1,0},{2,3},{3,2},{4,5},{5,4},{6,7},{7,6},{8,9},{9,8},{10,11... | collective-permute-start | bytes 2088968 | tf_op jit(solution)/shard_map/ppermute | solution.py:336
  12.5 6.8 %collective-permute-start.3 = (f32[2304,128]{1,0:T(8,128)S(1)}, f32[2304,128]{1,0:T(8,128)S(1)}, u32[]{:S(2)}, u32[]{:S(2)}) collective-permute-start(f32[2304,128]{1,0:T(8,128)S(1)} %get-tuple-element.63), channel_id=1, source_target_pairs={{0,1},{1,0},{2,3},{3,2},{4,5},{5,4},{6,7},{7,6},{8,9},{9,8},{10,11... | collective-permute-start | bytes 3538952 | tf_op jit(solution)/shard_map/ppermute | solution.py:336
  14.6 4.7 %collective-permute-start.1 = (f32[2048,128]{1,0:T(8,128)S(1)}, f32[2048,128]{1,0:T(8,128)S(1)}, u32[]{:S(2)}, u32[]{:S(2)}) collective-permute-start(f32[2048,128]{1,0:T(8,128)S(1)} %get-tuple-element.59), channel_id=1, source_target_pairs={{0,1},{1,0},{2,3},{3,2},{4,5},{5,4},{6,7},{7,6},{8,9},{9,8},{10,11... | collective-permute-start | bytes 3145736 | tf_op jit(solution)/shard_map/ppermute | solution.py:336
  15.7 8.7 %collective-permute-start.15 = (f32[864,128]{1,0:T(8,128)S(1)}, f32[864,128]{1,0:T(8,128)S(1)}, u32[]{:S(2)}, u32[]{:S(2)}) collective-permute-start(f32[864,128]{1,0:T(8,128)S(1)} %get-tuple-element.87), channel_id=1, source_target_pairs={{0,32},{1,35},{2,34},{3,33},{4,36},{5,39},{6,38},{7,37},{8,40},{9,... | collective-permute-start | bytes 1327112 | tf_op jit(solution)/shard_map/ppermute | solution.py:336
  16.6 7.9 %collective-permute-start.16 = (f32[768,128]{1,0:T(8,128)S(1)}, f32[768,128]{1,0:T(8,128)S(1)}, u32[]{:S(2)}, u32[]{:S(2)}) collective-permute-start(f32[768,128]{1,0:T(8,128)S(1)} %get-tuple-element.89), channel_id=1, source_target_pairs={{0,64},{1,193},{2,66},{3,195},{4,68},{5,197},{6,70},{7,199},{8,72}... | collective-permute-start | bytes 1179656 | tf_op jit(solution)/shard_map/ppermute | solution.py:336
  20.1 12.0 %collective-permute-start.4 = (f32[1152,128]{1,0:T(8,128)S(1)}, f32[1152,128]{1,0:T(8,128)S(1)}, u32[]{:S(2)}, u32[]{:S(2)}) collective-permute-start(f32[1152,128]{1,0:T(8,128)S(1)} %get-tuple-element.65), channel_id=1, source_target_pairs={{0,32},{1,35},{2,34},{3,33},{4,36},{5,39},{6,38},{7,37},{8,40},{9,... | collective-permute-start | bytes 1769480 | tf_op jit(solution)/shard_map/ppermute | solution.py:336
  20.4 11.7 %collective-permute-start.5 = (f32[1152,128]{1,0:T(8,128)S(1)}, f32[1152,128]{1,0:T(8,128)S(1)}, u32[]{:S(2)}, u32[]{:S(2)}) collective-permute-start(f32[1152,128]{1,0:T(8,128)S(1)} %get-tuple-element.67), channel_id=1, source_target_pairs={{0,64},{1,193},{2,66},{3,195},{4,68},{5,197},{6,70},{7,199},{8,72}... | collective-permute-start | bytes 1769480 | tf_op jit(solution)/shard_map/ppermute | solution.py:336
  25.1 8.2 %collective-permute-start.17 = (f32[576,128]{1,0:T(8,128)S(1)}, f32[576,128]{1,0:T(8,128)S(1)}, u32[]{:S(2)}, u32[]{:S(2)}) collective-permute-start(f32[576,128]{1,0:T(8,128)S(1)} %get-tuple-element.91), channel_id=1, source_target_pairs={{0,34},{1,33},{2,32},{3,35},{4,38},{5,37},{6,36},{7,39},{8,42},{9,... | collective-permute-start | bytes 884744 | tf_op jit(solution)/shard_map/ppermute | solution.py:336
  25.2 8.0 %collective-permute-start.18 = (f32[512,128]{1,0:T(8,128)S(1)}, f32[512,128]{1,0:T(8,128)S(1)}, u32[]{:S(2)}, u32[]{:S(2)}) collective-permute-start(f32[512,128]{1,0:T(8,128)S(1)} %get-tuple-element.93), channel_id=1, source_target_pairs={{0,192},{1,65},{2,194},{3,67},{4,196},{5,69},{6,198},{7,71},{8,200... | collective-permute-start | bytes 786440 | tf_op jit(solution)/shard_map/ppermute | solution.py:336
  32.8 12.0 %collective-permute-start.6 = (f32[640,128]{1,0:T(8,128)S(1)}, f32[640,128]{1,0:T(8,128)S(1)}, u32[]{:S(2)}, u32[]{:S(2)}) collective-permute-start(f32[640,128]{1,0:T(8,128)S(1)} %get-tuple-element.69), channel_id=1, source_target_pairs={{0,34},{1,33},{2,32},{3,35},{4,38},{5,37},{6,36},{7,39},{8,42},{9,... | collective-permute-start | bytes 983048 | tf_op jit(solution)/shard_map/ppermute | solution.py:336
  33.1 11.7 %collective-permute-start.7 = (f32[640,128]{1,0:T(8,128)S(1)}, f32[640,128]{1,0:T(8,128)S(1)}, u32[]{:S(2)}, u32[]{:S(2)}) collective-permute-start(f32[640,128]{1,0:T(8,128)S(1)} %get-tuple-element.71), channel_id=1, source_target_pairs={{0,192},{1,65},{2,194},{3,67},{4,196},{5,69},{6,198},{7,71},{8,200... | collective-permute-start | bytes 983048 | tf_op jit(solution)/shard_map/ppermute | solution.py:336
  34.0 9.8 %collective-permute-start.19 = (f32[432,128]{1,0:T(8,128)S(1)}, f32[432,128]{1,0:T(8,128)S(1)}, u32[]{:S(2)}, u32[]{:S(2)}) collective-permute-start(f32[432,128]{1,0:T(8,128)S(1)} %get-tuple-element.95), channel_id=1, source_target_pairs={{0,64},{1,193},{2,66},{3,195},{4,68},{5,197},{6,70},{7,199},{8,72}... | collective-permute-start | bytes 663560 | tf_op jit(solution)/shard_map/ppermute | solution.py:336
  35.8 8.0 %collective-permute-start.20 = (f32[384,128]{1,0:T(8,128)S(1)}, f32[384,128]{1,0:T(8,128)S(1)}, u32[]{:S(2)}, u32[]{:S(2)}) collective-permute-start(f32[384,128]{1,0:T(8,128)S(1)} %get-tuple-element.97), channel_id=1, source_target_pairs={{0,32},{1,35},{2,34},{3,33},{4,36},{5,39},{6,38},{7,37},{8,40},{9,... | collective-permute-start | bytes 589832 | tf_op jit(solution)/shard_map/ppermute | solution.py:336
  44.4 10.5 %collective-permute-start.21 = (f32[360,128]{1,0:T(8,128)S(1)}, f32[360,128]{1,0:T(8,128)S(1)}, u32[]{:S(2)}, u32[]{:S(2)}) collective-permute-start(f32[360,128]{1,0:T(8,128)S(1)} %get-tuple-element.99), channel_id=1, source_target_pairs={{0,192},{1,65},{2,194},{3,67},{4,196},{5,69},{6,198},{7,71},{8,200... | collective-permute-start | bytes 552968 | tf_op jit(solution)/shard_map/ppermute | solution.py:336
  45.4 15.8 %collective-permute-start.8 = (f32[384,128]{1,0:T(8,128)S(1)}, f32[384,128]{1,0:T(8,128)S(1)}, u32[]{:S(2)}, u32[]{:S(2)}) collective-permute-start(f32[384,128]{1,0:T(8,128)S(1)} %get-tuple-element.73), channel_id=1, source_target_pairs={{0,64},{1,193},{2,66},{3,195},{4,68},{5,197},{6,70},{7,199},{8,72}... | collective-permute-start | bytes 589832 | tf_op jit(solution)/shard_map/ppermute | solution.py:336
  47.0 14.3 %collective-permute-start.9 = (f32[384,128]{1,0:T(8,128)S(1)}, f32[384,128]{1,0:T(8,128)S(1)}, u32[]{:S(2)}, u32[]{:S(2)}) collective-permute-start(f32[384,128]{1,0:T(8,128)S(1)} %get-tuple-element.75), channel_id=1, source_target_pairs={{0,32},{1,35},{2,34},{3,33},{4,36},{5,39},{6,38},{7,37},{8,40},{9,... | collective-permute-start | bytes 589832 | tf_op jit(solution)/shard_map/ppermute | solution.py:336
  48.7 6.2 %collective-permute-start.22 = (f32[320,128]{1,0:T(8,128)S(1)}, f32[320,128]{1,0:T(8,128)S(1)}, u32[]{:S(2)}, u32[]{:S(2)}) collective-permute-start(f32[320,128]{1,0:T(8,128)S(1)} %get-tuple-element.101), channel_id=1, source_target_pairs={{0,34},{1,33},{2,32},{3,35},{4,38},{5,37},{6,36},{7,39},{8,42},{9,... | collective-permute-start | bytes 491528 | tf_op jit(solution)/shard_map/ppermute | solution.py:336
  55.5 8.5 %collective-permute-start.23 = (f32[272,128]{1,0:T(8,128)S(1)}, f32[272,128]{1,0:T(8,128)S(1)}, u32[]{:S(2)}, u32[]{:S(2)}) collective-permute-start(f32[272,128]{1,0:T(8,128)S(1)} %get-tuple-element.103), channel_id=1, source_target_pairs={{0,4},{1,29},{2,6},{3,31},{4,0},{5,9},{6,2},{7,11},{8,12},{9,5},{1... | collective-permute-start | bytes 417800 | tf_op jit(solution)/shard_map/ppermute | solution.py:336
  61.8 4.2 %collective-permute-start.10 = (f32[256,128]{1,0:T(8,128)S(1)}, f32[256,128]{1,0:T(8,128)S(1)}, u32[]{:S(2)}, u32[]{:S(2)}) collective-permute-start(f32[256,128]{1,0:T(8,128)S(1)} %get-tuple-element.77), channel_id=1, source_target_pairs={{0,192},{1,65},{2,194},{3,67},{4,196},{5,69},{6,198},{7,71},{8,200... | collective-permute-start | bytes 393224 | tf_op jit(solution)/shard_map/ppermute | solution.py:336
  62.2 4.1 %collective-permute-start.11 = (f32[256,128]{1,0:T(8,128)S(1)}, f32[256,128]{1,0:T(8,128)S(1)}, u32[]{:S(2)}, u32[]{:S(2)}) collective-permute-start(f32[256,128]{1,0:T(8,128)S(1)} %get-tuple-element.79), channel_id=1, source_target_pairs={{0,34},{1,33},{2,32},{3,35},{4,38},{5,37},{6,36},{7,39},{8,42},{9,... | collective-permute-start | bytes 393224 | tf_op jit(solution)/shard_map/ppermute | solution.py:336
  64.0 6.2 %collective-permute-start.24 = (f32[272,128]{1,0:T(8,128)S(1)}, f32[272,128]{1,0:T(8,128)S(1)}, u32[]{:S(2)}, u32[]{:S(2)}) collective-permute-start(f32[272,128]{1,0:T(8,128)S(1)} %add.36), channel_id=1, source_target_pairs={{0,8},{1,25},{2,10},{3,27},{4,12},{5,29},{6,14},{7,31},{8,0},{9,17... | collective-permute-start | bytes 417800 | tf_op jit(solution)/shard_map/ppermute | solution.py:336
  66.9 5.2 %collective-permute-start.12 = (f32[256,128]{1,0:T(8,128)S(1)}, f32[256,128]{1,0:T(8,128)S(1)}, u32[]{:S(2)}, u32[]{:S(2)}) collective-permute-start(f32[256,128]{1,0:T(8,128)S(1)} %get-tuple-element.81), channel_id=1, source_target_pairs={{0,4},{1,29},{2,6},{3,31},{4,0},{5,9},{6,2},{7,11},{8,12},{9,5},{1... | collective-permute-start | bytes 393224 | tf_op jit(solution)/shard_map/ppermute | solution.py:336
  70.2 6.7 %collective-permute-start.25 = (f32[272,128]{1,0:T(8,128)S(1)}, f32[272,128]{1,0:T(8,128)S(1)}, u32[]{:S(2)}, u32[]{:S(2)}) collective-permute-start(f32[272,128]{1,0:T(8,128)S(1)} %add.37), channel_id=1, source_target_pairs={{0,24},{1,9},{2,26},{3,11},{4,28},{5,13},{6,30},{7,15},{8,16},{9,1... | collective-permute-start | bytes 417800 | tf_op jit(solution)/shard_map/ppermute | solution.py:336
  72.1 9.8 %collective-permute-start.13 = (f32[256,128]{1,0:T(8,128)S(1)}, f32[256,128]{1,0:T(8,128)S(1)}, u32[]{:S(2)}, u32[]{:S(2)}) collective-permute-start(f32[256,128]{1,0:T(8,128)S(1)} %add.34), channel_id=1, source_target_pairs={{0,8},{1,25},{2,10},{3,27},{4,12},{5,29},{6,14},{7,31},{8,0},{9,17... | collective-permute-start | bytes 393224 | tf_op jit(solution)/shard_map/ppermute | solution.py:336
  76.9 8.0 %collective-permute-start.26 = (f32[272,128]{1,0:T(8,128)S(1)}, f32[272,128]{1,0:T(8,128)S(1)}, u32[]{:S(2)}, u32[]{:S(2)}) collective-permute-start(f32[272,128]{1,0:T(8,128)S(1)} %add.38.mine), channel_id=1, source_target_pairs={{0,1},{1,0},{2,3},{3,2},{4,5},{5,4},{6,7},{7,6},{8,9},{9,8},{10,11... | collective-permute-start | bytes 417800 | tf_op jit(solution)/shard_map/ppermute | solution.py:336
  82.0 7.3 %collective-permute-start.14 = (f32[256,128]{1,0:T(8,128)S(1)}, f32[256,128]{1,0:T(8,128)S(1)}, u32[]{:S(2)}, u32[]{:S(2)}) collective-permute-start(f32[256,128]{1,0:T(8,128)S(1)} %add.35), channel_id=1, source_target_pairs={{0,24},{1,9},{2,26},{3,11},{4,28},{5,13},{6,30},{7,15},{8,16},{9,1... | collective-permute-start | bytes 393224 | tf_op jit(solution)/shard_map/ppermute | solution.py:336
  89.4 4.1 %collective-permute-start.27 = (f32[256,128]{1,0:T(8,128)S(1)}, f32[256,128]{1,0:T(8,128)S(1)}, u32[]{:S(2)}, u32[]{:S(2)}) collective-permute-start(f32[256,128]{1,0:T(8,128)S(1)} %add.39.mine), channel_id=1, source_target_pairs={{0,1},{1,0},{2,3},{3,2},{4,5},{5,4},{6,7},{7,6},{8,9},{9,8},{10,11... | collective-permute-start | bytes 393224 | tf_op jit(solution)/shard_map/ppermute | solution.py:336
  94.7 4.4 %collective-permute-start.28 = (bf16[128,256]{1,0:T(8,128)(2,1)S(1)}, bf16[128,256]{1,0:T(8,128)(2,1)S(1)}, u32[]{:S(2)}, u32[]{:S(2)}) collective-permute-start(bf16[128,256]{1,0:T(8,128)(2,1)S(1)} %shard_map.100), channel_id=1, source_target_pairs={{0,4},{1,29},{2,6},{3,31},{4,0},{5,9},{6,2},{7,11},{8,12},{9,5},{1... | collective-permute-start | bytes 196616 | tf_op jit(solution)/shard_map/ppermute | solution.py:336
  116.6 5.7 %collective-permute-start.29 = (bf16[16,128,256]{2,1,0:T(8,128)(2,1)S(1)}, bf16[16,128,256]{2,1,0:T(8,128)(2,1)S(1)}, u32[]{:S(2)}, u32[]{:S(2)}) collective-permute-start(bf16[16,128,256]{2,1,0:T(8,128)(2,1)S(1)} %all_to_all.5.mine), channel_id=1, source_target_pairs={{0,1},{1,0},{2,3},{3,2},{4,5},{5,4},{6,7},{7,6},{8,9},{9,8},{10,11... | collective-permute-start | bytes 3145736 | tf_op jit(solution)/shard_map/ppermute | solution.py:336
  120.0 2.4 %collective-permute-start.30 = (bf16[128,256]{1,0:T(8,128)(2,1)S(1)}, bf16[128,256]{1,0:T(8,128)(2,1)S(1)}, u32[]{:S(2)}, u32[]{:S(2)}) collective-permute-start(bf16[128,256]{1,0:T(8,128)(2,1)S(1)} %get-tuple-element.109.last), channel_id=1, source_target_pairs={{0,1},{1,0},{2,3},{3,2},{4,5},{5,4},{6,7},{7,6},{8,9},{9,8},{10,11... | collective-permute-start | bytes 196616 | tf_op jit(solution)/shard_map/ppermute | solution.py:336
  (7 other events, 22.0 us)

commit v3 on v2

--- a/solution.py
+++ b/solution.py
@@ -84,16 +84,16 @@
 def shift(am, lines):
     h, w, n, c = am.shape
     step = 16 * n
-    whole = am[...]
-    for dx, moved in enumerate((widen(whole[:, : w - 1], 1), widen(whole, 0), widen(whole[:, 1:], 0))):
+    for dx, moved in enumerate((widen(am[:, : w - 1], 1), widen(am, 0), widen(am[:, 1:], 0))):
         lines[dx, :step, :] = jnp.zeros((step, c), BF16)
         lines[dx, step : step + h * step, :] = moved
         lines[dx, step + h * step :, :] = jnp.zeros((step, c), BF16)
     return step
 
 
-def patch_grams_kernel(bits, am, g2, keep, send, lines):
-    side = bits[0] == 1
+def patch_grams_kernel(bits, both, keep, send, lines):
+    side = bits[0] == 1
+    am, g2 = both[: both.shape[0] // 2], both[both.shape[0] // 2 :]
     step = shift(am, lines)
     second_out = columns(g2)
     put_gram(side, keep, send, 10, 9, dot_t(second_out, second_out))
@@ -107,10 +107,11 @@
         put_gram(side, keep, send, 10, 6 + dx, inner + bottom)
 
 
-def patch_tiles_kernel(bits, am, g2, keep, send, lines):
-    side = bits[0] == 1
+def patch_tiles_kernel(bits, both, keep, send, lines):
+    side = bits[0] == 1
+    am, g2 = both[: both.shape[0] // 2], both[both.shape[0] // 2 :]
     step = shift(am, lines)
-    second_out = widen(g2[...], 0)
+    second_out = widen(g2, 0)
     span = second_out.shape[0]
     for q in range(9):
         at = step * (q // 3)
@@ -285,7 +286,7 @@
         out_specs=tuple([VMEM] * len(outs)) if many else VMEM,
         scratch_shapes=list(scratch),
         compiler_params=pltpu.CompilerParams(vmem_limit_bytes=size * 5 // 4 + held + room * 2**20),
-        cost_estimate=pl.CostEstimate(flops=flops, bytes_accessed=size if flops else 1024, transcendentals=0),
+        cost_estimate=pl.CostEstimate(flops=flops or 7 * 10**8, bytes_accessed=size if flops else 1024, transcendentals=0),
     )(bits, *args)
 
 
@@ -316,16 +317,9 @@
 ROUTE_XY = [
     [route(lambda y, x, z, c: MOVE[ORDER[c][s][step]](y, x, z, c)) for step in range(4)] for s in range(SETS)
 ]
-STEP_Z = (
-    lambda z: z ^ 1,
-    lambda z: z - 1 + 2 * (z % 2),
-    lambda z: z ^ 2,
-    lambda z: z - 2 + 4 * (z // 2 % 2),
-)
-ROUTE_Z1, ROUTE_Z2, ROUTE_Z3 = (
-    [(d, device_of(*(lambda y, x, z, c: (y, x, STEP_Z[pair[c]](z) % 8, c))(*place_of(d)))) for d in range(256)]
-    for pair in ((0, 1), (2, 3), (3, 2))
-)
+ROUTE_Z1 = route(lambda y, x, z, c: (y, x, z ^ 1, c))
+ROUTE_Z2 = route(lambda y, x, z, c: (y, x, (z - 1 + 2 * (z % 2)) % 8, c))
+ROUTE_Z3 = route(lambda y, x, z, c: (y, x, (3, 6, 5, 0, 7, 2, 1, 4)[z], c))
 
 
 def tile_of(y, x):
@@ -345,7 +339,7 @@
     q = tile_of(y, x)
     own = [(q >> i) & 1 for i in range(4)]
     turns = [jnp.where(core == 1, own[ORDER[1][s][k]], own[ORDER[0][s][k]]) for s in range(SETS) for k in range(4)]
-    odd = z & 1
+    odd = ((z + 1) >> 1) & 1
     kind = jnp.where(q < 4, 0, jnp.where(q < 8, 1, 2))
     third = jnp.where((kind == 1) & (odd == 0), 1, 0)
     bits = jnp.stack([core, *own, odd, kind, third, q, *turns]).astype(jnp.int32)
@@ -355,7 +349,7 @@
 
     maps = [pltpu.VMEM((3, (height + 2) * 16 * images, middle), BF16)]
     ends = [a.transpose(1, 2, 0, 3) for a in (act_wide, act_narrow, grad_first, grad_third)]
-    patches = [a.transpose(1, 2, 0, 3) for a in (act_middle, grad_second)]
+    patches = [jnp.concatenate([a.transpose(1, 2, 0, 3) for a in (act_middle, grad_second)], axis=0)]
 
     def pairs(rec, records):
         return [shape(records * rec[s], HALF) for s in range(SETS) for _ in range(2)]

time: 125 us -> 121 us (0.968)
  waiting for transfers between devices: 36.1 us -> 25.3 us
  starting transfers between devices: 45.9 us -> 52.1 us
  local copies, waits for them, and re-layouts: 2.21 us -> 0.21 us
  other arithmetic: 0.12 us -> 1.77 us
    ppermute x31, waiting for transfers between devices: 36.1 us -> 25.3 us  [send_to(): return lax.ppermute(value, AXES, way)]
    ppermute x31, starting transfers between devices: 45.9 us -> 52.1 us  [send_to(): return lax.ppermute(value, AXES, way)]
    unnamed x16 -> x8, local copies, waits for them, and re-layouts: 2.02 us -> 0.03 us
    concatenate x0 -> x1, other arithmetic: none -> 1.64 us  [on_device(): jnp.concatenate([a.transpose(1, 2, 0, 3) for a in (act_middle, grad_secon...]
  transfers between devices with their start and end apart: 31 -> 31, of which waited for: 12 -> 13; matrix products, arithmetic and copies ran while one was open for 0% -> 0% of each run, Pallas kernels for 14% -> 14%
where the time goes in v3:
time: 121 us
  starting transfers between devices  52.1 us (43%)
  waiting for transfers between devices  25.3 us (21%)
  Pallas kernels  21.8 us (18%)
  blocking collectives  18.6 us (15%)
  other arithmetic  1.77 us (1%)
    ppermute x31, starting transfers between devices, send_to(): return lax.ppermute(value, AXES, way)  52.1 us
    ppermute x31, waiting for transfers between devices, send_to(): return lax.ppermute(value, AXES, way)  25.3 us
    pallas_call x17, Pallas kernels, call(): pl.pallas_call(kernel, out_shape=tuple(outs) if many else outs[0], in_spe...  21.8 us
    all_to_all x1, blocking collectives, on_device(): tiles = lax.all_to_all(tiles, ('y', 'x_lo', 'x_hi'), 0, 0)  18.6 us
  transfers between devices with their start and end apart: 31, of which 13 were waited for; matrix products, arithmetic and copies ran while one was open for 0% of the time, Pallas kernels for 14%

profile of v3, /device:TPU:1, one launch (start us, length us, event | category | flops | bytes accessed | tf_op | source)
XLA Modules:
  0.0 120.8 jit_solution(8492125543590819428)
XLA Ops:
  0.7 1.6 %pad_maximum_fusion.both = bf16[28,14,4,256]{3,2,1,0:T(4,128)(2,1)S(1)} fusion(bf16[14,14,4,256]{3,2,1,0:T(4,128)(2,1)} %bitcast.27, bf16[14,14,4,256]{3,2,1,0:T(4,128)(2,1)} %bitcast.28), kind=kLoop, calls=%fused_computation | loop fusion | flops 401408 | bytes 1605632 | tf_op jit(solution)/shard_map/concatenate | solution.py:352
  2.5 1.6 %shard_map.87 = (f32[1360,128]{1,0:T(8,128)S(1)}, f32[1360,128]{1,0:T(8,128)S(1)}) custom-call(s32[17]{0:T(128)S(1)} %stack.59.bits, bf16[28,14,4,256]{3,2,1,0:T(4,128)(2,1)S(1)} %pad_maximum_fusion.both), custom_call_target="tpu_custom_call" | custom-call | flops 1179648000 | bytes 2195456 | tf_op jit(solution)/shard_map/pallas_call | solution.py:282
  4.0 3.3 %collective-permute-start.2 = (f32[1360,128]{1,0:T(8,128)S(1)}, f32[1360,128]{1,0:T(8,128)S(1)}, u32[]{:S(2)}, u32[]{:S(2)}) collective-permute-start(f32[1360,128]{1,0:T(8,128)S(1)} %get-tuple-element.60), channel_id=1, source_target_pairs={{0,1},{1,0},{2,3},{3,2},{4,5},{5,4},{6,7},{7,6},{8,9},{9,8},{10,11... | collective-permute-start | bytes 2088968 | tf_op jit(solution)/shard_map/ppermute | solution.py:330
  7.4 2.2 %shard_map.85 = (f32[1360,128]{1,0:T(8,128)S(1)}, f32[1360,128]{1,0:T(8,128)S(1)}) custom-call(s32[17]{0:T(128)S(1)} %stack.59.bits, bf16[14,14,4,1024]{3,2,1,0:T(4,128)(2,1)S(1)} %bitcast.19, bf16[14,14,4,256]{3,2,1,0:T(4,128)(2,1)S(1)} %bitcast.23, bf16[14,14,4,256]{3,2,1,0:T(4,128)(2,1)S(1)} %bitcast.25, bf16[14,14,4,1024]{3,2,1,0:T(4,128)(2,1)S(1)} %bitcast.21), custom_call_target="tpu_custom_call" | custom-call | flops 1179648000 | bytes 5406720 | tf_op jit(solution)/shard_map/pallas_call | solution.py:282
  10.0 2.1 %shard_map.88 = (f32[2304,128]{1,0:T(8,128)S(1)}, f32[2304,128]{1,0:T(8,128)S(1)}) custom-call(s32[17]{0:T(128)S(1)} %stack.59.bits, bf16[28,14,4,256]{3,2,1,0:T(4,128)(2,1)S(1)} %pad_maximum_fusion.both), custom_call_target="tpu_custom_call" | custom-call | flops 1061683200 | bytes 3162112 | tf_op jit(solution)/shard_map/pallas_call | solution.py:282
  12.3 1.9 %shard_map.86 = (f32[2048,128]{1,0:T(8,128)S(1)}, f32[2048,128]{1,0:T(8,128)S(1)}) custom-call(s32[17]{0:T(128)S(1)} %stack.59.bits, bf16[14,14,4,1024]{3,2,1,0:T(4,128)(2,1)S(1)} %bitcast.20, bf16[14,14,4,256]{3,2,1,0:T(4,128)(2,1)S(1)} %bitcast.24, bf16[14,14,4,256]{3,2,1,0:T(4,128)(2,1)S(1)} %bitcast.26, bf16[14,14,4,1024]{3,2,1,0:T(4,128)(2,1)S(1)} %bitcast.22), custom_call_target="tpu_custom_call" | custom-call | flops 943718400 | bytes 6111232 | tf_op jit(solution)/shard_map/pallas_call | solution.py:282
  16.2 2.7 %collective-permute-start.16 = (f32[768,128]{1,0:T(8,128)S(1)}, f32[768,128]{1,0:T(8,128)S(1)}, u32[]{:S(2)}, u32[]{:S(2)}) collective-permute-start(f32[768,128]{1,0:T(8,128)S(1)} %get-tuple-element.89), channel_id=1, source_target_pairs={{0,64},{1,193},{2,66},{3,195},{4,68},{5,197},{6,70},{7,199},{8,72}... | collective-permute-start | bytes 1179656 | tf_op jit(solution)/shard_map/ppermute | solution.py:330
  20.0 1.7 %collective-permute-start.5 = (f32[1152,128]{1,0:T(8,128)S(1)}, f32[1152,128]{1,0:T(8,128)S(1)}, u32[]{:S(2)}, u32[]{:S(2)}) collective-permute-start(f32[1152,128]{1,0:T(8,128)S(1)} %get-tuple-element.67), channel_id=1, source_target_pairs={{0,64},{1,193},{2,66},{3,195},{4,68},{5,197},{6,70},{7,199},{8,72}... | collective-permute-start | bytes 1769480 | tf_op jit(solution)/shard_map/ppermute | solution.py:330
  21.7 2.4 %collective-permute-done.16.refs_3_ = f32[768,128]{1,0:T(8,128)S(1)} collective-permute-done((f32[768,128]{1,0:T(8,128)S(1)}, f32[768,128]{1,0:T(8,128)S(1)}, u32[]{:S(2)}, u32[]{:S(2)}) %collective-permute-start.16) | collective-permute-done | bytes 393248 | tf_op jit(solution)/shard_map/ppermute | solution.py:330
  25.4 6.3 %collective-permute-done.4.refs_1_ = f32[1152,128]{1,0:T(8,128)S(1)} collective-permute-done((f32[1152,128]{1,0:T(8,128)S(1)}, f32[1152,128]{1,0:T(8,128)S(1)}, u32[]{:S(2)}, u32[]{:S(2)}) %collective-permute-start.4) | collective-permute-done | bytes 589856 | tf_op jit(solution)/shard_map/ppermute | solution.py:330
  33.6 1.7 %collective-permute-start.19 = (f32[432,128]{1,0:T(8,128)S(1)}, f32[432,128]{1,0:T(8,128)S(1)}, u32[]{:S(2)}, u32[]{:S(2)}) collective-permute-start(f32[432,128]{1,0:T(8,128)S(1)} %get-tuple-element.95), channel_id=1, source_target_pairs={{0,64},{1,193},{2,66},{3,195},{4,68},{5,197},{6,70},{7,199},{8,72}... | collective-permute-start | bytes 663560 | tf_op jit(solution)/shard_map/ppermute | solution.py:330
  35.3 1.9 %collective-permute-start.20 = (f32[384,128]{1,0:T(8,128)S(1)}, f32[384,128]{1,0:T(8,128)S(1)}, u32[]{:S(2)}, u32[]{:S(2)}) collective-permute-start(f32[384,128]{1,0:T(8,128)S(1)} %get-tuple-element.97), channel_id=1, source_target_pairs={{0,32},{1,35},{2,34},{3,33},{4,36},{5,39},{6,38},{7,37},{8,40},{9,... | collective-permute-start | bytes 589832 | tf_op jit(solution)/shard_map/ppermute | solution.py:330
  37.2 6.0 %collective-permute-done.20.refs_3_ = f32[384,128]{1,0:T(8,128)S(1)} collective-permute-done((f32[384,128]{1,0:T(8,128)S(1)}, f32[384,128]{1,0:T(8,128)S(1)}, u32[]{:S(2)}, u32[]{:S(2)}) %collective-permute-start.20) | collective-permute-done | bytes 196640 | tf_op jit(solution)/shard_map/ppermute | solution.py:330
  44.8 1.8 %collective-permute-start.8 = (f32[384,128]{1,0:T(8,128)S(1)}, f32[384,128]{1,0:T(8,128)S(1)}, u32[]{:S(2)}, u32[]{:S(2)}) collective-permute-start(f32[384,128]{1,0:T(8,128)S(1)} %get-tuple-element.73), channel_id=1, source_target_pairs={{0,64},{1,193},{2,66},{3,195},{4,68},{5,197},{6,70},{7,199},{8,72}... | collective-permute-start | bytes 589832 | tf_op jit(solution)/shard_map/ppermute | solution.py:330
  46.6 1.7 %collective-permute-start.9 = (f32[384,128]{1,0:T(8,128)S(1)}, f32[384,128]{1,0:T(8,128)S(1)}, u32[]{:S(2)}, u32[]{:S(2)}) collective-permute-start(f32[384,128]{1,0:T(8,128)S(1)} %get-tuple-element.75), channel_id=1, source_target_pairs={{0,32},{1,35},{2,34},{3,33},{4,36},{5,39},{6,38},{7,37},{8,40},{9,... | collective-permute-start | bytes 589832 | tf_op jit(solution)/shard_map/ppermute | solution.py:330
  49.0 2.3 %collective-permute-start.23 = (f32[272,128]{1,0:T(8,128)S(1)}, f32[272,128]{1,0:T(8,128)S(1)}, u32[]{:S(2)}, u32[]{:S(2)}) collective-permute-start(f32[272,128]{1,0:T(8,128)S(1)} %get-tuple-element.103), channel_id=1, source_target_pairs={{0,4},{1,5},{2,6},{3,7},{4,0},{5,1},{6,2},{7,3},{8,12},{9,13},{10,... | collective-permute-start | bytes 417800 | tf_op jit(solution)/shard_map/ppermute | solution.py:330
  53.7 1.4 %collective-permute-start.10 = (f32[256,128]{1,0:T(8,128)S(1)}, f32[256,128]{1,0:T(8,128)S(1)}, u32[]{:S(2)}, u32[]{:S(2)}) collective-permute-start(f32[256,128]{1,0:T(8,128)S(1)} %get-tuple-element.77), channel_id=1, source_target_pairs={{0,192},{1,65},{2,194},{3,67},{4,196},{5,69},{6,198},{7,71},{8,200... | collective-permute-start | bytes 393224 | tf_op jit(solution)/shard_map/ppermute | solution.py:330
  55.2 5.6 %collective-permute-start.24 = (f32[272,128]{1,0:T(8,128)S(1)}, f32[272,128]{1,0:T(8,128)S(1)}, u32[]{:S(2)}, u32[]{:S(2)}) collective-permute-start(f32[272,128]{1,0:T(8,128)S(1)} %add.40), channel_id=1, source_target_pairs={{0,28},{1,29},{2,30},{3,31},{4,8},{5,9},{6,10},{7,11},{8,4},{9,5},... | collective-permute-start | bytes 417800 | tf_op jit(solution)/shard_map/ppermute | solution.py:330
  61.5 2.0 %collective-permute-done.24 = f32[272,128]{1,0:T(8,128)S(1)} collective-permute-done((f32[272,128]{1,0:T(8,128)S(1)}, f32[272,128]{1,0:T(8,128)S(1)}, u32[]{:S(2)}, u32[]{:S(2)}) %collective-permute-start.24) | collective-permute-done | bytes 139296 | tf_op jit(solution)/shard_map/ppermute | solution.py:330
  63.6 1.4 %collective-permute-start.25 = (f32[272,128]{1,0:T(8,128)S(1)}, f32[272,128]{1,0:T(8,128)S(1)}, u32[]{:S(2)}, u32[]{:S(2)}) collective-permute-start(f32[272,128]{1,0:T(8,128)S(1)} %add.41), channel_id=1, source_target_pairs={{0,12},{1,13},{2,14},{3,15},{4,24},{5,25},{6,26},{7,27},{8,20},{9,... | collective-permute-start | bytes 417800 | tf_op jit(solution)/shard_map/ppermute | solution.py:330
  65.3 3.8 %collective-permute-start.13 = (f32[256,128]{1,0:T(8,128)S(1)}, f32[256,128]{1,0:T(8,128)S(1)}, u32[]{:S(2)}, u32[]{:S(2)}) collective-permute-start(f32[256,128]{1,0:T(8,128)S(1)} %add.38), channel_id=1, source_target_pairs={{0,28},{1,29},{2,30},{3,31},{4,8},{5,9},{6,10},{7,11},{8,4},{9,5},... | collective-permute-start | bytes 393224 | tf_op jit(solution)/shard_map/ppermute | solution.py:330
  69.5 6.9 %collective-permute-start.26 = (f32[272,128]{1,0:T(8,128)S(1)}, f32[272,128]{1,0:T(8,128)S(1)}, u32[]{:S(2)}, u32[]{:S(2)}) collective-permute-start(f32[272,128]{1,0:T(8,128)S(1)} %add.42.mine), channel_id=1, source_target_pairs={{0,1},{1,0},{2,3},{3,2},{4,5},{5,4},{6,7},{7,6},{8,9},{9,8},{10,11... | collective-permute-start | bytes 417800 | tf_op jit(solution)/shard_map/ppermute | solution.py:330
  76.4 1.9 %collective-permute-start.14 = (f32[256,128]{1,0:T(8,128)S(1)}, f32[256,128]{1,0:T(8,128)S(1)}, u32[]{:S(2)}, u32[]{:S(2)}) collective-permute-start(f32[256,128]{1,0:T(8,128)S(1)} %add.39), channel_id=1, source_target_pairs={{0,12},{1,13},{2,14},{3,15},{4,24},{5,25},{6,26},{7,27},{8,20},{9,... | collective-permute-start | bytes 393224 | tf_op jit(solution)/shard_map/ppermute | solution.py:330
  78.3 4.5 %shard_map.99 = (f32[256,256]{1,0:T(8,128)S(1)}, f32[256,256]{1,0:T(8,128)S(1)}) custom-call(s32[17]{0:T(128)S(1)} %stack.59.bits, f32[272,128]{1,0:T(8,128)S(1)} %add.42.mine, f32[272,128]{1,0:T(8,128)S(1)} %collective-permute-done.26.mate), custom_call_target="tpu_custom_call" | custom-call | flops 700000000 | bytes 1024 | tf_op jit(solution)/shard_map/pallas_call | solution.py:282
  82.8 4.1 %collective-permute-start.27 = (f32[256,128]{1,0:T(8,128)S(1)}, f32[256,128]{1,0:T(8,128)S(1)}, u32[]{:S(2)}, u32[]{:S(2)}) collective-permute-start(f32[256,128]{1,0:T(8,128)S(1)} %add.43.mine), channel_id=1, source_target_pairs={{0,1},{1,0},{2,3},{3,2},{4,5},{5,4},{6,7},{7,6},{8,9},{9,8},{10,11... | collective-permute-start | bytes 393224 | tf_op jit(solution)/shard_map/ppermute | solution.py:330
  87.9 1.2 shard_map.100
  89.1 2.9 %collective-permute-start.28 = (bf16[128,256]{1,0:T(8,128)(2,1)S(1)}, bf16[128,256]{1,0:T(8,128)(2,1)S(1)}, u32[]{:S(2)}, u32[]{:S(2)}) collective-permute-start(bf16[128,256]{1,0:T(8,128)(2,1)S(1)} %shard_map.100), channel_id=1, source_target_pairs={{0,4},{1,5},{2,6},{3,7},{4,0},{5,1},{6,2},{7,3},{8,12},{9,13},{10,... | collective-permute-start | bytes 196616 | tf_op jit(solution)/shard_map/ppermute | solution.py:330
  92.1 2.2 %collective-permute-done.28 = bf16[128,256]{1,0:T(8,128)(2,1)S(1)} collective-permute-done((bf16[128,256]{1,0:T(8,128)(2,1)S(1)}, bf16[128,256]{1,0:T(8,128)(2,1)S(1)}, u32[]{:S(2)}, u32[]{:S(2)}) %collective-permute-start.28) | collective-permute-done | bytes 65568 | tf_op jit(solution)/shard_map/ppermute | solution.py:330
  94.4 18.6 %all_to_all.5.mine = bf16[16,128,256]{2,1,0:T(8,128)(2,1)S(1)} all-to-all(bf16[16,128,256]{2,1,0:T(8,128)(2,1)S(1)} %broadcast_in_dim.2), channel_id=1, replica_groups=mesh['y'=4,'x_lo'=2,'z'=8,'x_hi'=2,'core'=2] {'y','x_lo','x_hi'}, dimensions={0} | all-to-all | bytes 2097152 | tf_op jit(solution)/shard_map/all_to_all | solution.py:410
  113.0 3.3 %collective-permute-start.29 = (bf16[16,128,256]{2,1,0:T(8,128)(2,1)S(1)}, bf16[16,128,256]{2,1,0:T(8,128)(2,1)S(1)}, u32[]{:S(2)}, u32[]{:S(2)}) collective-permute-start(bf16[16,128,256]{2,1,0:T(8,128)(2,1)S(1)} %all_to_all.5.mine), channel_id=1, source_target_pairs={{0,1},{1,0},{2,3},{3,2},{4,5},{5,4},{6,7},{7,6},{8,9},{9,8},{10,11... | collective-permute-start | bytes 3145736 | tf_op jit(solution)/shard_map/ppermute | solution.py:330
  116.3 2.4 %collective-permute-done.30.last_mate = bf16[128,256]{1,0:T(8,128)(2,1)S(1)} collective-permute-done((bf16[128,256]{1,0:T(8,128)(2,1)S(1)}, bf16[128,256]{1,0:T(8,128)(2,1)S(1)}, u32[]{:S(2)}, u32[]{:S(2)}) %collective-permute-start.30) | collective-permute-done | bytes 65568 | tf_op jit(solution)/shard_map/ppermute | solution.py:330
  118.7 2.1 %shard_map.101 = (bf16[1024,256]{1,0:T(8,128)(2,1)}, bf16[2304,256]{1,0:T(8,128)(2,1)}, bf16[256,1024]{1,0:T(8,128)(2,1)}) custom-call(s32[17]{0:T(128)S(1)} %stack.59.bits, bf16[16,128,256]{2,1,0:T(8,128)(2,1)S(1)} %all_to_all.5.mine, bf16[16,128,256]{2,1,0:T(8,128)(2,1)S(1)} %collective-permute-done.29.mate, bf16[128,256]{1,0:T(8,128)(2,1)S(1)} %get-tuple-element.109.last, ...), custom_call_target="tpu_custom_call" | custom-call | flops 700000000 | bytes 1024 | tf_op jit(solution)/shard_map/pallas_call | solution.py:282
  (66 shorter events, 14.3 us)
Async XLA Ops:
  2.4 4.9 %copy-start = (bf16[4,14,14,1024]{3,0,2,1:T(4,128)(2,1)S(1)}, bf16[4,14,14,1024]{3,0,2,1:T(4,128)(2,1)}, u32[]{:S(2)}) copy-start(bf16[4,14,14,1024]{3,0,2,1:T(4,128)(2,1)} %param.6) | copy-start | bytes 4816900
  4.0 6.0 %collective-permute-start.2 = (f32[1360,128]{1,0:T(8,128)S(1)}, f32[1360,128]{1,0:T(8,128)S(1)}, u32[]{:S(2)}, u32[]{:S(2)}) collective-permute-start(f32[1360,128]{1,0:T(8,128)S(1)} %get-tuple-element.60), channel_id=1, source_target_pairs={{0,1},{1,0},{2,3},{3,2},{4,5},{5,4},{6,7},{7,6},{8,9},{9,8},{10,11... | collective-permute-start | bytes 2088968 | tf_op jit(solution)/shard_map/ppermute | solution.py:330
  9.5 2.8 %collective-permute-start = (f32[1360,128]{1,0:T(8,128)S(1)}, f32[1360,128]{1,0:T(8,128)S(1)}, u32[]{:S(2)}, u32[]{:S(2)}) collective-permute-start(f32[1360,128]{1,0:T(8,128)S(1)} %get-tuple-element.56), channel_id=1, source_target_pairs={{0,1},{1,0},{2,3},{3,2},{4,5},{5,4},{6,7},{7,6},{8,9},{9,8},{10,11... | collective-permute-start | bytes 2088968 | tf_op jit(solution)/shard_map/ppermute | solution.py:330
  12.1 6.8 %collective-permute-start.3 = (f32[2304,128]{1,0:T(8,128)S(1)}, f32[2304,128]{1,0:T(8,128)S(1)}, u32[]{:S(2)}, u32[]{:S(2)}) collective-permute-start(f32[2304,128]{1,0:T(8,128)S(1)} %get-tuple-element.63), channel_id=1, source_target_pairs={{0,1},{1,0},{2,3},{3,2},{4,5},{5,4},{6,7},{7,6},{8,9},{9,8},{10,11... | collective-permute-start | bytes 3538952 | tf_op jit(solution)/shard_map/ppermute | solution.py:330
  14.2 4.7 %collective-permute-start.1 = (f32[2048,128]{1,0:T(8,128)S(1)}, f32[2048,128]{1,0:T(8,128)S(1)}, u32[]{:S(2)}, u32[]{:S(2)}) collective-permute-start(f32[2048,128]{1,0:T(8,128)S(1)} %get-tuple-element.59), channel_id=1, source_target_pairs={{0,1},{1,0},{2,3},{3,2},{4,5},{5,4},{6,7},{7,6},{8,9},{9,8},{10,11... | collective-permute-start | bytes 3145736 | tf_op jit(solution)/shard_map/ppermute | solution.py:330
  15.4 8.7 %collective-permute-start.15 = (f32[864,128]{1,0:T(8,128)S(1)}, f32[864,128]{1,0:T(8,128)S(1)}, u32[]{:S(2)}, u32[]{:S(2)}) collective-permute-start(f32[864,128]{1,0:T(8,128)S(1)} %get-tuple-element.87), channel_id=1, source_target_pairs={{0,32},{1,35},{2,34},{3,33},{4,36},{5,39},{6,38},{7,37},{8,40},{9,... | collective-permute-start | bytes 1327112 | tf_op jit(solution)/shard_map/ppermute | solution.py:330
  16.2 7.9 %collective-permute-start.16 = (f32[768,128]{1,0:T(8,128)S(1)}, f32[768,128]{1,0:T(8,128)S(1)}, u32[]{:S(2)}, u32[]{:S(2)}) collective-permute-start(f32[768,128]{1,0:T(8,128)S(1)} %get-tuple-element.89), channel_id=1, source_target_pairs={{0,64},{1,193},{2,66},{3,195},{4,68},{5,197},{6,70},{7,199},{8,72}... | collective-permute-start | bytes 1179656 | tf_op jit(solution)/shard_map/ppermute | solution.py:330
  19.7 12.0 %collective-permute-start.4 = (f32[1152,128]{1,0:T(8,128)S(1)}, f32[1152,128]{1,0:T(8,128)S(1)}, u32[]{:S(2)}, u32[]{:S(2)}) collective-permute-start(f32[1152,128]{1,0:T(8,128)S(1)} %get-tuple-element.65), channel_id=1, source_target_pairs={{0,32},{1,35},{2,34},{3,33},{4,36},{5,39},{6,38},{7,37},{8,40},{9,... | collective-permute-start | bytes 1769480 | tf_op jit(solution)/shard_map/ppermute | solution.py:330
  20.0 11.7 %collective-permute-start.5 = (f32[1152,128]{1,0:T(8,128)S(1)}, f32[1152,128]{1,0:T(8,128)S(1)}, u32[]{:S(2)}, u32[]{:S(2)}) collective-permute-start(f32[1152,128]{1,0:T(8,128)S(1)} %get-tuple-element.67), channel_id=1, source_target_pairs={{0,64},{1,193},{2,66},{3,195},{4,68},{5,197},{6,70},{7,199},{8,72}... | collective-permute-start | bytes 1769480 | tf_op jit(solution)/shard_map/ppermute | solution.py:330
  24.7 8.2 %collective-permute-start.17 = (f32[576,128]{1,0:T(8,128)S(1)}, f32[576,128]{1,0:T(8,128)S(1)}, u32[]{:S(2)}, u32[]{:S(2)}) collective-permute-start(f32[576,128]{1,0:T(8,128)S(1)} %get-tuple-element.91), channel_id=1, source_target_pairs={{0,34},{1,33},{2,32},{3,35},{4,38},{5,37},{6,36},{7,39},{8,42},{9,... | collective-permute-start | bytes 884744 | tf_op jit(solution)/shard_map/ppermute | solution.py:330
  24.8 7.8 %collective-permute-start.18 = (f32[512,128]{1,0:T(8,128)S(1)}, f32[512,128]{1,0:T(8,128)S(1)}, u32[]{:S(2)}, u32[]{:S(2)}) collective-permute-start(f32[512,128]{1,0:T(8,128)S(1)} %get-tuple-element.93), channel_id=1, source_target_pairs={{0,192},{1,65},{2,194},{3,67},{4,196},{5,69},{6,198},{7,71},{8,200... | collective-permute-start | bytes 786440 | tf_op jit(solution)/shard_map/ppermute | solution.py:330
  32.4 11.7 %collective-permute-start.6 = (f32[640,128]{1,0:T(8,128)S(1)}, f32[640,128]{1,0:T(8,128)S(1)}, u32[]{:S(2)}, u32[]{:S(2)}) collective-permute-start(f32[640,128]{1,0:T(8,128)S(1)} %get-tuple-element.69), channel_id=1, source_target_pairs={{0,34},{1,33},{2,32},{3,35},{4,38},{5,37},{6,36},{7,39},{8,42},{9,... | collective-permute-start | bytes 983048 | tf_op jit(solution)/shard_map/ppermute | solution.py:330
  32.5 11.6 %collective-permute-start.7 = (f32[640,128]{1,0:T(8,128)S(1)}, f32[640,128]{1,0:T(8,128)S(1)}, u32[]{:S(2)}, u32[]{:S(2)}) collective-permute-start(f32[640,128]{1,0:T(8,128)S(1)} %get-tuple-element.71), channel_id=1, source_target_pairs={{0,192},{1,65},{2,194},{3,67},{4,196},{5,69},{6,198},{7,71},{8,200... | collective-permute-start | bytes 983048 | tf_op jit(solution)/shard_map/ppermute | solution.py:330
  33.6 9.6 %collective-permute-start.19 = (f32[432,128]{1,0:T(8,128)S(1)}, f32[432,128]{1,0:T(8,128)S(1)}, u32[]{:S(2)}, u32[]{:S(2)}) collective-permute-start(f32[432,128]{1,0:T(8,128)S(1)} %get-tuple-element.95), channel_id=1, source_target_pairs={{0,64},{1,193},{2,66},{3,195},{4,68},{5,197},{6,70},{7,199},{8,72}... | collective-permute-start | bytes 663560 | tf_op jit(solution)/shard_map/ppermute | solution.py:330
  35.3 7.9 %collective-permute-start.20 = (f32[384,128]{1,0:T(8,128)S(1)}, f32[384,128]{1,0:T(8,128)S(1)}, u32[]{:S(2)}, u32[]{:S(2)}) collective-permute-start(f32[384,128]{1,0:T(8,128)S(1)} %get-tuple-element.97), channel_id=1, source_target_pairs={{0,32},{1,35},{2,34},{3,33},{4,36},{5,39},{6,38},{7,37},{8,40},{9,... | collective-permute-start | bytes 589832 | tf_op jit(solution)/shard_map/ppermute | solution.py:330
  43.8 4.4 %collective-permute-start.22 = (f32[320,128]{1,0:T(8,128)S(1)}, f32[320,128]{1,0:T(8,128)S(1)}, u32[]{:S(2)}, u32[]{:S(2)}) collective-permute-start(f32[320,128]{1,0:T(8,128)S(1)} %get-tuple-element.101), channel_id=1, source_target_pairs={{0,34},{1,33},{2,32},{3,35},{4,38},{5,37},{6,36},{7,39},{8,42},{9,... | collective-permute-start | bytes 491528 | tf_op jit(solution)/shard_map/ppermute | solution.py:330
  43.9 4.5 %collective-permute-start.21 = (f32[360,128]{1,0:T(8,128)S(1)}, f32[360,128]{1,0:T(8,128)S(1)}, u32[]{:S(2)}, u32[]{:S(2)}) collective-permute-start(f32[360,128]{1,0:T(8,128)S(1)} %get-tuple-element.99), channel_id=1, source_target_pairs={{0,192},{1,65},{2,194},{3,67},{4,196},{5,69},{6,198},{7,71},{8,200... | collective-permute-start | bytes 552968 | tf_op jit(solution)/shard_map/ppermute | solution.py:330
  44.8 7.3 %collective-permute-start.8 = (f32[384,128]{1,0:T(8,128)S(1)}, f32[384,128]{1,0:T(8,128)S(1)}, u32[]{:S(2)}, u32[]{:S(2)}) collective-permute-start(f32[384,128]{1,0:T(8,128)S(1)} %get-tuple-element.73), channel_id=1, source_target_pairs={{0,64},{1,193},{2,66},{3,195},{4,68},{5,197},{6,70},{7,199},{8,72}... | collective-permute-start | bytes 589832 | tf_op jit(solution)/shard_map/ppermute | solution.py:330
  46.6 6.5 %collective-permute-start.9 = (f32[384,128]{1,0:T(8,128)S(1)}, f32[384,128]{1,0:T(8,128)S(1)}, u32[]{:S(2)}, u32[]{:S(2)}) collective-permute-start(f32[384,128]{1,0:T(8,128)S(1)} %get-tuple-element.75), channel_id=1, source_target_pairs={{0,32},{1,35},{2,34},{3,33},{4,36},{5,39},{6,38},{7,37},{8,40},{9,... | collective-permute-start | bytes 589832 | tf_op jit(solution)/shard_map/ppermute | solution.py:330
  49.0 6.2 %collective-permute-start.23 = (f32[272,128]{1,0:T(8,128)S(1)}, f32[272,128]{1,0:T(8,128)S(1)}, u32[]{:S(2)}, u32[]{:S(2)}) collective-permute-start(f32[272,128]{1,0:T(8,128)S(1)} %get-tuple-element.103), channel_id=1, source_target_pairs={{0,4},{1,5},{2,6},{3,7},{4,0},{5,1},{6,2},{7,3},{8,12},{9,13},{10,... | collective-permute-start | bytes 417800 | tf_op jit(solution)/shard_map/ppermute | solution.py:330
  53.7 7.1 %collective-permute-start.10 = (f32[256,128]{1,0:T(8,128)S(1)}, f32[256,128]{1,0:T(8,128)S(1)}, u32[]{:S(2)}, u32[]{:S(2)}) collective-permute-start(f32[256,128]{1,0:T(8,128)S(1)} %get-tuple-element.77), channel_id=1, source_target_pairs={{0,192},{1,65},{2,194},{3,67},{4,196},{5,69},{6,198},{7,71},{8,200... | collective-permute-start | bytes 393224 | tf_op jit(solution)/shard_map/ppermute | solution.py:330
  55.1 5.7 %collective-permute-start.11 = (f32[256,128]{1,0:T(8,128)S(1)}, f32[256,128]{1,0:T(8,128)S(1)}, u32[]{:S(2)}, u32[]{:S(2)}) collective-permute-start(f32[256,128]{1,0:T(8,128)S(1)} %get-tuple-element.79), channel_id=1, source_target_pairs={{0,34},{1,33},{2,32},{3,35},{4,38},{5,37},{6,36},{7,39},{8,42},{9,... | collective-permute-start | bytes 393224 | tf_op jit(solution)/shard_map/ppermute | solution.py:330
  55.2 8.4 %collective-permute-start.24 = (f32[272,128]{1,0:T(8,128)S(1)}, f32[272,128]{1,0:T(8,128)S(1)}, u32[]{:S(2)}, u32[]{:S(2)}) collective-permute-start(f32[272,128]{1,0:T(8,128)S(1)} %add.40), channel_id=1, source_target_pairs={{0,28},{1,29},{2,30},{3,31},{4,8},{5,9},{6,10},{7,11},{8,4},{9,5},... | collective-permute-start | bytes 417800 | tf_op jit(solution)/shard_map/ppermute | solution.py:330
  61.4 3.9 %collective-permute-start.12 = (f32[256,128]{1,0:T(8,128)S(1)}, f32[256,128]{1,0:T(8,128)S(1)}, u32[]{:S(2)}, u32[]{:S(2)}) collective-permute-start(f32[256,128]{1,0:T(8,128)S(1)} %get-tuple-element.81), channel_id=1, source_target_pairs={{0,4},{1,5},{2,6},{3,7},{4,0},{5,1},{6,2},{7,3},{8,12},{9,13},{10,... | collective-permute-start | bytes 393224 | tf_op jit(solution)/shard_map/ppermute | solution.py:330
  63.6 5.9 %collective-permute-start.25 = (f32[272,128]{1,0:T(8,128)S(1)}, f32[272,128]{1,0:T(8,128)S(1)}, u32[]{:S(2)}, u32[]{:S(2)}) collective-permute-start(f32[272,128]{1,0:T(8,128)S(1)} %add.41), channel_id=1, source_target_pairs={{0,12},{1,13},{2,14},{3,15},{4,24},{5,25},{6,26},{7,27},{8,20},{9,... | collective-permute-start | bytes 417800 | tf_op jit(solution)/shard_map/ppermute | solution.py:330
  65.3 11.1 %collective-permute-start.13 = (f32[256,128]{1,0:T(8,128)S(1)}, f32[256,128]{1,0:T(8,128)S(1)}, u32[]{:S(2)}, u32[]{:S(2)}) collective-permute-start(f32[256,128]{1,0:T(8,128)S(1)} %add.38), channel_id=1, source_target_pairs={{0,28},{1,29},{2,30},{3,31},{4,8},{5,9},{6,10},{7,11},{8,4},{9,5},... | collective-permute-start | bytes 393224 | tf_op jit(solution)/shard_map/ppermute | solution.py:330
  69.5 8.9 %collective-permute-start.26 = (f32[272,128]{1,0:T(8,128)S(1)}, f32[272,128]{1,0:T(8,128)S(1)}, u32[]{:S(2)}, u32[]{:S(2)}) collective-permute-start(f32[272,128]{1,0:T(8,128)S(1)} %add.42.mine), channel_id=1, source_target_pairs={{0,1},{1,0},{2,3},{3,2},{4,5},{5,4},{6,7},{7,6},{8,9},{9,8},{10,11... | collective-permute-start | bytes 417800 | tf_op jit(solution)/shard_map/ppermute | solution.py:330
  76.4 6.4 %collective-permute-start.14 = (f32[256,128]{1,0:T(8,128)S(1)}, f32[256,128]{1,0:T(8,128)S(1)}, u32[]{:S(2)}, u32[]{:S(2)}) collective-permute-start(f32[256,128]{1,0:T(8,128)S(1)} %add.39), channel_id=1, source_target_pairs={{0,12},{1,13},{2,14},{3,15},{4,24},{5,25},{6,26},{7,27},{8,20},{9,... | collective-permute-start | bytes 393224 | tf_op jit(solution)/shard_map/ppermute | solution.py:330
  82.8 5.1 %collective-permute-start.27 = (f32[256,128]{1,0:T(8,128)S(1)}, f32[256,128]{1,0:T(8,128)S(1)}, u32[]{:S(2)}, u32[]{:S(2)}) collective-permute-start(f32[256,128]{1,0:T(8,128)S(1)} %add.43.mine), channel_id=1, source_target_pairs={{0,1},{1,0},{2,3},{3,2},{4,5},{5,4},{6,7},{7,6},{8,9},{9,8},{10,11... | collective-permute-start | bytes 393224 | tf_op jit(solution)/shard_map/ppermute | solution.py:330
  89.1 5.1 %collective-permute-start.28 = (bf16[128,256]{1,0:T(8,128)(2,1)S(1)}, bf16[128,256]{1,0:T(8,128)(2,1)S(1)}, u32[]{:S(2)}, u32[]{:S(2)}) collective-permute-start(bf16[128,256]{1,0:T(8,128)(2,1)S(1)} %shard_map.100), channel_id=1, source_target_pairs={{0,4},{1,5},{2,6},{3,7},{4,0},{5,1},{6,2},{7,3},{8,12},{9,13},{10,... | collective-permute-start | bytes 196616 | tf_op jit(solution)/shard_map/ppermute | solution.py:330
  113.0 5.7 %collective-permute-start.29 = (bf16[16,128,256]{2,1,0:T(8,128)(2,1)S(1)}, bf16[16,128,256]{2,1,0:T(8,128)(2,1)S(1)}, u32[]{:S(2)}, u32[]{:S(2)}) collective-permute-start(bf16[16,128,256]{2,1,0:T(8,128)(2,1)S(1)} %all_to_all.5.mine), channel_id=1, source_target_pairs={{0,1},{1,0},{2,3},{3,2},{4,5},{5,4},{6,7},{7,6},{8,9},{9,8},{10,11... | collective-permute-start | bytes 3145736 | tf_op jit(solution)/shard_map/ppermute | solution.py:330
  116.3 2.4 %collective-permute-start.30 = (bf16[128,256]{1,0:T(8,128)(2,1)S(1)}, bf16[128,256]{1,0:T(8,128)(2,1)S(1)}, u32[]{:S(2)}, u32[]{:S(2)}) collective-permute-start(bf16[128,256]{1,0:T(8,128)(2,1)S(1)} %get-tuple-element.109.last), channel_id=1, source_target_pairs={{0,1},{1,0},{2,3},{3,2},{4,5},{5,4},{6,7},{7,6},{8,9},{9,8},{10,11... | collective-permute-start | bytes 196616 | tf_op jit(solution)/shard_map/ppermute | solution.py:330
  (3 other events, 14.8 us)

commit v4 on v3

--- a/solution.py
+++ b/solution.py
@@ -149,20 +149,16 @@
             send[(8 + i) * n : (9 + i) * n, :] = value
 
 
-def split_kernel(rec, step, bits, *refs):
-    tiles = 16 >> step
-    for s in range(SETS):
-        mine, got = refs[2 * s], refs[2 * s + 1]
-        keep, send = refs[2 * SETS + 2 * s], refs[2 * SETS + 2 * s + 1]
-        size = (tiles // 2) * rec[s]
-        bit = bits[9 + 4 * s + step]
-        here = pl.ds(pl.multiple_of(bit * size, 8), size)
-        there = pl.ds(pl.multiple_of((1 - bit) * size, 8), size)
-        keep[:size, :] = mine[here, :] + got[here, :]
-        send[:size, :] = mine[there, :] + got[there, :]
-        value = mine[2 * size :, :] + got[2 * size :, :]
-        keep[size:, :] = value
-        send[size:, :] = value
+def split_kernel(rows, s, step, bits, mine, got, keep, send):
+    size = (8 >> step) * rows
+    bit = bits[9 + 4 * s + step]
+    here = pl.ds(pl.multiple_of(bit * size, 8), size)
+    there = pl.ds(pl.multiple_of((1 - bit) * size, 8), size)
+    keep[:size, :] = mine[here, :] + got[here, :]
+    send[:size, :] = mine[there, :] + got[there, :]
+    value = mine[2 * size :, :] + got[2 * size :, :]
+    keep[size:, :] = value
+    send[size:, :] = value
 
 
 def gram_leaf_kernel(bits, mine0, got0, mine1, got1, keep, send):
@@ -372,7 +368,11 @@
             for s in range(SETS):
                 args += [held[2 * s], send_to(held[2 * s + 1], ROUTE_XY[s][step])]
             if step < 3:
-                held = call(functools.partial(split_kernel, rec, step + 1), bits, args, pairs(rec, (4 >> step) + extra))
+                outs = pairs(rec, (4 >> step) + extra)
+                held = []
+                for s in range(SETS):
+                    split = functools.partial(split_kernel, rec[s], s, step + 1)
+                    held += call(split, bits, args[2 * s : 2 * s + 2], outs[2 * s : 2 * s + 2])
         size = sum(rec) * (1 if extra == 1 else 2)
         keep, send = call(leaf, bits, args, [shape(size, HALF)] * 2)
         total = keep + send_to(send, ROUTE_Z1)

time: 121 us -> 119 us (0.983)
  waiting for transfers between devices: 25.3 us -> 21.9 us
  Pallas kernels: 21.8 us -> 25.1 us
  blocking collectives: 18.6 us -> 16.9 us
    ppermute x31, waiting for transfers between devices: 25.3 us -> 21.9 us  [send_to(): return lax.ppermute(value, AXES, way)]
    pallas_call x17 -> x23, Pallas kernels: 21.8 us -> 25.1 us  [call(): pl.pallas_call(kernel, out_shape=tuple(outs) if many else outs[0], in_spe...]
    all_to_all x1, blocking collectives: 18.6 us -> 16.9 us  [on_device(): tiles = lax.all_to_all(tiles, ('y', 'x_lo', 'x_hi'), 0, 0)]
  transfers between devices with their start and end apart: 31 -> 31, of which waited for: 13 -> 13; matrix products, arithmetic and copies ran while one was open for 0% -> 0% of each run, Pallas kernels for 14% -> 17%
where the time goes in v4:
time: 119 us
  starting transfers between devices  52.1 us (44%)
  Pallas kernels  25.1 us (21%)
  waiting for transfers between devices  21.9 us (18%)
  blocking collectives  16.9 us (14%)
  other arithmetic  1.77 us (1%)
    ppermute x31, starting transfers between devices, send_to(): return lax.ppermute(value, AXES, way)  52.1 us
    pallas_call x23, Pallas kernels, call(): pl.pallas_call(kernel, out_shape=tuple(outs) if many else outs[0], in_spe...  25.1 us
    ppermute x31, waiting for transfers between devices, send_to(): return lax.ppermute(value, AXES, way)  21.9 us
    all_to_all x1, blocking collectives, on_device(): tiles = lax.all_to_all(tiles, ('y', 'x_lo', 'x_hi'), 0, 0)  16.9 us
  transfers between devices with their start and end apart: 31, of which 13 were waited for; matrix products, arithmetic and copies ran while one was open for 0% of the time, Pallas kernels for 17%

profile of v4, /device:TPU:1, one launch (start us, length us, event | category | flops | bytes accessed | tf_op | source)
XLA Modules:
  0.0 119.0 jit_solution(1007448050843899545)
XLA Ops:
  0.7 1.6 %pad_maximum_fusion.both = bf16[28,14,4,256]{3,2,1,0:T(4,128)(2,1)S(1)} fusion(bf16[14,14,4,256]{3,2,1,0:T(4,128)(2,1)} %bitcast.27, bf16[14,14,4,256]{3,2,1,0:T(4,128)(2,1)} %bitcast.28), kind=kLoop, calls=%fused_computation | loop fusion | flops 401408 | bytes 1605632 | tf_op jit(solution)/shard_map/concatenate | solution.py:348
  2.5 1.6 %shard_map.87 = (f32[1360,128]{1,0:T(8,128)S(1)}, f32[1360,128]{1,0:T(8,128)S(1)}) custom-call(s32[17]{0:T(128)S(1)} %stack.59.bits, bf16[28,14,4,256]{3,2,1,0:T(4,128)(2,1)S(1)} %pad_maximum_fusion.both), custom_call_target="tpu_custom_call" | custom-call | flops 1179648000 | bytes 2195456 | tf_op jit(solution)/shard_map/pallas_call | solution.py:278
  4.0 3.3 %collective-permute-start.2 = (f32[1360,128]{1,0:T(8,128)S(1)}, f32[1360,128]{1,0:T(8,128)S(1)}, u32[]{:S(2)}, u32[]{:S(2)}) collective-permute-start(f32[1360,128]{1,0:T(8,128)S(1)} %get-tuple-element.60), channel_id=1, source_target_pairs={{0,1},{1,0},{2,3},{3,2},{4,5},{5,4},{6,7},{7,6},{8,9},{9,8},{10,11... | collective-permute-start | bytes 2088968 | tf_op jit(solution)/shard_map/ppermute | solution.py:326
  7.4 2.2 %shard_map.85 = (f32[1360,128]{1,0:T(8,128)S(1)}, f32[1360,128]{1,0:T(8,128)S(1)}) custom-call(s32[17]{0:T(128)S(1)} %stack.59.bits, bf16[14,14,4,1024]{3,2,1,0:T(4,128)(2,1)S(1)} %bitcast.19, bf16[14,14,4,256]{3,2,1,0:T(4,128)(2,1)S(1)} %bitcast.23, bf16[14,14,4,256]{3,2,1,0:T(4,128)(2,1)S(1)} %bitcast.25, bf16[14,14,4,1024]{3,2,1,0:T(4,128)(2,1)S(1)} %bitcast.21), custom_call_target="tpu_custom_call" | custom-call | flops 1179648000 | bytes 5406720 | tf_op jit(solution)/shard_map/pallas_call | solution.py:278
  10.0 2.1 %shard_map.88 = (f32[2304,128]{1,0:T(8,128)S(1)}, f32[2304,128]{1,0:T(8,128)S(1)}) custom-call(s32[17]{0:T(128)S(1)} %stack.59.bits, bf16[28,14,4,256]{3,2,1,0:T(4,128)(2,1)S(1)} %pad_maximum_fusion.both), custom_call_target="tpu_custom_call" | custom-call | flops 1061683200 | bytes 3162112 | tf_op jit(solution)/shard_map/pallas_call | solution.py:278
  12.3 1.9 %shard_map.86 = (f32[2048,128]{1,0:T(8,128)S(1)}, f32[2048,128]{1,0:T(8,128)S(1)}) custom-call(s32[17]{0:T(128)S(1)} %stack.59.bits, bf16[14,14,4,1024]{3,2,1,0:T(4,128)(2,1)S(1)} %bitcast.20, bf16[14,14,4,256]{3,2,1,0:T(4,128)(2,1)S(1)} %bitcast.24, bf16[14,14,4,256]{3,2,1,0:T(4,128)(2,1)S(1)} %bitcast.26, bf16[14,14,4,1024]{3,2,1,0:T(4,128)(2,1)S(1)} %bitcast.22), custom_call_target="tpu_custom_call" | custom-call | flops 943718400 | bytes 6111232 | tf_op jit(solution)/shard_map/pallas_call | solution.py:278
  16.4 2.5 %collective-permute-start.15 = (f32[864,128]{1,0:T(8,128)S(1)}, f32[864,128]{1,0:T(8,128)S(1)}, u32[]{:S(2)}, u32[]{:S(2)}) collective-permute-start(f32[864,128]{1,0:T(8,128)S(1)} %get-tuple-element.87), channel_id=1, source_target_pairs={{0,32},{1,35},{2,34},{3,33},{4,36},{5,39},{6,38},{7,37},{8,40},{9,... | collective-permute-start | bytes 1327112 | tf_op jit(solution)/shard_map/ppermute | solution.py:326
  20.0 1.7 %collective-permute-start.8 = (f32[1152,128]{1,0:T(8,128)S(1)}, f32[1152,128]{1,0:T(8,128)S(1)}, u32[]{:S(2)}, u32[]{:S(2)}) collective-permute-start(f32[1152,128]{1,0:T(8,128)S(1)} %get-tuple-element.73), channel_id=1, source_target_pairs={{0,64},{1,193},{2,66},{3,195},{4,68},{5,197},{6,70},{7,199},{8,72}... | collective-permute-start | bytes 1769480 | tf_op jit(solution)/shard_map/ppermute | solution.py:326
  21.7 1.6 %collective-permute-done.19.got = f32[768,128]{1,0:T(8,128)S(1)} collective-permute-done((f32[768,128]{1,0:T(8,128)S(1)}, f32[768,128]{1,0:T(8,128)S(1)}, u32[]{:S(2)}, u32[]{:S(2)}) %collective-permute-start.19) | collective-permute-done | bytes 393248 | tf_op jit(solution)/shard_map/ppermute | solution.py:326
  25.8 6.3 %collective-permute-done.20.got = f32[512,128]{1,0:T(8,128)S(1)} collective-permute-done((f32[512,128]{1,0:T(8,128)S(1)}, f32[512,128]{1,0:T(8,128)S(1)}, u32[]{:S(2)}, u32[]{:S(2)}) %collective-permute-start.20) | collective-permute-done | bytes 262176 | tf_op jit(solution)/shard_map/ppermute | solution.py:326
  32.7 1.3 %collective-permute-start.21 = (f32[384,128]{1,0:T(8,128)S(1)}, f32[384,128]{1,0:T(8,128)S(1)}, u32[]{:S(2)}, u32[]{:S(2)}) collective-permute-start(f32[384,128]{1,0:T(8,128)S(1)} %get-tuple-element.99), channel_id=1, source_target_pairs={{0,32},{1,35},{2,34},{3,33},{4,36},{5,39},{6,38},{7,37},{8,40},{9,... | collective-permute-start | bytes 589832 | tf_op jit(solution)/shard_map/ppermute | solution.py:326
  34.6 2.5 %collective-permute-start.17 = (f32[432,128]{1,0:T(8,128)S(1)}, f32[432,128]{1,0:T(8,128)S(1)}, u32[]{:S(2)}, u32[]{:S(2)}) collective-permute-start(f32[432,128]{1,0:T(8,128)S(1)} %get-tuple-element.91), channel_id=1, source_target_pairs={{0,64},{1,193},{2,66},{3,195},{4,68},{5,197},{6,70},{7,199},{8,72}... | collective-permute-start | bytes 663560 | tf_op jit(solution)/shard_map/ppermute | solution.py:326
  39.3 1.4 %collective-permute-start.22 = (f32[320,128]{1,0:T(8,128)S(1)}, f32[320,128]{1,0:T(8,128)S(1)}, u32[]{:S(2)}, u32[]{:S(2)}) collective-permute-start(f32[320,128]{1,0:T(8,128)S(1)} %get-tuple-element.101), channel_id=1, source_target_pairs={{0,34},{1,33},{2,32},{3,35},{4,38},{5,37},{6,36},{7,39},{8,42},{9,... | collective-permute-start | bytes 491528 | tf_op jit(solution)/shard_map/ppermute | solution.py:326
  41.5 1.2 %collective-permute-start.18 = (f32[360,128]{1,0:T(8,128)S(1)}, f32[360,128]{1,0:T(8,128)S(1)}, u32[]{:S(2)}, u32[]{:S(2)}) collective-permute-start(f32[360,128]{1,0:T(8,128)S(1)} %get-tuple-element.93), channel_id=1, source_target_pairs={{0,192},{1,65},{2,194},{3,67},{4,196},{5,69},{6,198},{7,71},{8,200... | collective-permute-start | bytes 552968 | tf_op jit(solution)/shard_map/ppermute | solution.py:326
  42.8 1.3 %collective-permute-done.5.got = f32[640,128]{1,0:T(8,128)S(1)} collective-permute-done((f32[640,128]{1,0:T(8,128)S(1)}, f32[640,128]{1,0:T(8,128)S(1)}, u32[]{:S(2)}, u32[]{:S(2)}) %collective-permute-start.5) | collective-permute-done | bytes 327712 | tf_op jit(solution)/shard_map/ppermute | solution.py:326
  46.1 1.8 %collective-permute-start.10 = (f32[384,128]{1,0:T(8,128)S(1)}, f32[384,128]{1,0:T(8,128)S(1)}, u32[]{:S(2)}, u32[]{:S(2)}) collective-permute-start(f32[384,128]{1,0:T(8,128)S(1)} %get-tuple-element.77), channel_id=1, source_target_pairs={{0,32},{1,35},{2,34},{3,33},{4,36},{5,39},{6,38},{7,37},{8,40},{9,... | collective-permute-start | bytes 589832 | tf_op jit(solution)/shard_map/ppermute | solution.py:326
  48.4 1.7 %collective-permute-start.23 = (f32[272,128]{1,0:T(8,128)S(1)}, f32[272,128]{1,0:T(8,128)S(1)}, u32[]{:S(2)}, u32[]{:S(2)}) collective-permute-start(f32[272,128]{1,0:T(8,128)S(1)} %get-tuple-element.103), channel_id=1, source_target_pairs={{0,4},{1,5},{2,6},{3,7},{4,0},{5,1},{6,2},{7,3},{8,12},{9,13},{10,... | collective-permute-start | bytes 417800 | tf_op jit(solution)/shard_map/ppermute | solution.py:326
  50.2 1.6 %collective-permute-done.6.got = f32[384,128]{1,0:T(8,128)S(1)} collective-permute-done((f32[384,128]{1,0:T(8,128)S(1)}, f32[384,128]{1,0:T(8,128)S(1)}, u32[]{:S(2)}, u32[]{:S(2)}) %collective-permute-start.6) | collective-permute-done | bytes 196640 | tf_op jit(solution)/shard_map/ppermute | solution.py:326
  53.2 5.5 %collective-permute-start.24 = (f32[272,128]{1,0:T(8,128)S(1)}, f32[272,128]{1,0:T(8,128)S(1)}, u32[]{:S(2)}, u32[]{:S(2)}) collective-permute-start(f32[272,128]{1,0:T(8,128)S(1)} %add.40), channel_id=1, source_target_pairs={{0,28},{1,29},{2,30},{3,31},{4,8},{5,9},{6,10},{7,11},{8,4},{9,5},... | collective-permute-start | bytes 417800 | tf_op jit(solution)/shard_map/ppermute | solution.py:326
  59.4 1.8 %collective-permute-done.24 = f32[272,128]{1,0:T(8,128)S(1)} collective-permute-done((f32[272,128]{1,0:T(8,128)S(1)}, f32[272,128]{1,0:T(8,128)S(1)}, u32[]{:S(2)}, u32[]{:S(2)}) %collective-permute-start.24) | collective-permute-done | bytes 139296 | tf_op jit(solution)/shard_map/ppermute | solution.py:326
  61.2 1.9 %collective-permute-start.25 = (f32[272,128]{1,0:T(8,128)S(1)}, f32[272,128]{1,0:T(8,128)S(1)}, u32[]{:S(2)}, u32[]{:S(2)}) collective-permute-start(f32[272,128]{1,0:T(8,128)S(1)} %add.41), channel_id=1, source_target_pairs={{0,12},{1,13},{2,14},{3,15},{4,24},{5,25},{6,26},{7,27},{8,20},{9,... | collective-permute-start | bytes 417800 | tf_op jit(solution)/shard_map/ppermute | solution.py:326
  63.5 3.8 %collective-permute-start.13 = (f32[256,128]{1,0:T(8,128)S(1)}, f32[256,128]{1,0:T(8,128)S(1)}, u32[]{:S(2)}, u32[]{:S(2)}) collective-permute-start(f32[256,128]{1,0:T(8,128)S(1)} %add.38), channel_id=1, source_target_pairs={{0,28},{1,29},{2,30},{3,31},{4,8},{5,9},{6,10},{7,11},{8,4},{9,5},... | collective-permute-start | bytes 393224 | tf_op jit(solution)/shard_map/ppermute | solution.py:326
  67.3 11.1 %collective-permute-start.26 = (f32[272,128]{1,0:T(8,128)S(1)}, f32[272,128]{1,0:T(8,128)S(1)}, u32[]{:S(2)}, u32[]{:S(2)}) collective-permute-start(f32[272,128]{1,0:T(8,128)S(1)} %add.42.mine), channel_id=1, source_target_pairs={{0,1},{1,0},{2,3},{3,2},{4,5},{5,4},{6,7},{7,6},{8,9},{9,8},{10,11... | collective-permute-start | bytes 417800 | tf_op jit(solution)/shard_map/ppermute | solution.py:326
  78.4 1.9 %collective-permute-start.14 = (f32[256,128]{1,0:T(8,128)S(1)}, f32[256,128]{1,0:T(8,128)S(1)}, u32[]{:S(2)}, u32[]{:S(2)}) collective-permute-start(f32[256,128]{1,0:T(8,128)S(1)} %add.39), channel_id=1, source_target_pairs={{0,12},{1,13},{2,14},{3,15},{4,24},{5,25},{6,26},{7,27},{8,20},{9,... | collective-permute-start | bytes 393224 | tf_op jit(solution)/shard_map/ppermute | solution.py:326
  80.3 4.5 %shard_map.105 = (f32[256,256]{1,0:T(8,128)S(1)}, f32[256,256]{1,0:T(8,128)S(1)}) custom-call(s32[17]{0:T(128)S(1)} %stack.59.bits, f32[272,128]{1,0:T(8,128)S(1)} %add.42.mine, f32[272,128]{1,0:T(8,128)S(1)} %collective-permute-done.26.mate), custom_call_target="tpu_custom_call" | custom-call | flops 700000000 | bytes 1024 | tf_op jit(solution)/shard_map/pallas_call | solution.py:278
  84.8 2.3 %collective-permute-done.14 = f32[256,128]{1,0:T(8,128)S(1)} collective-permute-done((f32[256,128]{1,0:T(8,128)S(1)}, f32[256,128]{1,0:T(8,128)S(1)}, u32[]{:S(2)}, u32[]{:S(2)}) %collective-permute-start.14) | collective-permute-done | bytes 131104 | tf_op jit(solution)/shard_map/ppermute | solution.py:326
  87.1 1.2 %collective-permute-start.27 = (f32[256,128]{1,0:T(8,128)S(1)}, f32[256,128]{1,0:T(8,128)S(1)}, u32[]{:S(2)}, u32[]{:S(2)}) collective-permute-start(f32[256,128]{1,0:T(8,128)S(1)} %add.43.mine), channel_id=1, source_target_pairs={{0,1},{1,0},{2,3},{3,2},{4,5},{5,4},{6,7},{7,6},{8,9},{9,8},{10,11... | collective-permute-start | bytes 393224 | tf_op jit(solution)/shard_map/ppermute | solution.py:326
  91.7 2.0 %collective-permute-done.28 = bf16[128,256]{1,0:T(8,128)(2,1)S(1)} collective-permute-done((bf16[128,256]{1,0:T(8,128)(2,1)S(1)}, bf16[128,256]{1,0:T(8,128)(2,1)S(1)}, u32[]{:S(2)}, u32[]{:S(2)}) %collective-permute-start.28) | collective-permute-done | bytes 65568 | tf_op jit(solution)/shard_map/ppermute | solution.py:326
  93.9 16.9 %all_to_all.5.mine = bf16[16,128,256]{2,1,0:T(8,128)(2,1)S(1)} all-to-all(bf16[16,128,256]{2,1,0:T(8,128)(2,1)S(1)} %broadcast_in_dim.2), channel_id=1, replica_groups=mesh['y'=4,'x_lo'=2,'z'=8,'x_hi'=2,'core'=2] {'y','x_lo','x_hi'}, dimensions={0} | all-to-all | bytes 2097152 | tf_op jit(solution)/shard_map/all_to_all | solution.py:410
  110.8 3.7 %collective-permute-start.29 = (bf16[16,128,256]{2,1,0:T(8,128)(2,1)S(1)}, bf16[16,128,256]{2,1,0:T(8,128)(2,1)S(1)}, u32[]{:S(2)}, u32[]{:S(2)}) collective-permute-start(bf16[16,128,256]{2,1,0:T(8,128)(2,1)S(1)} %all_to_all.5.mine), channel_id=1, source_target_pairs={{0,1},{1,0},{2,3},{3,2},{4,5},{5,4},{6,7},{7,6},{8,9},{9,8},{10,11... | collective-permute-start | bytes 3145736 | tf_op jit(solution)/shard_map/ppermute | solution.py:326
  114.5 2.4 %collective-permute-done.30.last_mate = bf16[128,256]{1,0:T(8,128)(2,1)S(1)} collective-permute-done((bf16[128,256]{1,0:T(8,128)(2,1)S(1)}, bf16[128,256]{1,0:T(8,128)(2,1)S(1)}, u32[]{:S(2)}, u32[]{:S(2)}) %collective-permute-start.30) | collective-permute-done | bytes 65568 | tf_op jit(solution)/shard_map/ppermute | solution.py:326
  116.8 2.1 %shard_map.107 = (bf16[1024,256]{1,0:T(8,128)(2,1)}, bf16[2304,256]{1,0:T(8,128)(2,1)}, bf16[256,1024]{1,0:T(8,128)(2,1)}) custom-call(s32[17]{0:T(128)S(1)} %stack.59.bits, bf16[16,128,256]{2,1,0:T(8,128)(2,1)S(1)} %all_to_all.5.mine, bf16[16,128,256]{2,1,0:T(8,128)(2,1)S(1)} %collective-permute-done.29.mate, bf16[128,256]{1,0:T(8,128)(2,1)S(1)} %get-tuple-element.109.last, ...), custom_call_target="tpu_custom_call" | custom-call | flops 700000000 | bytes 1024 | tf_op jit(solution)/shard_map/pallas_call | solution.py:278
  (72 shorter events, 19.4 us)
Async XLA Ops:
  2.4 4.9 %copy-start = (bf16[4,14,14,1024]{3,0,2,1:T(4,128)(2,1)S(1)}, bf16[4,14,14,1024]{3,0,2,1:T(4,128)(2,1)}, u32[]{:S(2)}) copy-start(bf16[4,14,14,1024]{3,0,2,1:T(4,128)(2,1)} %param.6) | copy-start | bytes 4816900
  4.0 6.0 %collective-permute-start.2 = (f32[1360,128]{1,0:T(8,128)S(1)}, f32[1360,128]{1,0:T(8,128)S(1)}, u32[]{:S(2)}, u32[]{:S(2)}) collective-permute-start(f32[1360,128]{1,0:T(8,128)S(1)} %get-tuple-element.60), channel_id=1, source_target_pairs={{0,1},{1,0},{2,3},{3,2},{4,5},{5,4},{6,7},{7,6},{8,9},{9,8},{10,11... | collective-permute-start | bytes 2088968 | tf_op jit(solution)/shard_map/ppermute | solution.py:326
  9.5 2.8 %collective-permute-start = (f32[1360,128]{1,0:T(8,128)S(1)}, f32[1360,128]{1,0:T(8,128)S(1)}, u32[]{:S(2)}, u32[]{:S(2)}) collective-permute-start(f32[1360,128]{1,0:T(8,128)S(1)} %get-tuple-element.56), channel_id=1, source_target_pairs={{0,1},{1,0},{2,3},{3,2},{4,5},{5,4},{6,7},{7,6},{8,9},{9,8},{10,11... | collective-permute-start | bytes 2088968 | tf_op jit(solution)/shard_map/ppermute | solution.py:326
  12.1 6.8 %collective-permute-start.3 = (f32[2304,128]{1,0:T(8,128)S(1)}, f32[2304,128]{1,0:T(8,128)S(1)}, u32[]{:S(2)}, u32[]{:S(2)}) collective-permute-start(f32[2304,128]{1,0:T(8,128)S(1)} %get-tuple-element.63), channel_id=1, source_target_pairs={{0,1},{1,0},{2,3},{3,2},{4,5},{5,4},{6,7},{7,6},{8,9},{9,8},{10,11... | collective-permute-start | bytes 3538952 | tf_op jit(solution)/shard_map/ppermute | solution.py:326
  14.2 4.7 %collective-permute-start.1 = (f32[2048,128]{1,0:T(8,128)S(1)}, f32[2048,128]{1,0:T(8,128)S(1)}, u32[]{:S(2)}, u32[]{:S(2)}) collective-permute-start(f32[2048,128]{1,0:T(8,128)S(1)} %get-tuple-element.59), channel_id=1, source_target_pairs={{0,1},{1,0},{2,3},{3,2},{4,5},{5,4},{6,7},{7,6},{8,9},{9,8},{10,11... | collective-permute-start | bytes 3145736 | tf_op jit(solution)/shard_map/ppermute | solution.py:326
  15.4 7.9 %collective-permute-start.19 = (f32[768,128]{1,0:T(8,128)S(1)}, f32[768,128]{1,0:T(8,128)S(1)}, u32[]{:S(2)}, u32[]{:S(2)}) collective-permute-start(f32[768,128]{1,0:T(8,128)S(1)} %get-tuple-element.95), channel_id=1, source_target_pairs={{0,64},{1,193},{2,66},{3,195},{4,68},{5,197},{6,70},{7,199},{8,72}... | collective-permute-start | bytes 1179656 | tf_op jit(solution)/shard_map/ppermute | solution.py:326
  16.4 8.4 %collective-permute-start.15 = (f32[864,128]{1,0:T(8,128)S(1)}, f32[864,128]{1,0:T(8,128)S(1)}, u32[]{:S(2)}, u32[]{:S(2)}) collective-permute-start(f32[864,128]{1,0:T(8,128)S(1)} %get-tuple-element.87), channel_id=1, source_target_pairs={{0,32},{1,35},{2,34},{3,33},{4,36},{5,39},{6,38},{7,37},{8,40},{9,... | collective-permute-start | bytes 1327112 | tf_op jit(solution)/shard_map/ppermute | solution.py:326
  19.7 17.4 %collective-permute-start.4 = (f32[1152,128]{1,0:T(8,128)S(1)}, f32[1152,128]{1,0:T(8,128)S(1)}, u32[]{:S(2)}, u32[]{:S(2)}) collective-permute-start(f32[1152,128]{1,0:T(8,128)S(1)} %get-tuple-element.65), channel_id=1, source_target_pairs={{0,32},{1,35},{2,34},{3,33},{4,36},{5,39},{6,38},{7,37},{8,40},{9,... | collective-permute-start | bytes 1769480 | tf_op jit(solution)/shard_map/ppermute | solution.py:326
  20.0 17.8 %collective-permute-start.8 = (f32[1152,128]{1,0:T(8,128)S(1)}, f32[1152,128]{1,0:T(8,128)S(1)}, u32[]{:S(2)}, u32[]{:S(2)}) collective-permute-start(f32[1152,128]{1,0:T(8,128)S(1)} %get-tuple-element.73), channel_id=1, source_target_pairs={{0,64},{1,193},{2,66},{3,195},{4,68},{5,197},{6,70},{7,199},{8,72}... | collective-permute-start | bytes 1769480 | tf_op jit(solution)/shard_map/ppermute | solution.py:326
  23.9 8.2 %collective-permute-start.20 = (f32[512,128]{1,0:T(8,128)S(1)}, f32[512,128]{1,0:T(8,128)S(1)}, u32[]{:S(2)}, u32[]{:S(2)}) collective-permute-start(f32[512,128]{1,0:T(8,128)S(1)} %get-tuple-element.97), channel_id=1, source_target_pairs={{0,192},{1,65},{2,194},{3,67},{4,196},{5,69},{6,198},{7,71},{8,200... | collective-permute-start | bytes 786440 | tf_op jit(solution)/shard_map/ppermute | solution.py:326
  25.4 8.6 %collective-permute-start.16 = (f32[576,128]{1,0:T(8,128)S(1)}, f32[576,128]{1,0:T(8,128)S(1)}, u32[]{:S(2)}, u32[]{:S(2)}) collective-permute-start(f32[576,128]{1,0:T(8,128)S(1)} %get-tuple-element.89), channel_id=1, source_target_pairs={{0,34},{1,33},{2,32},{3,35},{4,38},{5,37},{6,36},{7,39},{8,42},{9,... | collective-permute-start | bytes 884744 | tf_op jit(solution)/shard_map/ppermute | solution.py:326
  32.7 6.0 %collective-permute-start.21 = (f32[384,128]{1,0:T(8,128)S(1)}, f32[384,128]{1,0:T(8,128)S(1)}, u32[]{:S(2)}, u32[]{:S(2)}) collective-permute-start(f32[384,128]{1,0:T(8,128)S(1)} %get-tuple-element.99), channel_id=1, source_target_pairs={{0,32},{1,35},{2,34},{3,33},{4,36},{5,39},{6,38},{7,37},{8,40},{9,... | collective-permute-start | bytes 589832 | tf_op jit(solution)/shard_map/ppermute | solution.py:326
  34.6 6.4 %collective-permute-start.17 = (f32[432,128]{1,0:T(8,128)S(1)}, f32[432,128]{1,0:T(8,128)S(1)}, u32[]{:S(2)}, u32[]{:S(2)}) collective-permute-start(f32[432,128]{1,0:T(8,128)S(1)} %get-tuple-element.91), channel_id=1, source_target_pairs={{0,64},{1,193},{2,66},{3,195},{4,68},{5,197},{6,70},{7,199},{8,72}... | collective-permute-start | bytes 663560 | tf_op jit(solution)/shard_map/ppermute | solution.py:326
  37.7 6.3 %collective-permute-start.5 = (f32[640,128]{1,0:T(8,128)S(1)}, f32[640,128]{1,0:T(8,128)S(1)}, u32[]{:S(2)}, u32[]{:S(2)}) collective-permute-start(f32[640,128]{1,0:T(8,128)S(1)} %get-tuple-element.67), channel_id=1, source_target_pairs={{0,34},{1,33},{2,32},{3,35},{4,38},{5,37},{6,36},{7,39},{8,42},{9,... | collective-permute-start | bytes 983048 | tf_op jit(solution)/shard_map/ppermute | solution.py:326
  38.4 7.0 %collective-permute-start.9 = (f32[640,128]{1,0:T(8,128)S(1)}, f32[640,128]{1,0:T(8,128)S(1)}, u32[]{:S(2)}, u32[]{:S(2)}) collective-permute-start(f32[640,128]{1,0:T(8,128)S(1)} %get-tuple-element.75), channel_id=1, source_target_pairs={{0,192},{1,65},{2,194},{3,67},{4,196},{5,69},{6,198},{7,71},{8,200... | collective-permute-start | bytes 983048 | tf_op jit(solution)/shard_map/ppermute | solution.py:326
  39.3 8.6 %collective-permute-start.22 = (f32[320,128]{1,0:T(8,128)S(1)}, f32[320,128]{1,0:T(8,128)S(1)}, u32[]{:S(2)}, u32[]{:S(2)}) collective-permute-start(f32[320,128]{1,0:T(8,128)S(1)} %get-tuple-element.101), channel_id=1, source_target_pairs={{0,34},{1,33},{2,32},{3,35},{4,38},{5,37},{6,36},{7,39},{8,42},{9,... | collective-permute-start | bytes 491528 | tf_op jit(solution)/shard_map/ppermute | solution.py:326
  41.5 6.3 %collective-permute-start.18 = (f32[360,128]{1,0:T(8,128)S(1)}, f32[360,128]{1,0:T(8,128)S(1)}, u32[]{:S(2)}, u32[]{:S(2)}) collective-permute-start(f32[360,128]{1,0:T(8,128)S(1)} %get-tuple-element.93), channel_id=1, source_target_pairs={{0,192},{1,65},{2,194},{3,67},{4,196},{5,69},{6,198},{7,71},{8,200... | collective-permute-start | bytes 552968 | tf_op jit(solution)/shard_map/ppermute | solution.py:326
  44.6 7.2 %collective-permute-start.6 = (f32[384,128]{1,0:T(8,128)S(1)}, f32[384,128]{1,0:T(8,128)S(1)}, u32[]{:S(2)}, u32[]{:S(2)}) collective-permute-start(f32[384,128]{1,0:T(8,128)S(1)} %get-tuple-element.69), channel_id=1, source_target_pairs={{0,64},{1,193},{2,66},{3,195},{4,68},{5,197},{6,70},{7,199},{8,72}... | collective-permute-start | bytes 589832 | tf_op jit(solution)/shard_map/ppermute | solution.py:326
  46.1 6.4 %collective-permute-start.10 = (f32[384,128]{1,0:T(8,128)S(1)}, f32[384,128]{1,0:T(8,128)S(1)}, u32[]{:S(2)}, u32[]{:S(2)}) collective-permute-start(f32[384,128]{1,0:T(8,128)S(1)} %get-tuple-element.77), channel_id=1, source_target_pairs={{0,32},{1,35},{2,34},{3,33},{4,36},{5,39},{6,38},{7,37},{8,40},{9,... | collective-permute-start | bytes 589832 | tf_op jit(solution)/shard_map/ppermute | solution.py:326
  48.4 4.7 %collective-permute-start.23 = (f32[272,128]{1,0:T(8,128)S(1)}, f32[272,128]{1,0:T(8,128)S(1)}, u32[]{:S(2)}, u32[]{:S(2)}) collective-permute-start(f32[272,128]{1,0:T(8,128)S(1)} %get-tuple-element.103), channel_id=1, source_target_pairs={{0,4},{1,5},{2,6},{3,7},{4,0},{5,1},{6,2},{7,3},{8,12},{9,13},{10,... | collective-permute-start | bytes 417800 | tf_op jit(solution)/shard_map/ppermute | solution.py:326
  52.3 6.3 %collective-permute-start.7 = (f32[256,128]{1,0:T(8,128)S(1)}, f32[256,128]{1,0:T(8,128)S(1)}, u32[]{:S(2)}, u32[]{:S(2)}) collective-permute-start(f32[256,128]{1,0:T(8,128)S(1)} %get-tuple-element.71), channel_id=1, source_target_pairs={{0,192},{1,65},{2,194},{3,67},{4,196},{5,69},{6,198},{7,71},{8,200... | collective-permute-start | bytes 393224 | tf_op jit(solution)/shard_map/ppermute | solution.py:326
  53.0 5.7 %collective-permute-start.11 = (f32[256,128]{1,0:T(8,128)S(1)}, f32[256,128]{1,0:T(8,128)S(1)}, u32[]{:S(2)}, u32[]{:S(2)}) collective-permute-start(f32[256,128]{1,0:T(8,128)S(1)} %get-tuple-element.79), channel_id=1, source_target_pairs={{0,34},{1,33},{2,32},{3,35},{4,38},{5,37},{6,36},{7,39},{8,42},{9,... | collective-permute-start | bytes 393224 | tf_op jit(solution)/shard_map/ppermute | solution.py:326
  53.2 8.0 %collective-permute-start.24 = (f32[272,128]{1,0:T(8,128)S(1)}, f32[272,128]{1,0:T(8,128)S(1)}, u32[]{:S(2)}, u32[]{:S(2)}) collective-permute-start(f32[272,128]{1,0:T(8,128)S(1)} %add.40), channel_id=1, source_target_pairs={{0,28},{1,29},{2,30},{3,31},{4,8},{5,9},{6,10},{7,11},{8,4},{9,5},... | collective-permute-start | bytes 417800 | tf_op jit(solution)/shard_map/ppermute | solution.py:326
  59.3 4.2 %collective-permute-start.12 = (f32[256,128]{1,0:T(8,128)S(1)}, f32[256,128]{1,0:T(8,128)S(1)}, u32[]{:S(2)}, u32[]{:S(2)}) collective-permute-start(f32[256,128]{1,0:T(8,128)S(1)} %get-tuple-element.81), channel_id=1, source_target_pairs={{0,4},{1,5},{2,6},{3,7},{4,0},{5,1},{6,2},{7,3},{8,12},{9,13},{10,... | collective-permute-start | bytes 393224 | tf_op jit(solution)/shard_map/ppermute | solution.py:326
  61.2 6.1 %collective-permute-start.25 = (f32[272,128]{1,0:T(8,128)S(1)}, f32[272,128]{1,0:T(8,128)S(1)}, u32[]{:S(2)}, u32[]{:S(2)}) collective-permute-start(f32[272,128]{1,0:T(8,128)S(1)} %add.41), channel_id=1, source_target_pairs={{0,12},{1,13},{2,14},{3,15},{4,24},{5,25},{6,26},{7,27},{8,20},{9,... | collective-permute-start | bytes 417800 | tf_op jit(solution)/shard_map/ppermute | solution.py:326
  63.5 14.9 %collective-permute-start.13 = (f32[256,128]{1,0:T(8,128)S(1)}, f32[256,128]{1,0:T(8,128)S(1)}, u32[]{:S(2)}, u32[]{:S(2)}) collective-permute-start(f32[256,128]{1,0:T(8,128)S(1)} %add.38), channel_id=1, source_target_pairs={{0,28},{1,29},{2,30},{3,31},{4,8},{5,9},{6,10},{7,11},{8,4},{9,5},... | collective-permute-start | bytes 393224 | tf_op jit(solution)/shard_map/ppermute | solution.py:326
  67.3 13.1 %collective-permute-start.26 = (f32[272,128]{1,0:T(8,128)S(1)}, f32[272,128]{1,0:T(8,128)S(1)}, u32[]{:S(2)}, u32[]{:S(2)}) collective-permute-start(f32[272,128]{1,0:T(8,128)S(1)} %add.42.mine), channel_id=1, source_target_pairs={{0,1},{1,0},{2,3},{3,2},{4,5},{5,4},{6,7},{7,6},{8,9},{9,8},{10,11... | collective-permute-start | bytes 417800 | tf_op jit(solution)/shard_map/ppermute | solution.py:326
  78.4 8.7 %collective-permute-start.14 = (f32[256,128]{1,0:T(8,128)S(1)}, f32[256,128]{1,0:T(8,128)S(1)}, u32[]{:S(2)}, u32[]{:S(2)}) collective-permute-start(f32[256,128]{1,0:T(8,128)S(1)} %add.39), channel_id=1, source_target_pairs={{0,12},{1,13},{2,14},{3,15},{4,24},{5,25},{6,26},{7,27},{8,20},{9,... | collective-permute-start | bytes 393224 | tf_op jit(solution)/shard_map/ppermute | solution.py:326
  87.1 2.2 %collective-permute-start.27 = (f32[256,128]{1,0:T(8,128)S(1)}, f32[256,128]{1,0:T(8,128)S(1)}, u32[]{:S(2)}, u32[]{:S(2)}) collective-permute-start(f32[256,128]{1,0:T(8,128)S(1)} %add.43.mine), channel_id=1, source_target_pairs={{0,1},{1,0},{2,3},{3,2},{4,5},{5,4},{6,7},{7,6},{8,9},{9,8},{10,11... | collective-permute-start | bytes 393224 | tf_op jit(solution)/shard_map/ppermute | solution.py:326
  90.5 3.2 %collective-permute-start.28 = (bf16[128,256]{1,0:T(8,128)(2,1)S(1)}, bf16[128,256]{1,0:T(8,128)(2,1)S(1)}, u32[]{:S(2)}, u32[]{:S(2)}) collective-permute-start(bf16[128,256]{1,0:T(8,128)(2,1)S(1)} %shard_map.106), channel_id=1, source_target_pairs={{0,4},{1,5},{2,6},{3,7},{4,0},{5,1},{6,2},{7,3},{8,12},{9,13},{10,... | collective-permute-start | bytes 196616 | tf_op jit(solution)/shard_map/ppermute | solution.py:326
  110.8 6.1 %collective-permute-start.29 = (bf16[16,128,256]{2,1,0:T(8,128)(2,1)S(1)}, bf16[16,128,256]{2,1,0:T(8,128)(2,1)S(1)}, u32[]{:S(2)}, u32[]{:S(2)}) collective-permute-start(bf16[16,128,256]{2,1,0:T(8,128)(2,1)S(1)} %all_to_all.5.mine), channel_id=1, source_target_pairs={{0,1},{1,0},{2,3},{3,2},{4,5},{5,4},{6,7},{7,6},{8,9},{9,8},{10,11... | collective-permute-start | bytes 3145736 | tf_op jit(solution)/shard_map/ppermute | solution.py:326
  114.5 2.4 %collective-permute-start.30 = (bf16[128,256]{1,0:T(8,128)(2,1)S(1)}, bf16[128,256]{1,0:T(8,128)(2,1)S(1)}, u32[]{:S(2)}, u32[]{:S(2)}) collective-permute-start(bf16[128,256]{1,0:T(8,128)(2,1)S(1)} %get-tuple-element.109.last), channel_id=1, source_target_pairs={{0,1},{1,0},{2,3},{3,2},{4,5},{5,4},{6,7},{7,6},{8,9},{9,8},{10,11... | collective-permute-start | bytes 196616 | tf_op jit(solution)/shard_map/ppermute | solution.py:326
  (3 other events, 14.8 us)

commit v5 on v4

--- a/solution.py
+++ b/solution.py
@@ -282,7 +282,7 @@
         out_specs=tuple([VMEM] * len(outs)) if many else VMEM,
         scratch_shapes=list(scratch),
         compiler_params=pltpu.CompilerParams(vmem_limit_bytes=size * 5 // 4 + held + room * 2**20),
-        cost_estimate=pl.CostEstimate(flops=flops or 7 * 10**8, bytes_accessed=size if flops else 1024, transcendentals=0),
+        cost_estimate=pl.CostEstimate(flops=flops or 10**9, bytes_accessed=size if flops else 1024, transcendentals=0),
     )(bits, *args)
 
 

time: 119 us -> 119 us (level)
  no operation moved by 1% of the time
where the time goes in v5:
time: 119 us
  starting transfers between devices  52.2 us (44%)
  Pallas kernels  25.1 us (21%)
  waiting for transfers between devices  21.8 us (18%)
  blocking collectives  16.9 us (14%)
  other arithmetic  1.77 us (1%)
    ppermute x31, starting transfers between devices, send_to(): return lax.ppermute(value, AXES, way)  52.2 us
    pallas_call x23, Pallas kernels, call(): pl.pallas_call(kernel, out_shape=tuple(outs) if many else outs[0], in_spe...  25.1 us
    ppermute x31, waiting for transfers between devices, send_to(): return lax.ppermute(value, AXES, way)  21.8 us
    all_to_all x1, blocking collectives, on_device(): tiles = lax.all_to_all(tiles, ('y', 'x_lo', 'x_hi'), 0, 0)  16.9 us
  transfers between devices with their start and end apart: 31, of which 13 were waited for; matrix products, arithmetic and copies ran while one was open for 0% of the time, Pallas kernels for 17%

profile of v5, /device:TPU:1, one launch (start us, length us, event | category | flops | bytes accessed | tf_op | source)
XLA Modules:
  0.0 119.1 jit_solution(4747876737063351073)
XLA Ops:
  0.7 1.6 %pad_maximum_fusion.both = bf16[28,14,4,256]{3,2,1,0:T(4,128)(2,1)S(1)} fusion(bf16[14,14,4,256]{3,2,1,0:T(4,128)(2,1)} %bitcast.27, bf16[14,14,4,256]{3,2,1,0:T(4,128)(2,1)} %bitcast.28), kind=kLoop, calls=%fused_computation | loop fusion | flops 401408 | bytes 1605632 | tf_op jit(solution)/shard_map/concatenate | solution.py:348
  2.5 1.6 %shard_map.87 = (f32[1360,128]{1,0:T(8,128)S(1)}, f32[1360,128]{1,0:T(8,128)S(1)}) custom-call(s32[17]{0:T(128)S(1)} %stack.59.bits, bf16[28,14,4,256]{3,2,1,0:T(4,128)(2,1)S(1)} %pad_maximum_fusion.both), custom_call_target="tpu_custom_call" | custom-call | flops 1179648000 | bytes 2195456 | tf_op jit(solution)/shard_map/pallas_call | solution.py:278
  4.0 3.3 %collective-permute-start.2 = (f32[1360,128]{1,0:T(8,128)S(1)}, f32[1360,128]{1,0:T(8,128)S(1)}, u32[]{:S(2)}, u32[]{:S(2)}) collective-permute-start(f32[1360,128]{1,0:T(8,128)S(1)} %get-tuple-element.60), channel_id=1, source_target_pairs={{0,1},{1,0},{2,3},{3,2},{4,5},{5,4},{6,7},{7,6},{8,9},{9,8},{10,11... | collective-permute-start | bytes 2088968 | tf_op jit(solution)/shard_map/ppermute | solution.py:326
  7.4 2.2 %shard_map.85 = (f32[1360,128]{1,0:T(8,128)S(1)}, f32[1360,128]{1,0:T(8,128)S(1)}) custom-call(s32[17]{0:T(128)S(1)} %stack.59.bits, bf16[14,14,4,1024]{3,2,1,0:T(4,128)(2,1)S(1)} %bitcast.19, bf16[14,14,4,256]{3,2,1,0:T(4,128)(2,1)S(1)} %bitcast.23, bf16[14,14,4,256]{3,2,1,0:T(4,128)(2,1)S(1)} %bitcast.25, bf16[14,14,4,1024]{3,2,1,0:T(4,128)(2,1)S(1)} %bitcast.21), custom_call_target="tpu_custom_call" | custom-call | flops 1179648000 | bytes 5406720 | tf_op jit(solution)/shard_map/pallas_call | solution.py:278
  10.0 2.1 %shard_map.88 = (f32[2304,128]{1,0:T(8,128)S(1)}, f32[2304,128]{1,0:T(8,128)S(1)}) custom-call(s32[17]{0:T(128)S(1)} %stack.59.bits, bf16[28,14,4,256]{3,2,1,0:T(4,128)(2,1)S(1)} %pad_maximum_fusion.both), custom_call_target="tpu_custom_call" | custom-call | flops 1061683200 | bytes 3162112 | tf_op jit(solution)/shard_map/pallas_call | solution.py:278
  12.3 1.9 %shard_map.86 = (f32[2048,128]{1,0:T(8,128)S(1)}, f32[2048,128]{1,0:T(8,128)S(1)}) custom-call(s32[17]{0:T(128)S(1)} %stack.59.bits, bf16[14,14,4,1024]{3,2,1,0:T(4,128)(2,1)S(1)} %bitcast.20, bf16[14,14,4,256]{3,2,1,0:T(4,128)(2,1)S(1)} %bitcast.24, bf16[14,14,4,256]{3,2,1,0:T(4,128)(2,1)S(1)} %bitcast.26, bf16[14,14,4,1024]{3,2,1,0:T(4,128)(2,1)S(1)} %bitcast.22), custom_call_target="tpu_custom_call" | custom-call | flops 943718400 | bytes 6111232 | tf_op jit(solution)/shard_map/pallas_call | solution.py:278
  16.5 2.5 %collective-permute-start.15 = (f32[864,128]{1,0:T(8,128)S(1)}, f32[864,128]{1,0:T(8,128)S(1)}, u32[]{:S(2)}, u32[]{:S(2)}) collective-permute-start(f32[864,128]{1,0:T(8,128)S(1)} %get-tuple-element.87), channel_id=1, source_target_pairs={{0,32},{1,35},{2,34},{3,33},{4,36},{5,39},{6,38},{7,37},{8,40},{9,... | collective-permute-start | bytes 1327112 | tf_op jit(solution)/shard_map/ppermute | solution.py:326
  20.1 1.7 %collective-permute-start.8 = (f32[1152,128]{1,0:T(8,128)S(1)}, f32[1152,128]{1,0:T(8,128)S(1)}, u32[]{:S(2)}, u32[]{:S(2)}) collective-permute-start(f32[1152,128]{1,0:T(8,128)S(1)} %get-tuple-element.73), channel_id=1, source_target_pairs={{0,64},{1,193},{2,66},{3,195},{4,68},{5,197},{6,70},{7,199},{8,72}... | collective-permute-start | bytes 1769480 | tf_op jit(solution)/shard_map/ppermute | solution.py:326
  21.8 1.6 %collective-permute-done.19.got = f32[768,128]{1,0:T(8,128)S(1)} collective-permute-done((f32[768,128]{1,0:T(8,128)S(1)}, f32[768,128]{1,0:T(8,128)S(1)}, u32[]{:S(2)}, u32[]{:S(2)}) %collective-permute-start.19) | collective-permute-done | bytes 393248 | tf_op jit(solution)/shard_map/ppermute | solution.py:326
  25.9 6.3 %collective-permute-done.20.got = f32[512,128]{1,0:T(8,128)S(1)} collective-permute-done((f32[512,128]{1,0:T(8,128)S(1)}, f32[512,128]{1,0:T(8,128)S(1)}, u32[]{:S(2)}, u32[]{:S(2)}) %collective-permute-start.20) | collective-permute-done | bytes 262176 | tf_op jit(solution)/shard_map/ppermute | solution.py:326
  32.7 1.3 %collective-permute-start.21 = (f32[384,128]{1,0:T(8,128)S(1)}, f32[384,128]{1,0:T(8,128)S(1)}, u32[]{:S(2)}, u32[]{:S(2)}) collective-permute-start(f32[384,128]{1,0:T(8,128)S(1)} %get-tuple-element.99), channel_id=1, source_target_pairs={{0,32},{1,35},{2,34},{3,33},{4,36},{5,39},{6,38},{7,37},{8,40},{9,... | collective-permute-start | bytes 589832 | tf_op jit(solution)/shard_map/ppermute | solution.py:326
  34.7 2.5 %collective-permute-start.17 = (f32[432,128]{1,0:T(8,128)S(1)}, f32[432,128]{1,0:T(8,128)S(1)}, u32[]{:S(2)}, u32[]{:S(2)}) collective-permute-start(f32[432,128]{1,0:T(8,128)S(1)} %get-tuple-element.91), channel_id=1, source_target_pairs={{0,64},{1,193},{2,66},{3,195},{4,68},{5,197},{6,70},{7,199},{8,72}... | collective-permute-start | bytes 663560 | tf_op jit(solution)/shard_map/ppermute | solution.py:326
  39.3 1.4 %collective-permute-start.22 = (f32[320,128]{1,0:T(8,128)S(1)}, f32[320,128]{1,0:T(8,128)S(1)}, u32[]{:S(2)}, u32[]{:S(2)}) collective-permute-start(f32[320,128]{1,0:T(8,128)S(1)} %get-tuple-element.101), channel_id=1, source_target_pairs={{0,34},{1,33},{2,32},{3,35},{4,38},{5,37},{6,36},{7,39},{8,42},{9,... | collective-permute-start | bytes 491528 | tf_op jit(solution)/shard_map/ppermute | solution.py:326
  41.6 1.2 %collective-permute-start.18 = (f32[360,128]{1,0:T(8,128)S(1)}, f32[360,128]{1,0:T(8,128)S(1)}, u32[]{:S(2)}, u32[]{:S(2)}) collective-permute-start(f32[360,128]{1,0:T(8,128)S(1)} %get-tuple-element.93), channel_id=1, source_target_pairs={{0,192},{1,65},{2,194},{3,67},{4,196},{5,69},{6,198},{7,71},{8,200... | collective-permute-start | bytes 552968 | tf_op jit(solution)/shard_map/ppermute | solution.py:326
  42.8 1.3 %collective-permute-done.5.got = f32[640,128]{1,0:T(8,128)S(1)} collective-permute-done((f32[640,128]{1,0:T(8,128)S(1)}, f32[640,128]{1,0:T(8,128)S(1)}, u32[]{:S(2)}, u32[]{:S(2)}) %collective-permute-start.5) | collective-permute-done | bytes 327712 | tf_op jit(solution)/shard_map/ppermute | solution.py:326
  46.1 1.8 %collective-permute-start.10 = (f32[384,128]{1,0:T(8,128)S(1)}, f32[384,128]{1,0:T(8,128)S(1)}, u32[]{:S(2)}, u32[]{:S(2)}) collective-permute-start(f32[384,128]{1,0:T(8,128)S(1)} %get-tuple-element.77), channel_id=1, source_target_pairs={{0,32},{1,35},{2,34},{3,33},{4,36},{5,39},{6,38},{7,37},{8,40},{9,... | collective-permute-start | bytes 589832 | tf_op jit(solution)/shard_map/ppermute | solution.py:326
  48.5 1.7 %collective-permute-start.23 = (f32[272,128]{1,0:T(8,128)S(1)}, f32[272,128]{1,0:T(8,128)S(1)}, u32[]{:S(2)}, u32[]{:S(2)}) collective-permute-start(f32[272,128]{1,0:T(8,128)S(1)} %get-tuple-element.103), channel_id=1, source_target_pairs={{0,4},{1,5},{2,6},{3,7},{4,0},{5,1},{6,2},{7,3},{8,12},{9,13},{10,... | collective-permute-start | bytes 417800 | tf_op jit(solution)/shard_map/ppermute | solution.py:326
  50.2 1.6 %collective-permute-done.6.got = f32[384,128]{1,0:T(8,128)S(1)} collective-permute-done((f32[384,128]{1,0:T(8,128)S(1)}, f32[384,128]{1,0:T(8,128)S(1)}, u32[]{:S(2)}, u32[]{:S(2)}) %collective-permute-start.6) | collective-permute-done | bytes 196640 | tf_op jit(solution)/shard_map/ppermute | solution.py:326
  53.2 5.5 %collective-permute-start.24 = (f32[272,128]{1,0:T(8,128)S(1)}, f32[272,128]{1,0:T(8,128)S(1)}, u32[]{:S(2)}, u32[]{:S(2)}) collective-permute-start(f32[272,128]{1,0:T(8,128)S(1)} %add.40), channel_id=1, source_target_pairs={{0,28},{1,29},{2,30},{3,31},{4,8},{5,9},{6,10},{7,11},{8,4},{9,5},... | collective-permute-start | bytes 417800 | tf_op jit(solution)/shard_map/ppermute | solution.py:326
  59.4 1.8 %collective-permute-done.24 = f32[272,128]{1,0:T(8,128)S(1)} collective-permute-done((f32[272,128]{1,0:T(8,128)S(1)}, f32[272,128]{1,0:T(8,128)S(1)}, u32[]{:S(2)}, u32[]{:S(2)}) %collective-permute-start.24) | collective-permute-done | bytes 139296 | tf_op jit(solution)/shard_map/ppermute | solution.py:326
  61.2 1.9 %collective-permute-start.25 = (f32[272,128]{1,0:T(8,128)S(1)}, f32[272,128]{1,0:T(8,128)S(1)}, u32[]{:S(2)}, u32[]{:S(2)}) collective-permute-start(f32[272,128]{1,0:T(8,128)S(1)} %add.41), channel_id=1, source_target_pairs={{0,12},{1,13},{2,14},{3,15},{4,24},{5,25},{6,26},{7,27},{8,20},{9,... | collective-permute-start | bytes 417800 | tf_op jit(solution)/shard_map/ppermute | solution.py:326
  63.5 3.9 %collective-permute-start.13 = (f32[256,128]{1,0:T(8,128)S(1)}, f32[256,128]{1,0:T(8,128)S(1)}, u32[]{:S(2)}, u32[]{:S(2)}) collective-permute-start(f32[256,128]{1,0:T(8,128)S(1)} %add.38), channel_id=1, source_target_pairs={{0,28},{1,29},{2,30},{3,31},{4,8},{5,9},{6,10},{7,11},{8,4},{9,5},... | collective-permute-start | bytes 393224 | tf_op jit(solution)/shard_map/ppermute | solution.py:326
  67.3 11.1 %collective-permute-start.26 = (f32[272,128]{1,0:T(8,128)S(1)}, f32[272,128]{1,0:T(8,128)S(1)}, u32[]{:S(2)}, u32[]{:S(2)}) collective-permute-start(f32[272,128]{1,0:T(8,128)S(1)} %add.42.mine), channel_id=1, source_target_pairs={{0,1},{1,0},{2,3},{3,2},{4,5},{5,4},{6,7},{7,6},{8,9},{9,8},{10,11... | collective-permute-start | bytes 417800 | tf_op jit(solution)/shard_map/ppermute | solution.py:326
  78.5 1.9 %collective-permute-start.14 = (f32[256,128]{1,0:T(8,128)S(1)}, f32[256,128]{1,0:T(8,128)S(1)}, u32[]{:S(2)}, u32[]{:S(2)}) collective-permute-start(f32[256,128]{1,0:T(8,128)S(1)} %add.39), channel_id=1, source_target_pairs={{0,12},{1,13},{2,14},{3,15},{4,24},{5,25},{6,26},{7,27},{8,20},{9,... | collective-permute-start | bytes 393224 | tf_op jit(solution)/shard_map/ppermute | solution.py:326
  80.4 4.5 %shard_map.105 = (f32[256,256]{1,0:T(8,128)S(1)}, f32[256,256]{1,0:T(8,128)S(1)}) custom-call(s32[17]{0:T(128)S(1)} %stack.59.bits, f32[272,128]{1,0:T(8,128)S(1)} %add.42.mine, f32[272,128]{1,0:T(8,128)S(1)} %collective-permute-done.26.mate), custom_call_target="tpu_custom_call" | custom-call | flops 1000000000 | bytes 1024 | tf_op jit(solution)/shard_map/pallas_call | solution.py:278
  84.9 2.3 %collective-permute-done.14 = f32[256,128]{1,0:T(8,128)S(1)} collective-permute-done((f32[256,128]{1,0:T(8,128)S(1)}, f32[256,128]{1,0:T(8,128)S(1)}, u32[]{:S(2)}, u32[]{:S(2)}) %collective-permute-start.14) | collective-permute-done | bytes 131104 | tf_op jit(solution)/shard_map/ppermute | solution.py:326
  87.2 1.2 %collective-permute-start.27 = (f32[256,128]{1,0:T(8,128)S(1)}, f32[256,128]{1,0:T(8,128)S(1)}, u32[]{:S(2)}, u32[]{:S(2)}) collective-permute-start(f32[256,128]{1,0:T(8,128)S(1)} %add.43.mine), channel_id=1, source_target_pairs={{0,1},{1,0},{2,3},{3,2},{4,5},{5,4},{6,7},{7,6},{8,9},{9,8},{10,11... | collective-permute-start | bytes 393224 | tf_op jit(solution)/shard_map/ppermute | solution.py:326
  91.8 2.0 %collective-permute-done.28 = bf16[128,256]{1,0:T(8,128)(2,1)S(1)} collective-permute-done((bf16[128,256]{1,0:T(8,128)(2,1)S(1)}, bf16[128,256]{1,0:T(8,128)(2,1)S(1)}, u32[]{:S(2)}, u32[]{:S(2)}) %collective-permute-start.28) | collective-permute-done | bytes 65568 | tf_op jit(solution)/shard_map/ppermute | solution.py:326
  93.9 16.9 %all_to_all.5.mine = bf16[16,128,256]{2,1,0:T(8,128)(2,1)S(1)} all-to-all(bf16[16,128,256]{2,1,0:T(8,128)(2,1)S(1)} %broadcast_in_dim.2), channel_id=1, replica_groups=mesh['y'=4,'x_lo'=2,'z'=8,'x_hi'=2,'core'=2] {'y','x_lo','x_hi'}, dimensions={0} | all-to-all | bytes 2097152 | tf_op jit(solution)/shard_map/all_to_all | solution.py:410
  110.8 3.7 %collective-permute-start.29 = (bf16[16,128,256]{2,1,0:T(8,128)(2,1)S(1)}, bf16[16,128,256]{2,1,0:T(8,128)(2,1)S(1)}, u32[]{:S(2)}, u32[]{:S(2)}) collective-permute-start(bf16[16,128,256]{2,1,0:T(8,128)(2,1)S(1)} %all_to_all.5.mine), channel_id=1, source_target_pairs={{0,1},{1,0},{2,3},{3,2},{4,5},{5,4},{6,7},{7,6},{8,9},{9,8},{10,11... | collective-permute-start | bytes 3145736 | tf_op jit(solution)/shard_map/ppermute | solution.py:326
  114.5 2.4 %collective-permute-done.30.last_mate = bf16[128,256]{1,0:T(8,128)(2,1)S(1)} collective-permute-done((bf16[128,256]{1,0:T(8,128)(2,1)S(1)}, bf16[128,256]{1,0:T(8,128)(2,1)S(1)}, u32[]{:S(2)}, u32[]{:S(2)}) %collective-permute-start.30) | collective-permute-done | bytes 65568 | tf_op jit(solution)/shard_map/ppermute | solution.py:326
  116.9 2.1 %shard_map.107 = (bf16[1024,256]{1,0:T(8,128)(2,1)}, bf16[2304,256]{1,0:T(8,128)(2,1)}, bf16[256,1024]{1,0:T(8,128)(2,1)}) custom-call(s32[17]{0:T(128)S(1)} %stack.59.bits, bf16[16,128,256]{2,1,0:T(8,128)(2,1)S(1)} %all_to_all.5.mine, bf16[16,128,256]{2,1,0:T(8,128)(2,1)S(1)} %collective-permute-done.29.mate, bf16[128,256]{1,0:T(8,128)(2,1)S(1)} %get-tuple-element.109.last, ...), custom_call_target="tpu_custom_call" | custom-call | flops 1000000000 | bytes 1024 | tf_op jit(solution)/shard_map/pallas_call | solution.py:278
  (72 shorter events, 19.4 us)
Async XLA Ops:
  2.4 4.9 %copy-start = (bf16[4,14,14,1024]{3,0,2,1:T(4,128)(2,1)S(1)}, bf16[4,14,14,1024]{3,0,2,1:T(4,128)(2,1)}, u32[]{:S(2)}) copy-start(bf16[4,14,14,1024]{3,0,2,1:T(4,128)(2,1)} %param.6) | copy-start | bytes 4816900
  4.0 6.0 %collective-permute-start.2 = (f32[1360,128]{1,0:T(8,128)S(1)}, f32[1360,128]{1,0:T(8,128)S(1)}, u32[]{:S(2)}, u32[]{:S(2)}) collective-permute-start(f32[1360,128]{1,0:T(8,128)S(1)} %get-tuple-element.60), channel_id=1, source_target_pairs={{0,1},{1,0},{2,3},{3,2},{4,5},{5,4},{6,7},{7,6},{8,9},{9,8},{10,11... | collective-permute-start | bytes 2088968 | tf_op jit(solution)/shard_map/ppermute | solution.py:326
  9.5 2.8 %collective-permute-start = (f32[1360,128]{1,0:T(8,128)S(1)}, f32[1360,128]{1,0:T(8,128)S(1)}, u32[]{:S(2)}, u32[]{:S(2)}) collective-permute-start(f32[1360,128]{1,0:T(8,128)S(1)} %get-tuple-element.56), channel_id=1, source_target_pairs={{0,1},{1,0},{2,3},{3,2},{4,5},{5,4},{6,7},{7,6},{8,9},{9,8},{10,11... | collective-permute-start | bytes 2088968 | tf_op jit(solution)/shard_map/ppermute | solution.py:326
  12.1 6.9 %collective-permute-start.3 = (f32[2304,128]{1,0:T(8,128)S(1)}, f32[2304,128]{1,0:T(8,128)S(1)}, u32[]{:S(2)}, u32[]{:S(2)}) collective-permute-start(f32[2304,128]{1,0:T(8,128)S(1)} %get-tuple-element.63), channel_id=1, source_target_pairs={{0,1},{1,0},{2,3},{3,2},{4,5},{5,4},{6,7},{7,6},{8,9},{9,8},{10,11... | collective-permute-start | bytes 3538952 | tf_op jit(solution)/shard_map/ppermute | solution.py:326
  14.2 4.8 %collective-permute-start.1 = (f32[2048,128]{1,0:T(8,128)S(1)}, f32[2048,128]{1,0:T(8,128)S(1)}, u32[]{:S(2)}, u32[]{:S(2)}) collective-permute-start(f32[2048,128]{1,0:T(8,128)S(1)} %get-tuple-element.59), channel_id=1, source_target_pairs={{0,1},{1,0},{2,3},{3,2},{4,5},{5,4},{6,7},{7,6},{8,9},{9,8},{10,11... | collective-permute-start | bytes 3145736 | tf_op jit(solution)/shard_map/ppermute | solution.py:326
  15.4 7.9 %collective-permute-start.19 = (f32[768,128]{1,0:T(8,128)S(1)}, f32[768,128]{1,0:T(8,128)S(1)}, u32[]{:S(2)}, u32[]{:S(2)}) collective-permute-start(f32[768,128]{1,0:T(8,128)S(1)} %get-tuple-element.95), channel_id=1, source_target_pairs={{0,64},{1,193},{2,66},{3,195},{4,68},{5,197},{6,70},{7,199},{8,72}... | collective-permute-start | bytes 1179656 | tf_op jit(solution)/shard_map/ppermute | solution.py:326
  16.5 8.4 %collective-permute-start.15 = (f32[864,128]{1,0:T(8,128)S(1)}, f32[864,128]{1,0:T(8,128)S(1)}, u32[]{:S(2)}, u32[]{:S(2)}) collective-permute-start(f32[864,128]{1,0:T(8,128)S(1)} %get-tuple-element.87), channel_id=1, source_target_pairs={{0,32},{1,35},{2,34},{3,33},{4,36},{5,39},{6,38},{7,37},{8,40},{9,... | collective-permute-start | bytes 1327112 | tf_op jit(solution)/shard_map/ppermute | solution.py:326
  19.8 17.4 %collective-permute-start.4 = (f32[1152,128]{1,0:T(8,128)S(1)}, f32[1152,128]{1,0:T(8,128)S(1)}, u32[]{:S(2)}, u32[]{:S(2)}) collective-permute-start(f32[1152,128]{1,0:T(8,128)S(1)} %get-tuple-element.65), channel_id=1, source_target_pairs={{0,32},{1,35},{2,34},{3,33},{4,36},{5,39},{6,38},{7,37},{8,40},{9,... | collective-permute-start | bytes 1769480 | tf_op jit(solution)/shard_map/ppermute | solution.py:326
  20.1 17.8 %collective-permute-start.8 = (f32[1152,128]{1,0:T(8,128)S(1)}, f32[1152,128]{1,0:T(8,128)S(1)}, u32[]{:S(2)}, u32[]{:S(2)}) collective-permute-start(f32[1152,128]{1,0:T(8,128)S(1)} %get-tuple-element.73), channel_id=1, source_target_pairs={{0,64},{1,193},{2,66},{3,195},{4,68},{5,197},{6,70},{7,199},{8,72}... | collective-permute-start | bytes 1769480 | tf_op jit(solution)/shard_map/ppermute | solution.py:326
  23.9 8.2 %collective-permute-start.20 = (f32[512,128]{1,0:T(8,128)S(1)}, f32[512,128]{1,0:T(8,128)S(1)}, u32[]{:S(2)}, u32[]{:S(2)}) collective-permute-start(f32[512,128]{1,0:T(8,128)S(1)} %get-tuple-element.97), channel_id=1, source_target_pairs={{0,192},{1,65},{2,194},{3,67},{4,196},{5,69},{6,198},{7,71},{8,200... | collective-permute-start | bytes 786440 | tf_op jit(solution)/shard_map/ppermute | solution.py:326
  25.5 8.6 %collective-permute-start.16 = (f32[576,128]{1,0:T(8,128)S(1)}, f32[576,128]{1,0:T(8,128)S(1)}, u32[]{:S(2)}, u32[]{:S(2)}) collective-permute-start(f32[576,128]{1,0:T(8,128)S(1)} %get-tuple-element.89), channel_id=1, source_target_pairs={{0,34},{1,33},{2,32},{3,35},{4,38},{5,37},{6,36},{7,39},{8,42},{9,... | collective-permute-start | bytes 884744 | tf_op jit(solution)/shard_map/ppermute | solution.py:326
  32.7 6.0 %collective-permute-start.21 = (f32[384,128]{1,0:T(8,128)S(1)}, f32[384,128]{1,0:T(8,128)S(1)}, u32[]{:S(2)}, u32[]{:S(2)}) collective-permute-start(f32[384,128]{1,0:T(8,128)S(1)} %get-tuple-element.99), channel_id=1, source_target_pairs={{0,32},{1,35},{2,34},{3,33},{4,36},{5,39},{6,38},{7,37},{8,40},{9,... | collective-permute-start | bytes 589832 | tf_op jit(solution)/shard_map/ppermute | solution.py:326
  34.7 6.4 %collective-permute-start.17 = (f32[432,128]{1,0:T(8,128)S(1)}, f32[432,128]{1,0:T(8,128)S(1)}, u32[]{:S(2)}, u32[]{:S(2)}) collective-permute-start(f32[432,128]{1,0:T(8,128)S(1)} %get-tuple-element.91), channel_id=1, source_target_pairs={{0,64},{1,193},{2,66},{3,195},{4,68},{5,197},{6,70},{7,199},{8,72}... | collective-permute-start | bytes 663560 | tf_op jit(solution)/shard_map/ppermute | solution.py:326
  37.8 6.3 %collective-permute-start.5 = (f32[640,128]{1,0:T(8,128)S(1)}, f32[640,128]{1,0:T(8,128)S(1)}, u32[]{:S(2)}, u32[]{:S(2)}) collective-permute-start(f32[640,128]{1,0:T(8,128)S(1)} %get-tuple-element.67), channel_id=1, source_target_pairs={{0,34},{1,33},{2,32},{3,35},{4,38},{5,37},{6,36},{7,39},{8,42},{9,... | collective-permute-start | bytes 983048 | tf_op jit(solution)/shard_map/ppermute | solution.py:326
  38.5 7.0 %collective-permute-start.9 = (f32[640,128]{1,0:T(8,128)S(1)}, f32[640,128]{1,0:T(8,128)S(1)}, u32[]{:S(2)}, u32[]{:S(2)}) collective-permute-start(f32[640,128]{1,0:T(8,128)S(1)} %get-tuple-element.75), channel_id=1, source_target_pairs={{0,192},{1,65},{2,194},{3,67},{4,196},{5,69},{6,198},{7,71},{8,200... | collective-permute-start | bytes 983048 | tf_op jit(solution)/shard_map/ppermute | solution.py:326
  39.3 8.6 %collective-permute-start.22 = (f32[320,128]{1,0:T(8,128)S(1)}, f32[320,128]{1,0:T(8,128)S(1)}, u32[]{:S(2)}, u32[]{:S(2)}) collective-permute-start(f32[320,128]{1,0:T(8,128)S(1)} %get-tuple-element.101), channel_id=1, source_target_pairs={{0,34},{1,33},{2,32},{3,35},{4,38},{5,37},{6,36},{7,39},{8,42},{9,... | collective-permute-start | bytes 491528 | tf_op jit(solution)/shard_map/ppermute | solution.py:326
  41.6 6.3 %collective-permute-start.18 = (f32[360,128]{1,0:T(8,128)S(1)}, f32[360,128]{1,0:T(8,128)S(1)}, u32[]{:S(2)}, u32[]{:S(2)}) collective-permute-start(f32[360,128]{1,0:T(8,128)S(1)} %get-tuple-element.93), channel_id=1, source_target_pairs={{0,192},{1,65},{2,194},{3,67},{4,196},{5,69},{6,198},{7,71},{8,200... | collective-permute-start | bytes 552968 | tf_op jit(solution)/shard_map/ppermute | solution.py:326
  44.7 7.2 %collective-permute-start.6 = (f32[384,128]{1,0:T(8,128)S(1)}, f32[384,128]{1,0:T(8,128)S(1)}, u32[]{:S(2)}, u32[]{:S(2)}) collective-permute-start(f32[384,128]{1,0:T(8,128)S(1)} %get-tuple-element.69), channel_id=1, source_target_pairs={{0,64},{1,193},{2,66},{3,195},{4,68},{5,197},{6,70},{7,199},{8,72}... | collective-permute-start | bytes 589832 | tf_op jit(solution)/shard_map/ppermute | solution.py:326
  46.1 6.4 %collective-permute-start.10 = (f32[384,128]{1,0:T(8,128)S(1)}, f32[384,128]{1,0:T(8,128)S(1)}, u32[]{:S(2)}, u32[]{:S(2)}) collective-permute-start(f32[384,128]{1,0:T(8,128)S(1)} %get-tuple-element.77), channel_id=1, source_target_pairs={{0,32},{1,35},{2,34},{3,33},{4,36},{5,39},{6,38},{7,37},{8,40},{9,... | collective-permute-start | bytes 589832 | tf_op jit(solution)/shard_map/ppermute | solution.py:326
  48.5 4.7 %collective-permute-start.23 = (f32[272,128]{1,0:T(8,128)S(1)}, f32[272,128]{1,0:T(8,128)S(1)}, u32[]{:S(2)}, u32[]{:S(2)}) collective-permute-start(f32[272,128]{1,0:T(8,128)S(1)} %get-tuple-element.103), channel_id=1, source_target_pairs={{0,4},{1,5},{2,6},{3,7},{4,0},{5,1},{6,2},{7,3},{8,12},{9,13},{10,... | collective-permute-start | bytes 417800 | tf_op jit(solution)/shard_map/ppermute | solution.py:326
  52.4 6.3 %collective-permute-start.7 = (f32[256,128]{1,0:T(8,128)S(1)}, f32[256,128]{1,0:T(8,128)S(1)}, u32[]{:S(2)}, u32[]{:S(2)}) collective-permute-start(f32[256,128]{1,0:T(8,128)S(1)} %get-tuple-element.71), channel_id=1, source_target_pairs={{0,192},{1,65},{2,194},{3,67},{4,196},{5,69},{6,198},{7,71},{8,200... | collective-permute-start | bytes 393224 | tf_op jit(solution)/shard_map/ppermute | solution.py:326
  53.1 5.7 %collective-permute-start.11 = (f32[256,128]{1,0:T(8,128)S(1)}, f32[256,128]{1,0:T(8,128)S(1)}, u32[]{:S(2)}, u32[]{:S(2)}) collective-permute-start(f32[256,128]{1,0:T(8,128)S(1)} %get-tuple-element.79), channel_id=1, source_target_pairs={{0,34},{1,33},{2,32},{3,35},{4,38},{5,37},{6,36},{7,39},{8,42},{9,... | collective-permute-start | bytes 393224 | tf_op jit(solution)/shard_map/ppermute | solution.py:326
  53.2 8.0 %collective-permute-start.24 = (f32[272,128]{1,0:T(8,128)S(1)}, f32[272,128]{1,0:T(8,128)S(1)}, u32[]{:S(2)}, u32[]{:S(2)}) collective-permute-start(f32[272,128]{1,0:T(8,128)S(1)} %add.40), channel_id=1, source_target_pairs={{0,28},{1,29},{2,30},{3,31},{4,8},{5,9},{6,10},{7,11},{8,4},{9,5},... | collective-permute-start | bytes 417800 | tf_op jit(solution)/shard_map/ppermute | solution.py:326
  59.3 4.1 %collective-permute-start.12 = (f32[256,128]{1,0:T(8,128)S(1)}, f32[256,128]{1,0:T(8,128)S(1)}, u32[]{:S(2)}, u32[]{:S(2)}) collective-permute-start(f32[256,128]{1,0:T(8,128)S(1)} %get-tuple-element.81), channel_id=1, source_target_pairs={{0,4},{1,5},{2,6},{3,7},{4,0},{5,1},{6,2},{7,3},{8,12},{9,13},{10,... | collective-permute-start | bytes 393224 | tf_op jit(solution)/shard_map/ppermute | solution.py:326
  61.2 6.1 %collective-permute-start.25 = (f32[272,128]{1,0:T(8,128)S(1)}, f32[272,128]{1,0:T(8,128)S(1)}, u32[]{:S(2)}, u32[]{:S(2)}) collective-permute-start(f32[272,128]{1,0:T(8,128)S(1)} %add.41), channel_id=1, source_target_pairs={{0,12},{1,13},{2,14},{3,15},{4,24},{5,25},{6,26},{7,27},{8,20},{9,... | collective-permute-start | bytes 417800 | tf_op jit(solution)/shard_map/ppermute | solution.py:326
  63.5 15.0 %collective-permute-start.13 = (f32[256,128]{1,0:T(8,128)S(1)}, f32[256,128]{1,0:T(8,128)S(1)}, u32[]{:S(2)}, u32[]{:S(2)}) collective-permute-start(f32[256,128]{1,0:T(8,128)S(1)} %add.38), channel_id=1, source_target_pairs={{0,28},{1,29},{2,30},{3,31},{4,8},{5,9},{6,10},{7,11},{8,4},{9,5},... | collective-permute-start | bytes 393224 | tf_op jit(solution)/shard_map/ppermute | solution.py:326
  67.3 13.1 %collective-permute-start.26 = (f32[272,128]{1,0:T(8,128)S(1)}, f32[272,128]{1,0:T(8,128)S(1)}, u32[]{:S(2)}, u32[]{:S(2)}) collective-permute-start(f32[272,128]{1,0:T(8,128)S(1)} %add.42.mine), channel_id=1, source_target_pairs={{0,1},{1,0},{2,3},{3,2},{4,5},{5,4},{6,7},{7,6},{8,9},{9,8},{10,11... | collective-permute-start | bytes 417800 | tf_op jit(solution)/shard_map/ppermute | solution.py:326
  78.5 8.7 %collective-permute-start.14 = (f32[256,128]{1,0:T(8,128)S(1)}, f32[256,128]{1,0:T(8,128)S(1)}, u32[]{:S(2)}, u32[]{:S(2)}) collective-permute-start(f32[256,128]{1,0:T(8,128)S(1)} %add.39), channel_id=1, source_target_pairs={{0,12},{1,13},{2,14},{3,15},{4,24},{5,25},{6,26},{7,27},{8,20},{9,... | collective-permute-start | bytes 393224 | tf_op jit(solution)/shard_map/ppermute | solution.py:326
  87.2 2.2 %collective-permute-start.27 = (f32[256,128]{1,0:T(8,128)S(1)}, f32[256,128]{1,0:T(8,128)S(1)}, u32[]{:S(2)}, u32[]{:S(2)}) collective-permute-start(f32[256,128]{1,0:T(8,128)S(1)} %add.43.mine), channel_id=1, source_target_pairs={{0,1},{1,0},{2,3},{3,2},{4,5},{5,4},{6,7},{7,6},{8,9},{9,8},{10,11... | collective-permute-start | bytes 393224 | tf_op jit(solution)/shard_map/ppermute | solution.py:326
  90.6 3.2 %collective-permute-start.28 = (bf16[128,256]{1,0:T(8,128)(2,1)S(1)}, bf16[128,256]{1,0:T(8,128)(2,1)S(1)}, u32[]{:S(2)}, u32[]{:S(2)}) collective-permute-start(bf16[128,256]{1,0:T(8,128)(2,1)S(1)} %shard_map.106), channel_id=1, source_target_pairs={{0,4},{1,5},{2,6},{3,7},{4,0},{5,1},{6,2},{7,3},{8,12},{9,13},{10,... | collective-permute-start | bytes 196616 | tf_op jit(solution)/shard_map/ppermute | solution.py:326
  110.8 6.1 %collective-permute-start.29 = (bf16[16,128,256]{2,1,0:T(8,128)(2,1)S(1)}, bf16[16,128,256]{2,1,0:T(8,128)(2,1)S(1)}, u32[]{:S(2)}, u32[]{:S(2)}) collective-permute-start(bf16[16,128,256]{2,1,0:T(8,128)(2,1)S(1)} %all_to_all.5.mine), channel_id=1, source_target_pairs={{0,1},{1,0},{2,3},{3,2},{4,5},{5,4},{6,7},{7,6},{8,9},{9,8},{10,11... | collective-permute-start | bytes 3145736 | tf_op jit(solution)/shard_map/ppermute | solution.py:326
  114.5 2.4 %collective-permute-start.30 = (bf16[128,256]{1,0:T(8,128)(2,1)S(1)}, bf16[128,256]{1,0:T(8,128)(2,1)S(1)}, u32[]{:S(2)}, u32[]{:S(2)}) collective-permute-start(bf16[128,256]{1,0:T(8,128)(2,1)S(1)} %get-tuple-element.109.last), channel_id=1, source_target_pairs={{0,1},{1,0},{2,3},{3,2},{4,5},{5,4},{6,7},{7,6},{8,9},{9,8},{10,11... | collective-permute-start | bytes 196616 | tf_op jit(solution)/shard_map/ppermute | solution.py:326
  (3 other events, 14.8 us)
